TPU v7x, 32 devices: a whole 2x2x4 slice. The times are simulated.
32 devices in a mesh: dp: 4 (over y, x), expert: 8 (over z, core).
Axes of the slice: x: 2, y: 2, z: 4, core: 2. Of those that a mesh axis runs over, the one named last changes fastest.
Arguments:
- tokens: bfloat16 [25216, 768], P(('dp', 'expert')), may hold values from -6 to 6
- attn_qkv: bfloat16 [3, 768, 768], P(None, 'dp'), may hold values from -0.21875 to 0.21875
- attn_out: bfloat16 [768, 768], P('dp'), may hold values from -1.75 to 1.75
- router: bfloat16 [768, 8], P('dp'), may hold values from -0.15625 to 0.15625
- norm_gains: bfloat16 [2, 768], P(None, 'dp'), may hold values from 0.5 to 1.5
- expert_in: bfloat16 [8, 768, 3072], P('expert'), may hold values from -0.21875 to 0.21875
- expert_out: bfloat16 [8, 3072, 768], P('expert'), may hold values from -0.21875 to 0.21875
- routes: int32 [25216, 2], P(('dp', 'expert')), may hold values from 0 to 7, all different within a row; in each aligned block of 394 rows (0 to 393, 394 to 787, ...) at most 160 rows name the same one
- clip_limit: float32 [12], replicated, may hold values from 0.5 to 4
- cotangent: bfloat16 [25216, 768], P(('dp', 'expert')), may hold values from -6 to 6
Outputs:
- layer_out: bfloat16 [25216, 768], P(('dp', 'expert'))
- grad_input: bfloat16 [25216, 768], P(('dp', 'expert'))
- grad_attn_qkv: float32 [3, 768, 768], P(None, 'dp')
- grad_attn_out: float32 [768, 768], P('dp')
- grad_router: float32 [768, 8], P('dp')
- grad_gains: float32 [2, 768], P(None, 'dp')
- grad_expert_in: float32 [8, 768, 3072], P('expert', 'dp')
- grad_expert_out: float32 [8, 3072, 768], P('expert', 'dp')
- head_max: float32 [12], replicated
- clipped_qk: float32 [2, 768, 768], P(None, 'dp')
Inputs may be any that keep to these rules, and one draw needn't show every extreme that they name: `routes`: each row names two different experts.
All inputs are finite; a program needn't handle non-finite values.
Results may differ from a plain program's by a relative error of at most 0.02.
Values may be sent and summed in bfloat16 or wider, within the bound.
A program may use at most 192 MiB of HBM per device.

v0:
```python
import jax
import jax.numpy as jnp
from jax import lax
from jax.sharding import PartitionSpec as P

D = 768
HEADS = 12
HEAD_DIM = 64
FF = 3072
SEQ = 197
IMG_DEV = 2
MB = 2
TOK_MB = 394


epsilon = 1e-06
qk_scale = 0.125
gelu_coeff = 0.7978845608028654


def layer_norm(values_in, gain_row):
    row_mean = jnp.mean(values_in, axis=-1, keepdims=True)
    centred = values_in - row_mean
    row_var = jnp.mean(centred * centred, axis=-1, keepdims=True)
    return centred * lax.rsqrt(row_var + epsilon) * gain_row


def gelu_tanh(values_in):
    return (
        0.5
        * values_in
        * (1.0 + jnp.tanh(gelu_coeff * (values_in + 0.044715 * values_in * values_in * values_in)))
    )


def fetch_weights(shards):
    return (
        lax.all_gather(shards[0], "dp", axis=1, tiled=True),
        lax.all_gather(shards[1], "dp", axis=0, tiled=True),
        lax.all_gather(shards[2], "dp", axis=0, tiled=True),
        lax.all_gather(shards[3], "dp", axis=1, tiled=True),
    )


def attention_forward(token_rows, weights):
    qkv_weight = weights[0]
    out_weight = weights[1]
    gain_pair = weights[3]
    tokens_wide = token_rows.astype(jnp.float32)
    first_norm = layer_norm(tokens_wide, gain_pair[0].astype(jnp.float32)).astype(jnp.bfloat16)
    projected = jnp.einsum(
        "td,cde->cte", first_norm, qkv_weight, preferred_element_type=jnp.float32
    ).astype(jnp.bfloat16)
    split_heads = projected.reshape(3, IMG_DEV, SEQ, HEADS, HEAD_DIM)
    scores = (
        jnp.einsum(
            "bqhd,bkhd->bhqk", split_heads[0], split_heads[1], preferred_element_type=jnp.float32
        )
        * qk_scale
    )
    row_top = jnp.max(scores, axis=-1, keepdims=True)
    exp_scores = jnp.exp(scores - row_top)
    attn_probs = exp_scores / jnp.sum(exp_scores, axis=-1, keepdims=True)
    probs_low = attn_probs.astype(jnp.bfloat16)
    mixed_heads = jnp.einsum(
        "bhqk,bkhd->bqhd", probs_low, split_heads[2], preferred_element_type=jnp.float32
    ).astype(jnp.bfloat16)
    mixed_flat = mixed_heads.reshape(TOK_MB, D)
    residual = tokens_wide + jnp.dot(mixed_flat, out_weight, preferred_element_type=jnp.float32)
    head_top = jnp.max(row_top, axis=(0, 2, 3))
    return (first_norm, split_heads, attn_probs, probs_low, mixed_flat, residual, head_top)


def route_gates(residual, weights, route_rows):
    second_norm = layer_norm(residual, weights[3][1].astype(jnp.float32)).astype(jnp.bfloat16)
    logits = jnp.dot(second_norm, weights[2], preferred_element_type=jnp.float32)
    chosen = jnp.take_along_axis(logits, route_rows, axis=1)
    exp_chosen = jnp.exp(chosen - jnp.max(chosen, axis=1, keepdims=True))
    gate_values = exp_chosen / jnp.sum(exp_chosen, axis=1, keepdims=True)
    return (second_norm, gate_values)


def slot_table(route_rows, experts, capacity):
    flat_expert = route_rows.reshape(-1)
    onehot = (flat_expert[:, None] == jnp.arange(experts, dtype=jnp.int32)[None, :]).astype(
        jnp.int32
    )
    before = jnp.cumsum(onehot, axis=0) - onehot
    slot_index = jnp.sum(before * onehot, axis=1)
    kept_mask = (slot_index < capacity).reshape(-1, 2).astype(jnp.float32)
    slot_ids = jnp.where(slot_index < capacity, flat_expert * capacity + slot_index, -1)
    dispatch_rows = jnp.arange(experts * capacity, dtype=jnp.int32)
    placing = (dispatch_rows[:, None] == slot_ids[None, :]).astype(jnp.bfloat16)
    return (placing, kept_mask)


def pack_pairs(pair_rows, placing, experts, capacity):
    packed = jnp.dot(placing, pair_rows, preferred_element_type=jnp.float32)
    return packed.astype(jnp.bfloat16).reshape(experts, capacity, pair_rows.shape[-1])


def unpack_pairs(buffer, placing):
    flat_buffer = buffer.reshape(placing.shape[0], buffer.shape[-1])
    return jnp.einsum("sp,sd->pd", placing, flat_buffer, preferred_element_type=jnp.float32)


def expert_forward(arrived, weight_in, weight_out):
    arrived_rows = arrived.reshape(-1, arrived.shape[-1])
    pre_act = jnp.dot(arrived_rows, weight_in, preferred_element_type=jnp.float32)
    hidden = gelu_tanh(pre_act).astype(jnp.bfloat16)
    produced = jnp.dot(hidden, weight_out, preferred_element_type=jnp.float32).astype(jnp.bfloat16)
    return produced.reshape(arrived.shape)


def per_device(
    tokens,
    attn_qkv,
    attn_out,
    router,
    norm_gains,
    expert_in,
    expert_out,
    routes,
    clip_limit,
    cotangent,
):
    experts = lax.axis_size("expert") * expert_in.shape[0]
    capacity = max(8, (TOK_MB * 10 // (4 * experts) + 7) // 8 * 8)
    weight_in = expert_in[0]
    weight_out = expert_out[0]
    shards = (attn_qkv, attn_out, router, norm_gains)
    grad_qkv = jnp.zeros((3, D, D), jnp.float32)
    grad_attn = jnp.zeros((D, D), jnp.float32)
    grad_route = jnp.zeros((D, experts), jnp.float32)
    grad_gain = jnp.zeros((2, D), jnp.float32)
    grad_in = jnp.zeros((D, FF), jnp.float32)
    grad_out = jnp.zeros((FF, D), jnp.float32)
    running = jnp.full((HEADS,), -jnp.inf, jnp.float32)
    expert_ids = jnp.arange(experts, dtype=jnp.int32)
    out_blocks = []
    input_grads = []
    for micro_index in range(MB):
        start = micro_index * TOK_MB
        token_rows = lax.slice_in_dim(tokens, start, start + TOK_MB, axis=0)
        route_rows = lax.slice_in_dim(routes, start, start + TOK_MB, axis=0)
        cot_rows = lax.slice_in_dim(cotangent, start, start + TOK_MB, axis=0).astype(jnp.float32)
        placing, kept_mask = slot_table(route_rows, experts, capacity)
        token_placing = jnp.sum(placing.reshape(experts * capacity, TOK_MB, 2), axis=2)
        weights = fetch_weights(shards)
        forward_parts = attention_forward(token_rows, weights)
        running = jnp.maximum(running, forward_parts[6])
        second_norm, gate_values = route_gates(forward_parts[5], weights, route_rows)
        buffer = pack_pairs(second_norm, token_placing, experts, capacity)
        arrived = lax.all_to_all(buffer, "expert", split_axis=0, concat_axis=0, tiled=True)
        produced = expert_forward(arrived, weight_in, weight_out)
        returned, arrived = (
            lax.all_to_all(produced, "expert", split_axis=0, concat_axis=0, tiled=True),
            arrived,
        )
        pair_out = unpack_pairs(returned, placing).reshape(TOK_MB, 2, D)
        mix_weight = gate_values * kept_mask
        combined = jnp.sum(mix_weight[:, :, None] * pair_out, axis=1)
        out_blocks.append((forward_parts[5] + combined).astype(jnp.bfloat16))
        weights = fetch_weights(shards)
        first_norm, split_heads, attn_probs, probs_low, mixed_flat, residual, head_again = (
            attention_forward(token_rows, weights)
        )
        second_norm, gate_values = route_gates(residual, weights, route_rows)
        grad_pairs = (
            (mix_weight[:, :, None] * cot_rows[:, None, :])
            .astype(jnp.bfloat16)
            .reshape(2 * TOK_MB, D)
        )
        grad_buffer = pack_pairs(grad_pairs, placing, experts, capacity)
        grad_arrived = lax.all_to_all(
            grad_buffer, "expert", split_axis=0, concat_axis=0, tiled=True
        )
        arrived_rows = arrived.reshape(-1, D)
        grad_rows = grad_arrived.reshape(-1, D)
        pre_act = jnp.dot(arrived_rows, weight_in, preferred_element_type=jnp.float32)
        hidden_wide, gelu_back = jax.vjp(gelu_tanh, pre_act)
        hidden = hidden_wide.astype(jnp.bfloat16)
        grad_out = grad_out + jnp.einsum(
            "rf,rd->fd", hidden, grad_rows, preferred_element_type=jnp.float32
        )
        grad_hidden = jnp.einsum(
            "rd,fd->rf", grad_rows, weight_out, preferred_element_type=jnp.float32
        )
        grad_pre = gelu_back(grad_hidden)[0].astype(jnp.bfloat16)
        grad_in = grad_in + jnp.einsum(
            "rd,rf->df", arrived_rows, grad_pre, preferred_element_type=jnp.float32
        )
        grad_sent = jnp.einsum("rf,df->rd", grad_pre, weight_in, preferred_element_type=jnp.float32)
        grad_sent = grad_sent.astype(jnp.bfloat16).reshape(arrived.shape)
        grad_back = lax.all_to_all(grad_sent, "expert", split_axis=0, concat_axis=0, tiled=True)
        grad_pair_in = unpack_pairs(grad_back, placing).reshape(TOK_MB, 2, D)
        grad_gate = kept_mask * jnp.sum(cot_rows[:, None, :] * pair_out, axis=2)
        grad_chosen = gate_values * (
            grad_gate - jnp.sum(gate_values * grad_gate, axis=1, keepdims=True)
        )
        onehot_pairs = (route_rows[:, :, None] == expert_ids[None, None, :]).astype(jnp.float32)
        grad_logits = jnp.sum(onehot_pairs * grad_chosen[:, :, None], axis=1).astype(jnp.bfloat16)
        grad_route = grad_route + jnp.einsum(
            "td,te->de", second_norm, grad_logits, preferred_element_type=jnp.float32
        )
        grad_second = jnp.sum(grad_pair_in, axis=1) + jnp.einsum(
            "te,de->td", grad_logits, weights[2], preferred_element_type=jnp.float32
        )
        norm_value, norm_back = jax.vjp(layer_norm, residual, weights[3][1].astype(jnp.float32))
        grad_resid_norm, grad_gain_two = norm_back(grad_second)
        grad_resid = cot_rows + grad_resid_norm
        grad_attended = grad_resid.astype(jnp.bfloat16)
        grad_attn = grad_attn + jnp.einsum(
            "td,te->de", mixed_flat, grad_attended, preferred_element_type=jnp.float32
        )
        grad_mixed = jnp.einsum(
            "te,de->td", grad_attended, weights[1], preferred_element_type=jnp.float32
        )
        grad_mixed = grad_mixed.astype(jnp.bfloat16).reshape(IMG_DEV, SEQ, HEADS, HEAD_DIM)
        grad_probs = jnp.einsum(
            "bqhd,bkhd->bhqk", grad_mixed, split_heads[2], preferred_element_type=jnp.float32
        )
        grad_values = jnp.einsum(
            "bhqk,bqhd->bkhd", probs_low, grad_mixed, preferred_element_type=jnp.float32
        )
        row_dot = jnp.sum(attn_probs * grad_probs, axis=-1, keepdims=True)
        grad_scores = (attn_probs * (grad_probs - row_dot)).astype(jnp.bfloat16)
        grad_queries = (
            jnp.einsum(
                "bhqk,bkhd->bqhd", grad_scores, split_heads[1], preferred_element_type=jnp.float32
            )
            * qk_scale
        )
        grad_keys = (
            jnp.einsum(
                "bhqk,bqhd->bkhd", grad_scores, split_heads[0], preferred_element_type=jnp.float32
            )
            * qk_scale
        )
        grad_proj = (
            jnp.stack([grad_queries, grad_keys, grad_values])
            .astype(jnp.bfloat16)
            .reshape(3, TOK_MB, D)
        )
        grad_qkv = grad_qkv + jnp.einsum(
            "td,cte->cde", first_norm, grad_proj, preferred_element_type=jnp.float32
        )
        grad_first = jnp.einsum(
            "cte,cde->td", grad_proj, weights[0], preferred_element_type=jnp.float32
        )
        norm_value, norm_back = jax.vjp(
            layer_norm, token_rows.astype(jnp.float32), weights[3][0].astype(jnp.float32)
        )
        grad_tokens_norm, grad_gain_one = norm_back(grad_first)
        input_grads.append((grad_resid + grad_tokens_norm).astype(jnp.bfloat16))
        grad_gain = grad_gain + jnp.stack([grad_gain_one, grad_gain_two])
    head_max = lax.pmax(running, ("dp", "expert"))
    attn_grads = (grad_qkv, grad_attn, grad_route, grad_gain)
    totals = (
        lax.psum(attn_grads[0].astype(jnp.bfloat16), "expert").astype(jnp.float32),
        lax.psum(attn_grads[1].astype(jnp.bfloat16), "expert").astype(jnp.float32),
        lax.psum(attn_grads[2].astype(jnp.bfloat16), "expert").astype(jnp.float32),
        lax.psum(attn_grads[3].astype(jnp.bfloat16), "expert").astype(jnp.float32),
    )
    shares = (
        lax.psum_scatter(
            totals[0].astype(jnp.bfloat16), "dp", scatter_dimension=1, tiled=True
        ).astype(jnp.float32),
        lax.psum_scatter(
            totals[1].astype(jnp.bfloat16), "dp", scatter_dimension=0, tiled=True
        ).astype(jnp.float32),
        lax.psum_scatter(
            totals[2].astype(jnp.bfloat16), "dp", scatter_dimension=0, tiled=True
        ).astype(jnp.float32),
        lax.psum_scatter(
            totals[3].astype(jnp.bfloat16), "dp", scatter_dimension=1, tiled=True
        ).astype(jnp.float32),
    )
    expert_shares = (
        lax.psum_scatter(
            grad_in[None].astype(jnp.bfloat16), "dp", scatter_dimension=1, tiled=True
        ).astype(jnp.float32),
        lax.psum_scatter(
            grad_out[None].astype(jnp.bfloat16), "dp", scatter_dimension=1, tiled=True
        ).astype(jnp.float32),
    )
    factor = clip_limit / jnp.maximum(head_max, clip_limit)
    root_scale = jnp.repeat(jnp.sqrt(factor), HEAD_DIM)
    clipped_qk = attn_qkv[:2].astype(jnp.float32) * root_scale[None, None, :]
    return (
        jnp.concatenate(out_blocks, axis=0),
        jnp.concatenate(input_grads, axis=0),
        shares[0],
        shares[1],
        shares[2],
        shares[3],
        expert_shares[0],
        expert_shares[1],
        head_max,
        clipped_qk,
    )


def solution(mesh):
    placed = (
        P(("dp", "expert"), None),
        P(None, "dp", None),
        P("dp", None),
        P("dp", None),
        P(None, "dp"),
        P("expert", None, None),
        P("expert", None, None),
        P(("dp", "expert"), None),
        P(),
        P(("dp", "expert"), None),
    )
    return jax.shard_map(
        per_device,
        mesh=mesh,
        in_specs=placed,
        out_specs=(
            P(("dp", "expert"), None),
            P(("dp", "expert"), None),
            P(None, "dp", None),
            P("dp", None),
            P("dp", None),
            P(None, "dp"),
            P("expert", "dp", None),
            P("expert", "dp", None),
            P(),
            P(None, "dp", None),
        ),
        check_vma=False,
    )
```

profile of v0, /device:TPU:0, one launch (start us, length us, event | category | flops | bytes accessed | tf_op | source)
XLA Modules:
  0.0 894.4 jit_solution(11208329187765409721)
XLA Ops:
  10.9 9.5 %all-gather = bf16[4,192,2]{1,2,0:T(2,128)(2,1)S(1)} all-gather(bf16[1,192,2]{1,2,0:T(2,128)(2,1)S(1)} %bitcast.240), channel_id=1, replica_groups=mesh['dp'=4,'expert'=8] {'dp'}, dimensions={0}, use_global_device_ids=true | all-gather | bytes 3840 | tf_op jit(solution)/shard_map/all_gather | solution.py:41
  34.0 25.9 %all-gather.5.cloned.1.call-done = bf16[3,768,768]{2,1,0:T(8,128)(2,1)} async-done(((bf16[3,192,768]{2,1,0:T(8,128)(2,1)}), bf16[3,768,768]{2,1,0:T(8,128)(2,1)}) %all-gather.5.cloned.1.call-update) | async-done | bytes 3538960 | tf_op jit(solution)/shard_map/all_gather | solution.py:38
  76.5 5.6 fusion.163
  141.6 8.1 all-gather.1
  151.8 8.3 gather_fusion
  160.7 8.2 gather_fusion.1
  186.5 30.9 %all-to-all-done.4 = bf16[8,128,768]{2,1,0:T(8,128)(2,1)S(1)} async-done(((bf16[8,128,768]{2,1,0:T(8,128)(2,1)}), bf16[8,128,768]{2,1,0:T(8,128)(2,1)S(1)}, u32[]{:S(2)}, u32[]{:S(2)}) %all-to-all-start.4) | async-done | bytes 1572896 | tf_op jit(solution)/shard_map/all_to_all | solution.py:175
  232.3 9.4 %fusion.28 = f32[1024,3072]{1,0:T(8,128)} fusion(bf16[1024,768]{1,0:T(8,128)(2,1)} %bitcast.13, bf16[1,768,3072]{2,1,0:T(8,128)(2,1)S(1)} %bitcast.242), kind=kOutput, calls=%fused_computation.51 | convolution fusion | flops 4831838208 | bytes 18874368 | tf_op jit(solution)/shard_map/dot_general | solution.py:109
  241.7 17.8 %all-to-all-done.2 = bf16[8,128,768]{2,1,0:T(8,128)(2,1)} async-done(((bf16[8,128,768]{2,1,0:T(8,128)(2,1)}), bf16[8,128,768]{2,1,0:T(8,128)(2,1)}, u32[]{:S(2)}, u32[]{:S(2)}) %all-to-all-start.2) | async-done | bytes 1572896 | tf_op jit(solution)/shard_map/all_to_all | solution.py:154
  263.3 16.3 %fusion.5 = bf16[1024,3072]{1,0:T(8,128)(2,1)S(1)} fusion(f32[1024,3072]{1,0:T(8,128)} %fusion.28, bf16[1024,768]{1,0:T(8,128)(2,1)S(1)} %bitcast.221, bf16[1,3072,768]{2,1,0:T(8,128)(2,1)} %param.18), kind=kOutput, calls=%fused_computation.15 | convolution fusion | flops 4907335680 | bytes 25165824 | tf_op jit(solution)/shard_map/rd,fd->rf/dot_general | solution.py:186
  282.3 8.5 fusion.59
  290.8 10.2 %all-to-all-done.6 = bf16[8,128,768]{2,1,0:T(8,128)(2,1)S(1)} async-done(((bf16[8,128,768]{2,1,0:T(8,128)(2,1)}), bf16[8,128,768]{2,1,0:T(8,128)(2,1)S(1)}, u32[]{:S(2)}, u32[]{:S(2)}) %all-to-all-start.6) | async-done | bytes 1572896 | tf_op jit(solution)/shard_map/all_to_all | solution.py:175
  304.6 10.0 %fusion.26 = f32[1024,3072]{1,0:T(8,128)} fusion(bf16[1024,768]{1,0:T(8,128)(2,1)} %bitcast.28, bf16[1,768,3072]{2,1,0:T(8,128)(2,1)} %param.17), kind=kOutput, calls=%fused_computation.49 | convolution fusion | flops 4831838208 | bytes 18874368 | tf_op jit(solution)/shard_map/dot_general | solution.py:109
  314.6 12.5 %fusion.65 = bf16[1024,768]{1,0:T(8,128)(2,1)} fusion(bf16[1,3072,768]{2,1,0:T(8,128)(2,1)} %param.18, f32[1024,3072]{1,0:T(8,128)} %fusion.28), kind=kOutput, calls=%fused_computation.107 | convolution fusion | flops 4860936192 | bytes 18874368 | tf_op jit(solution)/shard_map/dot_general | solution.py:111
  327.1 15.3 %all-to-all-done.5 = bf16[8,128,768]{2,1,0:T(8,128)(2,1)S(1)} async-done(((bf16[8,128,768]{2,1,0:T(8,128)(2,1)}), bf16[8,128,768]{2,1,0:T(8,128)(2,1)S(1)}, u32[]{:S(2)}, u32[]{:S(2)}) %all-to-all-start.5) | async-done | bytes 1572896 | tf_op jit(solution)/shard_map/all_to_all | solution.py:195
  347.1 16.3 %fusion.9 = bf16[1024,3072]{1,0:T(8,128)(2,1)S(1)} fusion(f32[1024,3072]{1,0:T(8,128)} %fusion.26, bf16[1024,768]{1,0:T(8,128)(2,1)S(1)} %bitcast.222, bf16[1,3072,768]{2,1,0:T(8,128)(2,1)} %param.18), kind=kOutput, calls=%fused_computation.19 | convolution fusion | flops 4907335680 | bytes 25165824 | tf_op jit(solution)/shard_map/rd,fd->rf/dot_general | solution.py:186
  366.0 8.5 fusion.62
  374.5 10.4 %all-to-all-done.1 = bf16[8,128,768]{2,1,0:T(8,128)(2,1)} async-done(((bf16[8,128,768]{2,1,0:T(8,128)(2,1)}), bf16[8,128,768]{2,1,0:T(8,128)(2,1)}, u32[]{:S(2)}, u32[]{:S(2)}) %all-to-all-start.1) | async-done | bytes 1572896 | tf_op jit(solution)/shard_map/all_to_all | solution.py:157
  388.5 12.6 %fusion.68 = bf16[1024,768]{1,0:T(8,128)(2,1)} fusion(bf16[1,3072,768]{2,1,0:T(8,128)(2,1)} %param.18, f32[1024,3072]{1,0:T(8,128)} %fusion.26), kind=kOutput, calls=%fused_computation.108 | convolution fusion | flops 4860936192 | bytes 18874368 | tf_op jit(solution)/shard_map/dot_general | solution.py:111
  401.1 25.2 %all-to-all-done.7 = bf16[8,128,768]{2,1,0:T(8,128)(2,1)S(1)} async-done(((bf16[8,128,768]{2,1,0:T(8,128)(2,1)}), bf16[8,128,768]{2,1,0:T(8,128)(2,1)S(1)}, u32[]{:S(2)}, u32[]{:S(2)}) %all-to-all-start.7) | async-done | bytes 1572896 | tf_op jit(solution)/shard_map/all_to_all | solution.py:195
  448.4 20.0 %all-to-all-done.3 = bf16[8,128,768]{2,1,0:T(8,128)(2,1)} async-done(((bf16[8,128,768]{2,1,0:T(8,128)(2,1)}), bf16[8,128,768]{2,1,0:T(8,128)(2,1)}, u32[]{:S(2)}, u32[]{:S(2)}) %all-to-all-start.3) | async-done | bytes 1572896 | tf_op jit(solution)/shard_map/all_to_all | solution.py:157
  555.6 8.3 copy.282
  574.2 10.3 %fusion.167 = f32[768,3072]{1,0:T(8,128)} fusion(bf16[1024,768]{1,0:T(8,128)(2,1)} %bitcast.13, bf16[1024,3072]{1,0:T(8,128)(2,1)} %copy-done.113), kind=kOutput, calls=%fused_computation.296 | convolution fusion | flops 4831838208 | bytes 17301504 | tf_op jit(solution)/shard_map/rd,rf->df/dot_general | solution.py:190
  593.1 10.7 %fusion.30 = bf16[1,768,3072]{2,1,0:T(8,128)(2,1)} fusion(f32[768,3072]{1,0:T(8,128)} %fusion.167, bf16[1024,768]{1,0:T(8,128)(2,1)} %bitcast.28, bf16[1024,3072]{1,0:T(8,128)(2,1)} %copy-done.12), kind=kOutput, calls=%fused_computation.53 | convolution fusion | flops 4836556800 | bytes 22020096 | tf_op jit(solution)/shard_map/rd,rf->df/dot_general | solution.py:190
  603.9 10.6 %fusion.151 = f32[3072,768]{1,0:T(8,128)S(1)} fusion(bf16[1024,768]{1,0:T(8,128)(2,1)} %bitcast.220, f32[1024,3072]{1,0:T(8,128)} %fusion.28), kind=kOutput, calls=%fused_computation.282 | convolution fusion | flops 4860149760 | bytes 23592960 | tf_op jit(solution)/shard_map/rf,rd->fd/dot_general | solution.py:183
  614.5 12.2 %fusion.31 = bf16[1,3072,768]{2,1,0:T(8,128)(2,1)} fusion(f32[3072,768]{1,0:T(8,128)S(1)} %fusion.151, bf16[1024,768]{1,0:T(8,128)(2,1)S(1)} %bitcast.223, f32[1024,3072]{1,0:T(8,128)} %fusion.26), kind=kOutput, calls=%fused_computation.54 | convolution fusion | flops 4864868352 | bytes 28311552 | tf_op jit(solution)/shard_map/rf,rd->fd/dot_general | solution.py:183
  630.3 37.3 %pmax.7 = f32[12]{0:T(128)S(1)} all-reduce(f32[12]{0:T(128)S(1)} %max.8), channel_id=1, replica_groups=mesh['dp'=4,'expert'=8] {'dp','expert'}, use_global_device_ids=true, to_apply=%region_60.62 | all-reduce | flops 12 | bytes 96 | tf_op jit(solution)/shard_map/pmax | solution.py:257
  683.0 17.2 %reduce-scatter.21.cloned.1.call-done = bf16[192,8]{1,0:T(8,128)(2,1)} async-done(((bf16[768,8]{1,0:T(8,128)(2,1)}), bf16[192,8]{1,0:T(8,128)(2,1)}) %reduce-scatter.21.cloned.1.call-update) | async-done | bytes 3088
  701.0 16.1 %all-reduce.2 = (bf16[192,8]{0,1:T(8,128)(2,1)S(1)}, bf16[2,192]{1,0:T(2,128)(2,1)S(1)}) all-reduce(bf16[192,8]{0,1:T(8,128)(2,1)S(1)} %copy.285, bf16[2,192]{1,0:T(2,128)(2,1)S(1)} %copy.287), channel_id=1, replica_groups=mesh['dp'=4,'expert'=8] {'expert'}, use_global_device_ids=true, to_apply=%region_48.50 | all-reduce | flops 1920 | bytes 7680 | tf_op jit(solution)/shard_map/psum | solution.py:262
  718.3 41.9 %reduce-scatter.13.cloned.1.call-done = bf16[1,192,3072]{2,1,0:T(8,128)(2,1)} async-done(((bf16[1,768,3072]{2,1,0:T(8,128)(2,1)}), bf16[1,192,3072]{2,1,0:T(8,128)(2,1)}) %reduce-scatter.13.cloned.1.call-update) | async-done | bytes 1179664 | tf_op jit(solution)/shard_map/reduce_scatter | solution.py:280
  763.2 57.2 %reduce-scatter.15.cloned.1.call-done = bf16[1,768,768]{2,1,0:T(8,128)(2,1)} async-done(((bf16[1,3072,768]{2,1,0:T(8,128)(2,1)}), bf16[1,768,768]{2,1,0:T(8,128)(2,1)}) %reduce-scatter.15.cloned.1.call-update) | async-done | bytes 1179664 | tf_op jit(solution)/shard_map/reduce_scatter | solution.py:283
  823.2 60.8 %all-reduce.6.cloned.1.call-done = (bf16[3,192,768]{1,2,0:T(8,128)(2,1)}, bf16[192,768]{1,0:T(8,128)(2,1)}) async-done(((bf16[3,192,768]{1,2,0:T(8,128)(2,1)}, bf16[192,768]{1,0:T(8,128)(2,1)}), (bf16[3,192,768]{1,2,0:T(8,128)(2,1)}, bf16[192,768]{1,0:T(8,128)(2,1)})) %all-reduce.6.cloned.1.call-update) | async-done | bytes 1179664 | tf_op jit(solution)/shard_map/psum | solution.py:260
  (475 shorter events, 306.4 us)
Async XLA Ops:
  7.2 52.7 %all-gather.5.cloned.1.call-start = ((), (), s32[]{:S(2)}) async-start(), calls=%async_computation.14 | async-start | bytes 4423680 | tf_op jit(solution)/shard_map/all_gather | solution.py:38
  7.9 81.5 %all-gather.7.cloned.1.call-start = ((), (), s32[]{:S(2)}) async-start(), calls=%async_computation.15 | async-start | bytes 1474560 | tf_op jit(solution)/shard_map/all_gather | solution.py:39
  10.3 49.6 %copy-start.86 = (f32[394]{0:T(512)}, f32[394]{0:T(512)S(1)}, u32[]{:S(2)}) copy-start(f32[394]{0:T(512)S(1)} %get-tuple-element.130) | copy-start | bytes 4732
  10.3 81.8 %copy-start.74 = (f32[394]{0:T(512)}, f32[394]{0:T(512)S(1)}, u32[]{:S(2)}) copy-start(f32[394]{0:T(512)S(1)} %get-tuple-element.131) | copy-start | bytes 4732
  10.9 49.0 %copy-start.94 = (f32[394]{0:T(512)}, f32[394]{0:T(512)S(1)}, u32[]{:S(2)}) copy-start(f32[394]{0:T(512)S(1)} %fusion.144) | copy-start | bytes 4732
  20.6 71.5 %copy-start.64 = (f32[768]{0:T(1024)}, f32[768]{0:T(1024)S(1)}, u32[]{:S(2)}) copy-start(f32[768]{0:T(1024)S(1)} %get-tuple-element.72) | copy-start | bytes 9220
  20.6 106.6 %copy-start.66 = (f32[768]{0:T(1024)}, f32[768]{0:T(1024)S(1)}, u32[]{:S(2)}) copy-start(f32[768]{0:T(1024)S(1)} %get-tuple-element.71) | copy-start | bytes 9220
  24.5 39.2 %copy-start.62 = (s32[394,2]{0,1:T(2,128)}, s32[394,2]{0,1:T(2,128)S(1)}, u32[]{:S(2)}) copy-start(s32[394,2]{0,1:T(2,128)S(1)} %copy.207) | copy-start | bytes 9460
  27.4 36.3 %copy-start.76 = (s32[788]{0:T(1024)}, s32[788]{0:T(1024)S(1)}, u32[]{:S(2)}) copy-start(s32[788]{0:T(1024)S(1)} %fusion.127) | copy-start | bytes 9460
  27.7 36.0 %copy-start.60 = (s32[394,2]{0,1:T(2,128)}, s32[394,2]{0,1:T(2,128)S(1)}, u32[]{:S(2)}) copy-start(s32[394,2]{0,1:T(2,128)S(1)} %copy.225) | copy-start | bytes 9460
  34.0 58.1 %copy-start.92 = (f32[394]{0:T(512)}, f32[394]{0:T(512)S(1)}, u32[]{:S(2)}) copy-start(f32[394]{0:T(512)S(1)} %fusion.142) | copy-start | bytes 4732
  91.7 35.5 %copy-start.2 = (f32[394,768]{1,0:T(8,128)}, f32[394,768]{1,0:T(8,128)S(1)}, u32[]{:S(2)}) copy-start(f32[394,768]{1,0:T(8,128)S(1)} %get-tuple-element.123) | copy-start | bytes 3631108
  91.8 35.5 %copy-start.70 = (f32[394]{0:T(512)}, f32[394]{0:T(512)S(1)}, u32[]{:S(2)}) copy-start(f32[394]{0:T(512)S(1)} %broadcast_multiply_fusion) | copy-start | bytes 4732
  127.9 56.4 %copy-start.13 = (bf16[394,768]{1,0:T(8,128)(2,1)}, bf16[394,768]{1,0:T(8,128)(2,1)S(1)}, u32[]{:S(2)}) copy-start(bf16[394,768]{1,0:T(8,128)(2,1)S(1)} %get-tuple-element.115) | copy-start | bytes 1815556
  130.7 43.8 %all-to-all-start = ((bf16[8,128,768]{2,1,0:T(8,128)(2,1)}), bf16[8,128,768]{2,1,0:T(8,128)(2,1)}, u32[]{:S(2)}, u32[]{:S(2)}) async-start(bf16[8,128,768]{2,1,0:T(8,128)(2,1)} %bitcast.224), calls=%async_computation | async-start | bytes 3145728 | tf_op jit(solution)/shard_map/all_to_all | solution.py:154
  174.4 42.9 %all-to-all-start.4 = ((bf16[8,128,768]{2,1,0:T(8,128)(2,1)}), bf16[8,128,768]{2,1,0:T(8,128)(2,1)S(1)}, u32[]{:S(2)}, u32[]{:S(2)}) async-start(bf16[8,128,768]{2,1,0:T(8,128)(2,1)} %bitcast.228), calls=%async_computation.4 | async-start | bytes 3145728 | tf_op jit(solution)/shard_map/all_to_all | solution.py:175
  217.3 42.1 %all-to-all-start.2 = ((bf16[8,128,768]{2,1,0:T(8,128)(2,1)}), bf16[8,128,768]{2,1,0:T(8,128)(2,1)}, u32[]{:S(2)}, u32[]{:S(2)}) async-start(bf16[8,128,768]{2,1,0:T(8,128)(2,1)} %bitcast.227), calls=%async_computation.2 | async-start | bytes 3145728 | tf_op jit(solution)/shard_map/all_to_all | solution.py:154
  259.5 41.5 %all-to-all-start.6 = ((bf16[8,128,768]{2,1,0:T(8,128)(2,1)}), bf16[8,128,768]{2,1,0:T(8,128)(2,1)S(1)}, u32[]{:S(2)}, u32[]{:S(2)}) async-start(bf16[8,128,768]{2,1,0:T(8,128)(2,1)} %bitcast.229), calls=%async_computation.6 | async-start | bytes 3145728 | tf_op jit(solution)/shard_map/all_to_all | solution.py:175
  301.0 46.1 %copy-start.39 = (bf16[8,128,768]{2,1,0:T(8,128)(2,1)}, bf16[8,128,768]{2,1,0:T(8,128)(2,1)S(1)}, u32[]{:S(2)}) copy-start(bf16[8,128,768]{2,1,0:T(8,128)(2,1)S(1)} %all-to-all-done.6) | copy-start | bytes 4718596
  301.0 41.3 %all-to-all-start.5 = ((bf16[8,128,768]{2,1,0:T(8,128)(2,1)}), bf16[8,128,768]{2,1,0:T(8,128)(2,1)S(1)}, u32[]{:S(2)}, u32[]{:S(2)}) async-start(bf16[8,128,768]{2,1,0:T(8,128)(2,1)} %bitcast.230), calls=%async_computation.5 | async-start | bytes 3145728 | tf_op jit(solution)/shard_map/all_to_all | solution.py:195
  342.4 42.5 %all-to-all-start.1 = ((bf16[8,128,768]{2,1,0:T(8,128)(2,1)}), bf16[8,128,768]{2,1,0:T(8,128)(2,1)}, u32[]{:S(2)}, u32[]{:S(2)}) async-start(bf16[8,128,768]{2,1,0:T(8,128)(2,1)} %bitcast.231), calls=%async_computation.1 | async-start | bytes 3145728 | tf_op jit(solution)/shard_map/all_to_all | solution.py:157
  384.9 41.3 %all-to-all-start.7 = ((bf16[8,128,768]{2,1,0:T(8,128)(2,1)}), bf16[8,128,768]{2,1,0:T(8,128)(2,1)S(1)}, u32[]{:S(2)}, u32[]{:S(2)}) async-start(bf16[8,128,768]{2,1,0:T(8,128)(2,1)} %bitcast.43), calls=%async_computation.7 | async-start | bytes 3145728 | tf_op jit(solution)/shard_map/all_to_all | solution.py:195
  426.3 42.1 %all-to-all-start.3 = ((bf16[8,128,768]{2,1,0:T(8,128)(2,1)}), bf16[8,128,768]{2,1,0:T(8,128)(2,1)}, u32[]{:S(2)}, u32[]{:S(2)}) async-start(bf16[8,128,768]{2,1,0:T(8,128)(2,1)} %bitcast.29), calls=%async_computation.3 | async-start | bytes 3145728 | tf_op jit(solution)/shard_map/all_to_all | solution.py:157
  430.6 240.7 %reduce-scatter.19.cloned.1.call-start = ((), (), s32[]{:S(2)}) async-start(), calls=%async_computation.19 | async-start | bytes 4423680
  568.7 109.0 %reduce-scatter.17.cloned.1.call-start = ((), (), s32[]{:S(2)}) async-start(), calls=%async_computation.18 | async-start | bytes 1474560 | tf_op jit(solution)/shard_map/reduce_scatter | solution.py:269
  574.2 107.9 %reduce-scatter.23.cloned.1.call-start = ((), (), s32[]{:S(2)}) async-start(), calls=%async_computation.21 | async-start | bytes 245760
  592.0 108.1 %reduce-scatter.21.cloned.1.call-start = ((), (), s32[]{:S(2)}) async-start(), calls=%async_computation.20 | async-start | bytes 245760
  593.1 167.2 %reduce-scatter.13.cloned.1.call-start = ((), (), s32[]{:S(2)}) async-start(), calls=%async_computation.16 | async-start | bytes 5898240 | tf_op jit(solution)/shard_map/reduce_scatter | solution.py:280
  603.8 216.5 %reduce-scatter.15.cloned.1.call-start = ((), (), s32[]{:S(2)}) async-start(), calls=%async_computation.17 | async-start | bytes 5898240 | tf_op jit(solution)/shard_map/reduce_scatter | solution.py:283
  626.7 257.3 %all-reduce.6.cloned.1.call-start = ((), (), s32[]{:S(2)}) async-start(), calls=%async_computation.22 | async-start | bytes 2949120 | tf_op jit(solution)/shard_map/psum | solution.py:260
  629.3 38.3 %copy-start.111 = (f32[12]{0:T(128)S(1)}, f32[12]{0:T(128)}, u32[]{:S(2)}) copy-start(f32[12]{0:T(128)} %param.20) | copy-start | bytes 148
  630.3 39.7 %copy-start.32 = (bf16[394,768]{1,0:T(8,128)(2,1)S(1)}, bf16[394,768]{1,0:T(8,128)(2,1)}, u32[]{:S(2)}) copy-start(bf16[394,768]{1,0:T(8,128)(2,1)} %get-tuple-element.97) | copy-start | bytes 1815556
  (105 other events, 499.4 us)
Sparse Core Ops, SparseCore 0:
  9.9 49.9 all-gather.4
  61.7 27.7 all-gather.6
  568.8 45.1 reduce-scatter.18
  616.8 28.8 reduce-scatter.16
  648.8 23.9 reduce-scatter.22
  676.0 24.0 reduce-scatter.20
  703.1 57.0 reduce-scatter.12
  763.2 57.0 reduce-scatter.14
  822.8 61.1 all-reduce.5
where the time goes:
time: 904 us; the launch traced here: 894 us
  waiting for transfers between devices  337 us (37%)
  matrix products  237 us (26%)
  local copies, waits for them, and re-layouts  151 us (17%)
  blocking collectives  71.1 us (8%)
  other arithmetic  46.9 us (5%)
  starting transfers between devices  34.6 us (4%)
  between operations  16.1 us (2%)
    psum x1, waiting for transfers between devices, per_device(): lax.psum(attn_grads[0].astype(jnp.bfloat16), 'expert').astype(jnp.float32)  60.8 us
    reduce_scatter x1, waiting for transfers between devices, per_device(): lax.psum_scatter(grad_out[None].astype(jnp.bfloat16), 'dp', scatter_dimen...  57.2 us
    unnamed x255, local copies, waits for them, and re-layouts  44.5 us
    reduce_scatter x1, waiting for transfers between devices, per_device(): lax.psum_scatter(grad_in[None].astype(jnp.bfloat16), 'dp', scatter_dimens...  41.9 us
    all_to_all x2, waiting for transfers between devices, per_device(): lax.all_to_all(grad_buffer, 'expert', split_axis=0, concat_axis=0, tiled=...  41.1 us
    all_to_all x2, waiting for transfers between devices, per_device(): lax.all_to_all(grad_sent, 'expert', split_axis=0, concat_axis=0, tiled=True)  40.4 us
    pmax x1, blocking collectives, per_device(): head_max = lax.pmax(running, ('dp', 'expert'))  37.3 us
    dot_general x2, matrix products, per_device(): jnp.einsum('rd,fd->rf', grad_rows, weight_out, preferred_element_type=jnp...  32.5 us
  transfers between devices with their start and end apart: 17, of which 13 were waited for; matrix products, arithmetic and copies ran while one was open for 32% of the time, Pallas kernels for 0%

commit v1 on v0

v1 whole, which is shorter than its diff:
```python
import jax
import jax.numpy as jnp
from jax import lax
from jax.sharding import PartitionSpec as P

D = 768
HEADS = 12
HEAD_DIM = 64
FF = 3072
SEQ = 197
IMG_DEV = 2
MB = 2
TOK_MB = 394


epsilon = 1e-06
qk_scale = 0.125
gelu_coeff = 0.7978845608028654


def norm_parts(values_in):
    row_mean = jnp.mean(values_in, axis=-1, keepdims=True)
    centred = values_in - row_mean
    row_var = jnp.mean(centred * centred, axis=-1, keepdims=True)
    inverse = lax.rsqrt(row_var + epsilon)
    return centred * inverse, inverse


def norm_back(unit, inverse, gain_row, incoming):
    scaled = incoming * gain_row
    mean_one = jnp.mean(scaled, axis=-1, keepdims=True)
    mean_two = jnp.mean(scaled * unit, axis=-1, keepdims=True)
    return (scaled - mean_one - unit * mean_two) * inverse, jnp.sum(incoming * unit, axis=0)


def gelu_both(values_in):
    squared = values_in * values_in
    inner = gelu_coeff * (values_in + 0.044715 * squared * values_in)
    bent = jnp.tanh(inner)
    value = 0.5 * values_in * (1.0 + bent)
    slope = 0.5 * (1.0 + bent) + 0.5 * values_in * (1.0 - bent * bent) * gelu_coeff * (
        1.0 + 3.0 * 0.044715 * squared
    )
    return value, slope


def attention_forward(tokens_wide, gain_row, qkv_weight, out_weight):
    unit, inverse = norm_parts(tokens_wide)
    first_norm = (unit * gain_row).astype(jnp.bfloat16)
    projected = jnp.einsum(
        "td,cde->cte", first_norm, qkv_weight, preferred_element_type=jnp.float32
    ).astype(jnp.bfloat16)
    split_heads = projected.reshape(3, IMG_DEV, SEQ, HEADS, HEAD_DIM)
    scores = (
        jnp.einsum(
            "bqhd,bkhd->bhqk", split_heads[0], split_heads[1], preferred_element_type=jnp.float32
        )
        * qk_scale
    )
    row_top = jnp.max(scores, axis=-1, keepdims=True)
    exp_scores = jnp.exp(scores - row_top)
    attn_probs = exp_scores / jnp.sum(exp_scores, axis=-1, keepdims=True)
    probs_low = attn_probs.astype(jnp.bfloat16)
    mixed_heads = jnp.einsum(
        "bhqk,bkhd->bqhd", probs_low, split_heads[2], preferred_element_type=jnp.float32
    ).astype(jnp.bfloat16)
    mixed_flat = mixed_heads.reshape(TOK_MB, D)
    residual = tokens_wide + jnp.dot(mixed_flat, out_weight, preferred_element_type=jnp.float32)
    head_top = jnp.max(row_top, axis=(0, 2, 3))
    return dict(
        unit=unit,
        inverse=inverse,
        first_norm=first_norm,
        split_heads=split_heads,
        probs=attn_probs,
        probs_low=probs_low,
        mixed=mixed_flat,
        residual=residual,
        head_top=head_top,
    )


def attention_backward(kept, grad_attended, qkv_weight, out_weight):
    split_heads = kept["split_heads"]
    grad_mixed = jnp.einsum(
        "te,de->td", grad_attended, out_weight, preferred_element_type=jnp.float32
    )
    grad_mixed = grad_mixed.astype(jnp.bfloat16).reshape(IMG_DEV, SEQ, HEADS, HEAD_DIM)
    grad_probs = jnp.einsum(
        "bqhd,bkhd->bhqk", grad_mixed, split_heads[2], preferred_element_type=jnp.float32
    )
    grad_values = jnp.einsum(
        "bhqk,bqhd->bkhd", kept["probs_low"], grad_mixed, preferred_element_type=jnp.float32
    )
    row_dot = jnp.sum(kept["probs"] * grad_probs, axis=-1, keepdims=True)
    grad_scores = (kept["probs"] * (grad_probs - row_dot)).astype(jnp.bfloat16)
    grad_queries = (
        jnp.einsum(
            "bhqk,bkhd->bqhd", grad_scores, split_heads[1], preferred_element_type=jnp.float32
        )
        * qk_scale
    )
    grad_keys = (
        jnp.einsum(
            "bhqk,bqhd->bkhd", grad_scores, split_heads[0], preferred_element_type=jnp.float32
        )
        * qk_scale
    )
    grad_proj = [
        part.astype(jnp.bfloat16).reshape(TOK_MB, D)
        for part in (grad_queries, grad_keys, grad_values)
    ]
    grad_first = sum(
        jnp.einsum("te,de->td", grad_proj[c], qkv_weight[c], preferred_element_type=jnp.float32)
        for c in range(3)
    )
    return grad_proj, grad_first


def slot_numbers(route_rows, experts, capacity):
    flat_expert = route_rows.reshape(-1)
    onehot = (flat_expert[:, None] == jnp.arange(experts, dtype=jnp.int32)[None, :]).astype(
        jnp.int32
    )
    before = jnp.cumsum(onehot, axis=0) - onehot
    slot_index = jnp.sum(before * onehot, axis=1)
    kept = slot_index < capacity
    slot_ids = jnp.where(kept, flat_expert * capacity + slot_index, -1)
    return slot_ids.reshape(-1, 2), kept.reshape(-1, 2).astype(jnp.float32)


def exchange(rows):
    return lax.all_to_all(rows, "expert", split_axis=0, concat_axis=0, tiled=True)


def per_device(
    tokens,
    attn_qkv,
    attn_out,
    router,
    norm_gains,
    expert_in,
    expert_out,
    routes,
    clip_limit,
    cotangent,
):
    devices = lax.axis_size("expert")
    experts = devices * expert_in.shape[0]
    capacity = max(8, (TOK_MB * 10 // (4 * experts) + 7) // 8 * 8)
    slots = experts * capacity
    weight_in = expert_in[0]
    weight_out = expert_out[0]
    expert_ids = jnp.arange(experts, dtype=jnp.int32)
    slot_ids_all = jnp.arange(slots, dtype=jnp.int32)

    def block(array, index):
        return lax.slice_in_dim(array, index * TOK_MB, (index + 1) * TOK_MB, axis=0)

    tables, cot_arrived = [], []
    for index in range(MB):
        slot_ids, kept = slot_numbers(block(routes, index), experts, capacity)
        pick = [(slot_ids_all[:, None] == slot_ids[None, :, k]) for k in range(2)]
        token_pick = (pick[0] | pick[1]).astype(jnp.bfloat16)
        tables.append((kept, pick, token_pick))
        packed = jnp.dot(
            token_pick, block(cotangent, index), preferred_element_type=jnp.float32
        ).astype(jnp.bfloat16)
        cot_arrived.append(exchange(packed.reshape(experts, capacity, D)).reshape(slots, D))

    gains = lax.all_gather(norm_gains, "dp", axis=1, tiled=True).astype(jnp.float32)
    qkv_weight = lax.all_gather(attn_qkv, "dp", axis=1, tiled=True)
    out_weight = lax.all_gather(attn_out, "dp", axis=0, tiled=True)
    router_weight = lax.all_gather(router, "dp", axis=0, tiled=True)

    keeps, mids = [], []
    for index in range(MB):
        kept, pick, token_pick = tables[index]
        kept_rows = attention_forward(
            block(tokens, index).astype(jnp.float32), gains[0], qkv_weight, out_weight
        )
        unit_two, inverse_two = norm_parts(kept_rows["residual"])
        second_norm = (unit_two * gains[1]).astype(jnp.bfloat16)
        logits = jnp.dot(second_norm, router_weight, preferred_element_type=jnp.float32)
        named = block(routes, index)[:, :, None] == expert_ids[None, None, :]
        chosen = jnp.sum(jnp.where(named, logits[:, None, :], 0.0), axis=2)
        exp_chosen = jnp.exp(chosen - jnp.max(chosen, axis=1, keepdims=True))
        gate = exp_chosen / jnp.sum(exp_chosen, axis=1, keepdims=True)
        packed = jnp.dot(token_pick, second_norm, preferred_element_type=jnp.float32)
        arrived = exchange(packed.astype(jnp.bfloat16).reshape(experts, capacity, D))
        slot_gate = sum(
            jnp.sum(jnp.where(pick[k], gate[None, :, k], 0.0), axis=1) for k in range(2)
        )
        gate_arrived = exchange(slot_gate.reshape(experts, capacity))
        keeps.append(kept_rows)
        mids.append(
            dict(
                unit=unit_two,
                inverse=inverse_two,
                norm=second_norm,
                gate=gate,
                named=named,
                arrived=arrived.reshape(slots, D),
                gate_arrived=gate_arrived.reshape(slots, 1),
            )
        )

    head_top = jnp.maximum(keeps[0]["head_top"], keeps[1]["head_top"])

    returned, grad_back, gate_back, hiddens, grad_pres, grad_rows_all = [], [], [], [], [], []
    for index in range(MB):
        mid = mids[index]
        cot_wide = cot_arrived[index].astype(jnp.float32)
        pre_act = jnp.dot(mid["arrived"], weight_in, preferred_element_type=jnp.float32)
        value, slope = gelu_both(pre_act)
        hidden = value.astype(jnp.bfloat16)
        grad_rows = (mid["gate_arrived"] * cot_wide).astype(jnp.bfloat16)
        grad_hidden = jnp.einsum(
            "rd,fd->rf", grad_rows, weight_out, preferred_element_type=jnp.float32
        )
        grad_pre = (grad_hidden * slope).astype(jnp.bfloat16)
        grad_sent = jnp.einsum("rf,df->rd", grad_pre, weight_in, preferred_element_type=jnp.float32)
        grad_back.append(
            exchange(grad_sent.astype(jnp.bfloat16).reshape(experts, capacity, D)).reshape(slots, D)
        )
        produced = jnp.dot(hidden, weight_out, preferred_element_type=jnp.float32)
        gate_grad = jnp.sum(produced * cot_wide, axis=1)
        gate_back.append(exchange(gate_grad.reshape(experts, capacity)).reshape(slots))
        returned.append(
            exchange(
                (produced * mid["gate_arrived"])
                .astype(jnp.bfloat16)
                .reshape(experts, capacity, D)
            ).reshape(slots, D)
        )
        hiddens.append(hidden)
        grad_pres.append(grad_pre)
        grad_rows_all.append(grad_rows)

    grad_out = jnp.einsum(
        "rf,rd->fd",
        jnp.concatenate(hiddens, axis=0),
        jnp.concatenate(grad_rows_all, axis=0),
        preferred_element_type=jnp.float32,
    ).astype(jnp.bfloat16)
    grad_out_share = lax.psum_scatter(grad_out[None], "dp", scatter_dimension=1, tiled=True)
    grad_in = jnp.einsum(
        "rd,rf->df",
        jnp.concatenate([mid["arrived"] for mid in mids], axis=0),
        jnp.concatenate(grad_pres, axis=0),
        preferred_element_type=jnp.float32,
    ).astype(jnp.bfloat16)
    grad_in_share = lax.psum_scatter(grad_in[None], "dp", scatter_dimension=1, tiled=True)

    out_blocks, input_grads = [], []
    grad_gain_one, grad_gain_two = 0.0, 0.0
    attended_all, proj_all, logit_all = [], [], []
    for index in range(MB):
        kept, pick, token_pick = tables[index]
        mid, kept_rows = mids[index], keeps[index]
        cot_wide = block(cotangent, index).astype(jnp.float32)
        grad_gate = jnp.stack(
            [
                jnp.sum(jnp.where(pick[k], gate_back[index][:, None], 0.0), axis=0)
                for k in range(2)
            ],
            axis=1,
        )
        grad_chosen = mid["gate"] * (
            grad_gate - jnp.sum(mid["gate"] * grad_gate, axis=1, keepdims=True)
        )
        grad_logits = jnp.sum(
            jnp.where(mid["named"], grad_chosen[:, :, None], 0.0), axis=1
        ).astype(jnp.bfloat16)
        grad_second = jnp.einsum(
            "sp,sd->pd", token_pick, grad_back[index], preferred_element_type=jnp.float32
        ) + jnp.einsum(
            "te,de->td", grad_logits, router_weight, preferred_element_type=jnp.float32
        )
        grad_resid_norm, gain_two = norm_back(mid["unit"], mid["inverse"], gains[1], grad_second)
        grad_resid = cot_wide + grad_resid_norm
        grad_attended = grad_resid.astype(jnp.bfloat16)
        grad_proj, grad_first = attention_backward(
            kept_rows, grad_attended, qkv_weight, out_weight
        )
        grad_tokens, gain_one = norm_back(
            kept_rows["unit"], kept_rows["inverse"], gains[0], grad_first
        )
        input_grads.append((grad_resid + grad_tokens).astype(jnp.bfloat16))
        grad_gain_one += gain_one
        grad_gain_two += gain_two
        attended_all.append(grad_attended)
        proj_all.append(grad_proj)
        logit_all.append(grad_logits)

    def joined(parts):
        return jnp.concatenate(parts, axis=0)

    first_all = joined([kept_rows["first_norm"] for kept_rows in keeps])
    grad_qkv = [
        jnp.einsum(
            "td,te->de",
            first_all,
            joined([grad_proj[c] for grad_proj in proj_all]),
            preferred_element_type=jnp.float32,
        )
        for c in range(3)
    ]
    grad_attn = jnp.einsum(
        "td,te->de",
        joined([kept_rows["mixed"] for kept_rows in keeps]),
        joined(attended_all),
        preferred_element_type=jnp.float32,
    )
    grad_route = jnp.einsum(
        "td,te->de",
        joined([mid["norm"] for mid in mids]),
        joined(logit_all),
        preferred_element_type=jnp.float32,
    )
    small = jnp.concatenate(
        [grad_route, jnp.stack([grad_gain_one, grad_gain_two], axis=1)], axis=1
    )
    packed_grads = jnp.concatenate(grad_qkv + [grad_attn, small], axis=1).astype(jnp.bfloat16)
    share = lax.psum_scatter(packed_grads, "dp", scatter_dimension=0, tiled=True)
    share = lax.psum(share, "expert").astype(jnp.float32)

    for index in range(MB):
        combined = jnp.einsum(
            "sp,sd->pd", tables[index][2], returned[index], preferred_element_type=jnp.float32
        )
        out_blocks.append((keeps[index]["residual"] + combined).astype(jnp.bfloat16))

    head_max = lax.pmax(head_top, ("dp", "expert"))
    factor = clip_limit / jnp.maximum(head_max, clip_limit)
    root_scale = jnp.repeat(jnp.sqrt(factor), HEAD_DIM)
    clipped_qk = attn_qkv[:2].astype(jnp.float32) * root_scale[None, None, :]
    return (
        jnp.concatenate(out_blocks, axis=0),
        jnp.concatenate(input_grads, axis=0),
        jnp.stack([share[:, c * D : (c + 1) * D] for c in range(3)]),
        share[:, 3 * D : 4 * D],
        share[:, 4 * D : 4 * D + experts],
        share[:, 4 * D + experts :].T,
        grad_in_share.astype(jnp.float32),
        grad_out_share.astype(jnp.float32),
        head_max,
        clipped_qk,
    )


def solution(mesh):
    placed = (
        P(("dp", "expert"), None),
        P(None, "dp", None),
        P("dp", None),
        P("dp", None),
        P(None, "dp"),
        P("expert", None, None),
        P("expert", None, None),
        P(("dp", "expert"), None),
        P(),
        P(("dp", "expert"), None),
    )
    return jax.shard_map(
        per_device,
        mesh=mesh,
        in_specs=placed,
        out_specs=(
            P(("dp", "expert"), None),
            P(("dp", "expert"), None),
            P(None, "dp", None),
            P("dp", None),
            P("dp", None),
            P(None, "dp"),
            P("expert", "dp", None),
            P("expert", "dp", None),
            P(),
            P(None, "dp", None),
        ),
        check_vma=False,
    )
```

time: 904 us -> 836 us (0.925)
  waiting for transfers between devices: 337 us -> 275 us
  blocking collectives: 71.1 us -> 122 us
  local copies, waits for them, and re-layouts: 151 us -> 119 us
  matrix products: 237 us -> 212 us
    reduce_scatter x3 -> x2, waiting for transfers between devices: 99.1 us -> 17.8 us  [the longest x1 17.7 us: per_device(): lax.psum_scatter(grad_in[None], 'dp', scatter_dimension=1, tiled=True)]
    all_to_all x0 -> x2, blocking collectives: none -> 50.3 us  [exchange(): lax.all_to_all(rows, 'expert', split_axis=0, concat_axis=0, tiled=True)]
    all_to_all x8 -> x10, waiting for transfers between devices: 130 us -> 159 us  [exchange(): lax.all_to_all(rows, 'expert', split_axis=0, concat_axis=0, tiled=True)]
    another operation x18 -> x5, local copies, waits for them, and re-layouts: 28 us -> 0.54 us  [the longest x14 27.6 us: per_device(): jnp.stack([grad_queries, grad_keys, grad_values]).astype(jnp.bfloat16)]
    unnamed x255 -> x183, local copies, waits for them, and re-layouts: 44.5 us -> 20 us
    concatenate x0 -> x1, local copies, waits for them, and re-layouts: none -> 24.4 us  [per_device(): jnp.concatenate(grad_qkv + [grad_attn, small], axis=1).astype(jnp.bfloat16)]
    gather x10 -> x0, local copies, waits for them, and re-layouts: 17.6 us -> none  [route_gates(): chosen = jnp.take_along_axis(logits, route_rows, axis=1)]
    unnamed x12 -> x7, waiting for transfers between devices: 18.7 us -> 1.46 us
  transfers between devices with their start and end apart: 17 -> 16, of which waited for: 13 -> 13; matrix products, arithmetic and copies ran while one was open for 32% -> 21% of each run, Pallas kernels for 0% -> 0%
where the time goes in v1:
time: 836 us; the launch traced here: 826 us
  waiting for transfers between devices  275 us (33%)
  matrix products  212 us (25%)
  blocking collectives  122 us (15%)
  local copies, waits for them, and re-layouts  119 us (14%)
  starting transfers between devices  42.2 us (5%)
  other arithmetic  40.9 us (5%)
  between operations  15.6 us (2%)
    all_to_all x10, waiting for transfers between devices, exchange(): lax.all_to_all(rows, 'expert', split_axis=0, concat_axis=0, tiled=True)  159 us
    psum x1, waiting for transfers between devices, per_device(): share = lax.psum(share, 'expert').astype(jnp.float32)  61 us
    pmax x1, blocking collectives, per_device(): head_max = lax.pmax(head_top, ('dp', 'expert'))  54.2 us
    all_to_all x2, blocking collectives, exchange(): lax.all_to_all(rows, 'expert', split_axis=0, concat_axis=0, tiled=True)  50.3 us
    all_to_all x10, starting transfers between devices, exchange(): lax.all_to_all(rows, 'expert', split_axis=0, concat_axis=0, tiled=True)  41.9 us
    all_gather x1, waiting for transfers between devices, per_device(): qkv_weight = lax.all_gather(attn_qkv, 'dp', axis=1, tiled=True)  34.5 us
    dot_general x2, matrix products, per_device(): jnp.einsum('rd,fd->rf', grad_rows, weight_out, preferred_element_type=jnp...  26.1 us
    dot_general x2, matrix products, per_device(): jnp.dot(mid['arrived'], weight_in, preferred_element_type=jnp.float32)  25.2 us
  transfers between devices with their start and end apart: 16, of which 13 were waited for; matrix products, arithmetic and copies ran while one was open for 21% of the time, Pallas kernels for 0%

profile of v1, /device:TPU:0, one launch (start us, length us, event | category | flops | bytes accessed | tf_op | source)
XLA Modules:
  0.0 826.5 jit_solution(11292253524056074236)
XLA Ops:
  10.9 9.5 %all-gather = bf16[4,192,2]{1,2,0:T(2,128)(2,1)S(1)} all-gather(bf16[1,192,2]{1,2,0:T(2,128)(2,1)S(1)} %bitcast.278), channel_id=1, replica_groups=mesh['dp'=4,'expert'=8] {'dp'}, dimensions={0}, use_global_device_ids=true | all-gather | bytes 3840 | tf_op jit(solution)/shard_map/all_gather | solution.py:171
  25.4 34.5 %all-gather.5.cloned.1.call-done = bf16[3,768,768]{2,1,0:T(8,128)(2,1)} async-done(((bf16[3,192,768]{2,1,0:T(8,128)(2,1)}), bf16[3,768,768]{2,1,0:T(8,128)(2,1)}) %all-gather.5.cloned.1.call-update) | async-done | bytes 3538960 | tf_op jit(solution)/shard_map/all_gather | solution.py:172
  94.6 4.7 all-to-all-start
  99.3 8.1 all-gather.1
  113.8 23.5 %all-to-all-done = bf16[8,128,768]{2,1,0:T(8,128)(2,1)} async-done(((bf16[8,128,768]{2,1,0:T(8,128)(2,1)}), bf16[8,128,768]{2,1,0:T(8,128)(2,1)}, u32[]{:S(2)}, u32[]{:S(2)}) %all-to-all-start) | async-done | bytes 1572896 | tf_op jit(solution)/shard_map/all_to_all | solution.py:133
  137.2 4.8 all-to-all-start.6
  143.1 12.6 %multiply_convert_fusion.3 = (bf16[1024,3072]{1,0:T(8,128)(2,1)}, f32[1024,3072]{1,0:T(8,128)}) fusion(bf16[1024,768]{1,0:T(8,128)(2,1)} %bitcast.11, bf16[1,768,3072]{2,1,0:T(8,128)(2,1)} %param.15), kind=kOutput, calls=%fused_computation.19 | convolution fusion | flops 4860149760 | bytes 25165824 | tf_op jit(solution)/shard_map/dot_general | solution.py:214
  155.7 24.2 %all-to-all-done.6 = bf16[8,128,768]{2,1,0:T(8,128)(2,1)} async-done(((bf16[8,128,768]{2,1,0:T(8,128)(2,1)}), bf16[8,128,768]{2,1,0:T(8,128)(2,1)}, u32[]{:S(2)}, u32[]{:S(2)}) %all-to-all-start.6) | async-done | bytes 1572896 | tf_op jit(solution)/shard_map/all_to_all | solution.py:133
  179.9 10.6 %fusion.56 = (f32[1024]{0:T(1024)}, f32[1024,768]{1,0:T(8,128)}) fusion(bf16[8,128,768]{2,1,0:T(8,128)(2,1)} %all-to-all-done.6, bf16[1024,3072]{1,0:T(8,128)(2,1)} %get-tuple-element.139, bf16[1,3072,768]{2,1,0:T(8,128)(2,1)} %param.16), kind=kOutput, calls=%fused_computation.66 | convolution fusion | flops 4834196480 | bytes 15732736 | tf_op jit(solution)/shard_map/dot_general | solution.py:226
  193.9 5.4 all-to-all-done.8
  204.1 4.8 convert_bitcast_fusion
  211.4 13.0 %multiply_convert_fusion.1 = bf16[1024,3072]{1,0:T(8,128)(2,1)S(1)} fusion(f32[1024,3072]{1,0:T(8,128)} %get-tuple-element.140, bf16[1024,768]{1,0:T(8,128)(2,1)S(1)} %bitcast.251, bf16[1,3072,768]{2,1,0:T(8,128)(2,1)} %param.16), kind=kOutput, calls=%fused_computation.17 | convolution fusion | flops 4888461312 | bytes 25165824 | tf_op jit(solution)/shard_map/rd,fd->rf/dot_general | solution.py:218
  224.5 6.2 fusion.60
  230.7 4.7 all-to-all-start.7
  254.5 5.2 fusion.180
  288.2 34.2 %all-to-all-done.3 = bf16[8,128,768]{2,1,0:T(8,128)(2,1)} async-done(((bf16[8,128,768]{2,1,0:T(8,128)(2,1)}), bf16[8,128,768]{2,1,0:T(8,128)(2,1)}, u32[]{:S(2)}, u32[]{:S(2)}) %all-to-all-start.3) | async-done | bytes 1572896 | tf_op jit(solution)/shard_map/all_to_all | solution.py:133
  327.1 12.6 %multiply_convert_fusion.2 = (bf16[1024,3072]{1,0:T(8,128)(2,1)}, f32[1024,3072]{1,0:T(8,128)}) fusion(bf16[1024,768]{1,0:T(8,128)(2,1)} %bitcast.29, bf16[1,768,3072]{2,1,0:T(8,128)(2,1)} %param.15), kind=kOutput, calls=%fused_computation.18 | convolution fusion | flops 4860149760 | bytes 25165824 | tf_op jit(solution)/shard_map/dot_general | solution.py:214
  339.7 24.8 %all-to-all-done.9 = bf16[8,128,768]{2,1,0:T(8,128)(2,1)} async-done(((bf16[8,128,768]{2,1,0:T(8,128)(2,1)}), bf16[8,128,768]{2,1,0:T(8,128)(2,1)}, u32[]{:S(2)}, u32[]{:S(2)}) %all-to-all-start.9) | async-done | bytes 1572896 | tf_op jit(solution)/shard_map/all_to_all | solution.py:133
  364.5 10.7 %fusion.53 = (f32[1024]{0:T(1024)}, f32[1024,768]{1,0:T(8,128)}) fusion(bf16[8,128,768]{2,1,0:T(8,128)(2,1)} %all-to-all-done.9, bf16[1024,3072]{1,0:T(8,128)(2,1)} %get-tuple-element.146, bf16[1,3072,768]{2,1,0:T(8,128)(2,1)} %param.16), kind=kOutput, calls=%fused_computation.60 | convolution fusion | flops 4834196480 | bytes 15732736 | tf_op jit(solution)/shard_map/dot_general | solution.py:226
  378.5 5.4 all-to-all-done.11
  384.9 8.2 all_to_all.70
  394.8 13.1 %multiply_convert_fusion = bf16[1024,3072]{1,0:T(8,128)(2,1)S(1)} fusion(f32[1024,3072]{1,0:T(8,128)} %get-tuple-element.147, bf16[1024,768]{1,0:T(8,128)(2,1)S(1)} %bitcast.252, bf16[1,3072,768]{2,1,0:T(8,128)(2,1)} %param.16), kind=kOutput, calls=%fused_computation.16 | convolution fusion | flops 4888461312 | bytes 25165824 | tf_op jit(solution)/shard_map/rd,fd->rf/dot_general | solution.py:218
  407.9 6.2 fusion.63
  420.1 36.3 %all-to-all-done.10 = bf16[8,128,768]{2,1,0:T(8,128)(2,1)} async-done(((bf16[8,128,768]{2,1,0:T(8,128)(2,1)}), bf16[8,128,768]{2,1,0:T(8,128)(2,1)}, u32[]{:S(2)}, u32[]{:S(2)}) %all-to-all-start.10) | async-done | bytes 1572896 | tf_op jit(solution)/shard_map/all_to_all | solution.py:133
  538.4 24.4 %concatenate.64 = bf16[768,3082]{0,1:T(8,128)(2,1)} concatenate(bf16[768,768]{0,1:T(8,128)(2,1)} %convolution_convert_fusion.7, bf16[768,768]{0,1:T(8,128)(2,1)} %convolution_convert_fusion.6, bf16[768,768]{0,1:T(8,128)(2,1)} %convolution_convert_fusion.5, bf16[768,768]{0,1:T(8,128)(2,1)} %convolution_convert_fusion.4, bf16[768,8]{0,1:T(8,128)(2,1)S(1)} %fusion.129, ...), dimensions={1} | concatenate | bytes 9467904 | tf_op jit(solution)/shard_map/concatenate | solution.py:324
  562.8 7.4 copy.328
  578.5 14.2 %fusion.34 = bf16[1,3072,768]{2,1,0:T(8,128)(2,1)} fusion(bf16[1024,3072]{1,0:T(8,128)(2,1)} %get-tuple-element.146, bf16[1024,3072]{1,0:T(8,128)(2,1)S(1)} %bitcast.284, bf16[1024,768]{1,0:T(8,128)(2,1)S(1)} %get-tuple-element.126, bf16[1024,768]{1,0:T(8,128)(2,1)S(1)} %get-tuple-element.124), kind=kOutput, calls=%fused_computation.42 | convolution fusion | flops 9697492992 | bytes 20447232 | tf_op jit(solution)/shard_map/rf,rd->fd/dot_general | solution.py:240
  592.7 15.6 %fusion.37 = bf16[1,768,3072]{2,1,0:T(8,128)(2,1)} fusion(bf16[1024,3072]{1,0:T(8,128)(2,1)} %copy-done.77, bf16[1024,3072]{1,0:T(8,128)(2,1)} %copy-done.76, bf16[1024,768]{1,0:T(8,128)(2,1)} %bitcast.29, bf16[1024,768]{1,0:T(8,128)(2,1)} %bitcast.11), kind=kOutput, calls=%fused_computation.43 | convolution fusion | flops 9697492992 | bytes 20447232 | tf_op jit(solution)/shard_map/rd,rf->df/dot_general | solution.py:247
  608.4 42.1 %all_to_all.71 = bf16[8,128,768]{2,1,0:T(8,128)(2,1)} all-to-all(bf16[8,128,768]{2,1,0:T(8,128)(2,1)} %bitcast.239), channel_id=1, replica_groups=mesh['dp'=4,'expert'=8] {'expert'}, dimensions={0} | all-to-all | bytes 3145728 | tf_op jit(solution)/shard_map/all_to_all | solution.py:133
  658.3 54.2 %pmax.7 = f32[12]{0:T(128)S(1)} all-reduce(f32[12]{0:T(128)S(1)} %max.8), channel_id=1, replica_groups=mesh['dp'=4,'expert'=8] {'dp','expert'}, use_global_device_ids=true, to_apply=%region_58.59 | all-reduce | flops 12 | bytes 96 | tf_op jit(solution)/shard_map/pmax | solution.py:334
  730.0 17.7 %reduce-scatter.6.cloned.1.call-done = bf16[1,192,3072]{2,1,0:T(8,128)(2,1)} async-done(((bf16[1,768,3072]{2,1,0:T(8,128)(2,1)}), bf16[1,192,3072]{2,1,0:T(8,128)(2,1)}) %reduce-scatter.6.cloned.1.call-update) | async-done | bytes 1179664 | tf_op jit(solution)/shard_map/reduce_scatter | solution.py:253
  750.7 61.0 %all-reduce.4.cloned.1.call-done = bf16[192,3082]{0,1:T(8,128)(2,1)} async-done(((bf16[192,3082]{0,1:T(8,128)(2,1)}), bf16[192,3082]{0,1:T(8,128)(2,1)}) %all-reduce.4.cloned.1.call-update) | async-done | bytes 1183504 | tf_op jit(solution)/shard_map/psum | solution.py:326
  (386 shorter events, 250.6 us)
Async XLA Ops:
  7.2 52.7 %all-gather.5.cloned.1.call-start = ((), (), s32[]{:S(2)}) async-start(), calls=%async_computation.15 | async-start | bytes 4423680 | tf_op jit(solution)/shard_map/all_gather | solution.py:172
  7.9 81.6 %all-gather.7.cloned.1.call-start = ((), (), s32[]{:S(2)}) async-start(), calls=%async_computation.16 | async-start | bytes 1474560 | tf_op jit(solution)/shard_map/all_gather | solution.py:173
  10.3 13.8 %copy-start.57 = (f32[394]{0:T(512)}, f32[394]{0:T(512)S(1)}, u32[]{:S(2)}) copy-start(f32[394]{0:T(512)S(1)} %get-tuple-element.156) | copy-start | bytes 4732
  10.9 14.5 %copy-start.61 = (f32[394]{0:T(512)}, f32[394]{0:T(512)S(1)}, u32[]{:S(2)}) copy-start(f32[394]{0:T(512)S(1)} %add_rsqrt_fusion.1) | copy-start | bytes 4732
  10.9 14.5 %copy-start.63 = (f32[394]{0:T(512)}, f32[394]{0:T(512)S(1)}, u32[]{:S(2)}) copy-start(f32[394]{0:T(512)S(1)} %add_rsqrt_fusion.3) | copy-start | bytes 4732
  24.1 249.3 %copy-start.66 = (s32[394]{0:T(512)}, s32[394]{0:T(512)S(1)}, u32[]{:S(2)}) copy-start(s32[394]{0:T(512)S(1)} %get-tuple-element.89) | copy-start | bytes 4732
  24.1 249.3 %copy-start.68 = (s32[394]{0:T(512)}, s32[394]{0:T(512)S(1)}, u32[]{:S(2)}) copy-start(s32[394]{0:T(512)S(1)} %get-tuple-element.90) | copy-start | bytes 4732
  25.4 34.5 %copy-start.42 = (bf16[394,768]{1,0:T(8,128)(2,1)}, bf16[394,768]{1,0:T(8,128)(2,1)S(1)}, u32[]{:S(2)}) copy-start(bf16[394,768]{1,0:T(8,128)(2,1)S(1)} %get-tuple-element.120) | copy-start | bytes 1815556
  92.1 50.6 %copy-start.28 = (bf16[394,768]{1,0:T(8,128)(2,1)}, bf16[394,768]{1,0:T(8,128)(2,1)S(1)}, u32[]{:S(2)}) copy-start(bf16[394,768]{1,0:T(8,128)(2,1)S(1)} %multiply_convert_fusion.13) | copy-start | bytes 1815556
  94.6 42.7 %all-to-all-start = ((bf16[8,128,768]{2,1,0:T(8,128)(2,1)}), bf16[8,128,768]{2,1,0:T(8,128)(2,1)}, u32[]{:S(2)}, u32[]{:S(2)}) async-start(bf16[8,128,768]{2,1,0:T(8,128)(2,1)} %bitcast.247), calls=%async_computation | async-start | bytes 3145728 | tf_op jit(solution)/shard_map/all_to_all | solution.py:133
  137.2 42.7 %all-to-all-start.6 = ((bf16[8,128,768]{2,1,0:T(8,128)(2,1)}), bf16[8,128,768]{2,1,0:T(8,128)(2,1)}, u32[]{:S(2)}, u32[]{:S(2)}) async-start(bf16[8,128,768]{2,1,0:T(8,128)(2,1)} %bitcast.245), calls=%async_computation.6 | async-start | bytes 3145728 | tf_op jit(solution)/shard_map/all_to_all | solution.py:133
  179.9 24.2 %copy-start.44 = (bf16[394,768]{1,0:T(8,128)(2,1)S(1)}, bf16[394,768]{1,0:T(8,128)(2,1)}, u32[]{:S(2)}) copy-start(bf16[394,768]{1,0:T(8,128)(2,1)} %get-tuple-element.121) | copy-start | bytes 1815556
  190.5 8.7 %all-to-all-start.8 = ((f32[8,1,128]{2,1,0:T(1,128)}), f32[8,1,128]{2,1,0:T(1,128)S(1)}, u32[]{:S(2)}, u32[]{:S(2)}) async-start(f32[8,1,128]{2,1,0:T(1,128)} %bitcast.42), calls=%async_computation.8 | async-start | bytes 8192 | tf_op jit(solution)/shard_map/all_to_all | solution.py:133
  200.8 8.7 %all-to-all-start.1 = ((f32[8,1,128]{2,1,0:T(1,128)}), f32[8,1,128]{2,1,0:T(1,128)S(1)}, u32[]{:S(2)}, u32[]{:S(2)}) async-start(f32[8,1,128]{2,1,0:T(1,128)} %bitcast.17), calls=%async_computation.1 | async-start | bytes 8192 | tf_op jit(solution)/shard_map/all_to_all | solution.py:133
  209.5 14.9 %copy-start.51 = (f32[8,1,128]{2,1,0:T(1,128)}, f32[8,1,128]{2,1,0:T(1,128)S(1)}, u32[]{:S(2)}) copy-start(f32[8,1,128]{2,1,0:T(1,128)S(1)} %all-to-all-done.1) | copy-start | bytes 12292
  209.5 14.9 %slice-start.4 = ((s8[4718592]{0:T(1024)(128)(4,1)}), s8[4194304]{0:T(1024)(128)(4,1)S(1)}, s32[]{:S(2)}) async-start(s8[4718592]{0:T(1024)(128)(4,1)} %bitcast.279), calls=%async_computation.25 | async-start | bytes 8388608
  230.7 42.6 %all-to-all-start.7 = ((bf16[8,128,768]{2,1,0:T(8,128)(2,1)}), bf16[8,128,768]{2,1,0:T(8,128)(2,1)}, u32[]{:S(2)}, u32[]{:S(2)}) async-start(bf16[8,128,768]{2,1,0:T(8,128)(2,1)} %bitcast.244), calls=%async_computation.7 | async-start | bytes 3145728 | tf_op jit(solution)/shard_map/all_to_all | solution.py:133
  277.6 49.1 %copy-start.30 = (bf16[394,768]{1,0:T(8,128)(2,1)}, bf16[394,768]{1,0:T(8,128)(2,1)S(1)}, u32[]{:S(2)}) copy-start(bf16[394,768]{1,0:T(8,128)(2,1)S(1)} %get-tuple-element.128) | copy-start | bytes 1815556
  280.1 42.3 %all-to-all-start.3 = ((bf16[8,128,768]{2,1,0:T(8,128)(2,1)}), bf16[8,128,768]{2,1,0:T(8,128)(2,1)}, u32[]{:S(2)}, u32[]{:S(2)}) async-start(bf16[8,128,768]{2,1,0:T(8,128)(2,1)} %bitcast.250), calls=%async_computation.3 | async-start | bytes 3145728 | tf_op jit(solution)/shard_map/all_to_all | solution.py:133
  322.4 42.1 %all-to-all-start.9 = ((bf16[8,128,768]{2,1,0:T(8,128)(2,1)}), bf16[8,128,768]{2,1,0:T(8,128)(2,1)}, u32[]{:S(2)}, u32[]{:S(2)}) async-start(bf16[8,128,768]{2,1,0:T(8,128)(2,1)} %bitcast.249), calls=%async_computation.9 | async-start | bytes 3145728 | tf_op jit(solution)/shard_map/all_to_all | solution.py:133
  364.5 43.4 %slice-start.6 = ((s8[4718592]{0:T(1024)(128)(4,1)}), s8[524288]{0:T(1024)(128)(4,1)S(1)}, s32[]{:S(2)}) async-start(s8[4718592]{0:T(1024)(128)(4,1)} %bitcast.281), calls=%async_computation.27 | async-start | bytes 1048576
  375.2 8.7 %all-to-all-start.11 = ((f32[8,1,128]{2,1,0:T(1,128)}), f32[8,1,128]{2,1,0:T(1,128)S(1)}, u32[]{:S(2)}, u32[]{:S(2)}) async-start(f32[8,1,128]{2,1,0:T(1,128)} %bitcast.58), calls=%async_computation.11 | async-start | bytes 8192 | tf_op jit(solution)/shard_map/all_to_all | solution.py:133
  414.2 42.3 %all-to-all-start.10 = ((bf16[8,128,768]{2,1,0:T(8,128)(2,1)}), bf16[8,128,768]{2,1,0:T(8,128)(2,1)}, u32[]{:S(2)}, u32[]{:S(2)}) async-start(bf16[8,128,768]{2,1,0:T(8,128)(2,1)} %bitcast.248), calls=%async_computation.10 | async-start | bytes 3145728 | tf_op jit(solution)/shard_map/all_to_all | solution.py:133
  418.6 300.5 %reduce-scatter.10.cloned.1.call-start = ((), (), s32[]{:S(2)}) async-start(), calls=%async_computation.20 | async-start | bytes 6144000
  570.2 157.0 %reduce-scatter.8.cloned.1.call-start = ((), (), s32[]{:S(2)}) async-start(), calls=%async_computation.19 | async-start | bytes 5898240 | tf_op jit(solution)/shard_map/reduce_scatter | solution.py:246
  592.7 155.1 %reduce-scatter.6.cloned.1.call-start = ((), (), s32[]{:S(2)}) async-start(), calls=%async_computation.18 | async-start | bytes 5898240 | tf_op jit(solution)/shard_map/reduce_scatter | solution.py:253
  650.5 72.5 %all-to-all-start.5 = ((bf16[8,128,768]{2,1,0:T(8,128)(2,1)}), bf16[8,128,768]{2,1,0:T(8,128)(2,1)}, u32[]{:S(2)}, u32[]{:S(2)}) async-start(bf16[8,128,768]{2,1,0:T(8,128)(2,1)} %bitcast.238), calls=%async_computation.5 | async-start | bytes 3145728 | tf_op jit(solution)/shard_map/all_to_all | solution.py:133
  655.0 156.7 %all-reduce.4.cloned.1.call-start = ((), (), s32[]{:S(2)}) async-start(), calls=%async_computation.17 | async-start | bytes 3162112 | tf_op jit(solution)/shard_map/psum | solution.py:326
  657.3 55.2 %copy-start.74 = (f32[12]{0:T(128)S(1)}, f32[12]{0:T(128)}, u32[]{:S(2)}) copy-start(f32[12]{0:T(128)} %param.18) | copy-start | bytes 148
  657.4 55.3 %copy-start.27 = (bf16[3,192,768]{2,1,0:T(8,128)(2,1)S(1)}, bf16[3,192,768]{2,1,0:T(8,128)(2,1)}, u32[]{:S(2)}) copy-start(bf16[3,192,768]{2,1,0:T(8,128)(2,1)} %param.11) | copy-start | bytes 2654212
  658.3 55.5 %copy-start.67 = (s32[394]{0:T(512)S(1)}, s32[394]{0:T(512)}, u32[]{:S(2)}) copy-start(s32[394]{0:T(512)} %copy-done.66) | copy-start | bytes 4732
  658.3 55.5 %copy-start.69 = (s32[394]{0:T(512)S(1)}, s32[394]{0:T(512)}, u32[]{:S(2)}) copy-start(s32[394]{0:T(512)} %copy-done.68) | copy-start | bytes 4732
  (72 other events, 284.2 us)
Sparse Core Ops, SparseCore 0:
  9.9 49.9 all-gather.4
  61.7 27.7 all-gather.6
  570.3 56.6 reduce-scatter.9
  629.8 57.3 reduce-scatter.7
  690.0 57.6 reduce-scatter.5
  750.6 61.0 all-reduce.3

commit v2 on v0

v2 whole, which is shorter than its diff:
```python
import functools
import jax
import jax.numpy as jnp
from jax import lax
from jax.experimental import pallas as pl
from jax.experimental.pallas import tpu as pltpu
from jax.sharding import PartitionSpec as P

D = 768
HEADS = 12
HEAD_DIM = 64
FF = 3072
SEQ = 197
IMG_DEV = 2
MB = 2
TOK_MB = 394
SEQ_PAD = 208
TOK_PAD = IMG_DEV * SEQ_PAD
PAIRS = HEADS // 2
CHUNK = 32
COLS = 256

epsilon = 1e-06
qk_scale = 0.125
gelu_coeff = 0.7978845608028654
low = jnp.bfloat16
wide = jnp.float32

NN = (((1,), (0,)), ((), ()))
NT = (((1,), (1,)), ((), ()))
TN = (((0,), (0,)), ((), ()))


def dot(left, right, dims=NN):
    return lax.dot_general(left, right, dims, preferred_element_type=wide)


def rows_of(index, size):
    return pl.ds(pl.multiple_of(index * size, size), size)


def loop(count, body):
    def step(index, carry):
        body(index)
        return carry

    lax.fori_loop(0, count, step, 0)


def norm_parts(values_in):
    row_mean = jnp.sum(values_in, axis=-1, keepdims=True) * (1.0 / D)
    centred = values_in - row_mean
    row_var = jnp.sum(centred * centred, axis=-1, keepdims=True) * (1.0 / D)
    inverse = lax.rsqrt(row_var + epsilon)
    return centred * inverse, inverse


def norm_back(unit, inverse, gain_row, incoming):
    scaled = incoming * gain_row
    mean_one = jnp.sum(scaled, axis=-1, keepdims=True) * (1.0 / D)
    mean_two = jnp.sum(scaled * unit, axis=-1, keepdims=True) * (1.0 / D)
    return (scaled - mean_one - unit * mean_two) * inverse


def fold_rows(values_in):
    return jnp.sum(values_in.reshape(-1, 8, values_in.shape[-1]), axis=0)


def gelu_both(values_in):
    squared = values_in * values_in
    bent = jnp.tanh(values_in * (gelu_coeff + (gelu_coeff * 0.044715) * squared))
    half = 0.5 + 0.5 * bent
    slope = half + half * (1.0 - bent) * values_in * (
        gelu_coeff + (3.0 * 0.044715 * gelu_coeff) * squared
    )
    return values_in * half, slope


def head_mask(half):
    lane = lax.broadcasted_iota(jnp.int32, (1, 2 * HEAD_DIM), 1)
    return (lane // HEAD_DIM) == half


def attention_forward(tok, gains, wqkv, wout, first, qkv, probs, mixed, resid, second, tops):
    def norm_one(index):
        rows = rows_of(index, CHUNK)
        unit, _ = norm_parts(tok[rows, :].astype(wide))
        first[rows, :] = (unit * gains[0:1, :]).astype(low)

    loop(TOK_PAD // CHUNK, norm_one)

    def project(index):
        part, cols = index // (D // COLS), rows_of(index % (D // COLS), COLS)
        qkv[part, :, cols] = dot(first[...], wqkv[part, :, cols]).astype(low)

    loop(3 * (D // COLS), project)

    def attend(index):
        image, pair = index // PAIRS, index % PAIRS
        rows, cols = rows_of(image, SEQ_PAD), rows_of(pair, 2 * HEAD_DIM)
        query, key, value = qkv[0, rows, cols], qkv[1, rows, cols], qkv[2, rows, cols]
        key_id = lax.broadcasted_iota(jnp.int32, (SEQ_PAD, SEQ_PAD), 1)
        row_id = lax.broadcasted_iota(jnp.int32, (SEQ_PAD, 1), 0)
        total = jnp.zeros((SEQ_PAD, 2 * HEAD_DIM), wide)
        for half in range(2):
            mask = head_mask(half)
            scores = dot(jnp.where(mask, query * qk_scale, 0.0).astype(low), key, NT)
            scores = jnp.where(key_id < SEQ, scores, -jnp.inf)
            row_top = jnp.max(scores, axis=-1, keepdims=True)
            exp_scores = jnp.exp(scores - row_top)
            attn = exp_scores * (1.0 / jnp.sum(exp_scores, axis=-1, keepdims=True))
            attn = attn.astype(low)
            probs[2 * index + half] = attn
            total += dot(attn, jnp.where(mask, value, 0.0).astype(low))
            top = jnp.max(jnp.where(row_id < SEQ, row_top, -jnp.inf), axis=0, keepdims=True)
            slot = pl.ds(2 * pair + half, 1)
            tops[slot, :] = jnp.maximum(tops[slot, :], jnp.broadcast_to(top, (1, 128)))
        mixed[rows, cols] = total.astype(low)

    loop(IMG_DEV * PAIRS, attend)

    def add_out(index):
        cols = rows_of(index, COLS)
        resid[:, cols] = tok[:, cols].astype(wide) + dot(mixed[...], wout[:, cols])

    loop(D // COLS, add_out)

    def norm_two(index):
        rows = rows_of(index, CHUNK)
        unit, _ = norm_parts(resid[rows, :])
        second[rows, :] = (unit * gains[1:2, :]).astype(low)

    loop(TOK_PAD // CHUNK, norm_two)


def place_tokens(route, capacity, named, place):
    experts = named.shape[0]
    expert_id = lax.broadcasted_iota(jnp.int32, (experts, TOK_PAD), 0)
    is_named = (route[0:1, :] == expert_id) | (route[1:2, :] == expert_id)
    earlier = lax.broadcasted_iota(jnp.int32, (TOK_PAD, TOK_PAD), 0) < lax.broadcasted_iota(
        jnp.int32, (TOK_PAD, TOK_PAD), 1
    )
    ones = jnp.where(is_named, 1.0, 0.0)
    count = dot(ones.astype(low), jnp.where(earlier, 1.0, 0.0).astype(low))
    named[...] = jnp.where(is_named, count, -1.0)
    slot_id = lax.broadcasted_iota(jnp.int32, (capacity, TOK_PAD), 0).astype(wide)

    def one(expert):
        hit = slot_id == named[pl.ds(expert, 1), :]
        place[rows_of(expert, capacity), :] = jnp.where(hit, 1.0, 0.0).astype(low)

    loop(experts, one)


def split_three(values_in):
    head = values_in.astype(low)
    rest = values_in - head.astype(wide)
    middle = rest.astype(low)
    return [head, middle, (rest - middle.astype(wide)).astype(low)]


def gate_tokens(second, router_t, named, gate):
    logits = dot(router_t[...], second[...], NT)
    is_named = named[...] >= 0.0
    top = jnp.max(jnp.where(is_named, logits, -jnp.inf), axis=0, keepdims=True)
    exp_logits = jnp.where(is_named, jnp.exp(logits - jnp.where(top > -jnp.inf, top, 0.0)), 0.0)
    total = jnp.sum(exp_logits, axis=0, keepdims=True)
    gate[...] = exp_logits / jnp.where(total > 0.0, total, 1.0)


def gate_slots(expert, gate, place, capacity, slot_gate):
    experts = gate.shape[0]
    only = lax.broadcasted_iota(jnp.int32, (experts, 1), 0) == expert
    row = jnp.sum(jnp.where(only, gate[...], 0.0), axis=0, keepdims=True)
    spot = place[rows_of(expert, capacity), :]
    found = sum(
        dot(jnp.broadcast_to(part, (16, TOK_PAD)), spot, NT) for part in split_three(row)
    )
    slot_gate[expert, :, 0:capacity] = found[0:8, :]


def attention_backward(
    tok, gains, wqkv, wout, qkv, probs, resid, grad, attended, proj, scratch, gain_sums, result, cot
):
    def norm_two(index):
        rows = rows_of(index, CHUNK)
        unit, inverse = norm_parts(resid[rows, :])
        incoming = grad[rows, :]
        grad_resid = cot[rows, :].astype(wide) + norm_back(
            unit, inverse, gains[1:2, :], incoming
        )
        gain_sums[1] += fold_rows(incoming * unit)
        grad[rows, :] = grad_resid
        attended[rows, :] = grad_resid.astype(low)

    loop(TOK_PAD // CHUNK, norm_two)

    def through_out(index):
        cols = rows_of(index, COLS)
        scratch[:, cols] = dot(attended[...], wout[cols, :], NT).astype(low)

    loop(D // COLS, through_out)

    def attend(index):
        image, pair = index // PAIRS, index % PAIRS
        rows, cols = rows_of(image, SEQ_PAD), rows_of(pair, 2 * HEAD_DIM)
        query, key, value = qkv[0, rows, cols], qkv[1, rows, cols], qkv[2, rows, cols]
        incoming = scratch[rows, cols]
        shape = (SEQ_PAD, 2 * HEAD_DIM)
        grad_query, grad_key, grad_value = (jnp.zeros(shape, wide) for _ in range(3))
        for half in range(2):
            mask = head_mask(half)
            attn_low = probs[2 * index + half]
            attn = attn_low.astype(wide)
            grad_mixed = jnp.where(mask, incoming, 0.0).astype(low)
            grad_probs = dot(grad_mixed, value, NT)
            grad_value += dot(attn_low, grad_mixed, TN)
            row_dot = jnp.sum(attn * grad_probs, axis=-1, keepdims=True)
            grad_scores = (attn * (grad_probs - row_dot)).astype(low)
            grad_query += dot(grad_scores, jnp.where(mask, key * qk_scale, 0.0).astype(low))
            grad_key += dot(grad_scores, jnp.where(mask, query * qk_scale, 0.0).astype(low), TN)
        proj[0, rows, cols] = grad_query.astype(low)
        proj[1, rows, cols] = grad_key.astype(low)
        proj[2, rows, cols] = grad_value.astype(low)

    loop(IMG_DEV * PAIRS, attend)

    def through_qkv(index):
        cols = rows_of(index, COLS)
        total = dot(proj[0], wqkv[0, cols, :], NT)
        total += dot(proj[1], wqkv[1, cols, :], NT)
        result[:, cols] = total + dot(proj[2], wqkv[2, cols, :], NT)

    loop(D // COLS, through_qkv)

    def norm_one(index):
        rows = rows_of(index, CHUNK)
        unit, inverse = norm_parts(tok[rows, :].astype(wide))
        incoming = result[rows, :]
        gain_sums[0] += fold_rows(incoming * unit)
        grad[rows, :] += norm_back(unit, inverse, gains[0:1, :], incoming)

    loop(TOK_PAD // CHUNK, norm_one)


ANY = pl.BlockSpec(memory_space=pl.ANY)
VMEM = pl.BlockSpec(memory_space=pltpu.VMEM)
MESH = pl.DeviceIdType.MESH
BLOCK_ROWS = 512
MADE_ROWS = 256
BLOCK_FF = 512
GRAD_FF = 256
KIND_COT, KIND_ROW, KIND_GATE, KIND_BACK, KIND_SLOPE, KIND_MADE = range(6)


def wait_bytes(ref, sem):
    pltpu.make_async_copy(ref, ref, sem).wait()


def local_copy(source, target, sem):
    copy = pltpu.make_async_copy(source, target, sem)
    copy.start()
    return copy


def block_kernel(
    n_dp,
    n_ex,
    capacity,
    tok_in,
    cot_in,
    route,
    qkv_in,
    out_in,
    small_in,
    expert_in,
    expert_out,
    layer_out,
    grad_input,
    share,
    share_small,
    share_in,
    share_out,
    tops_out,
    land,
    spill_hidden,
    spill_grad,
    spill_probs,
    spill_qkv,
    spill_rows,
    stage_in,
    stage_out,
    pair_land,
    dp_land,
    part_land,
    half_land,
    wqkv,
    wout,
    small,
    small_t,
    gains,
    resid,
    place,
    named,
    gate,
    send,
    gate_send,
    gate_land,
    slope_send,
    slope_land,
    tops,
    tops_land,
    tops_dp,
    small_pair,
    small_dp,
    small_part,
    small_sum,
    gain_sums,
    gather_send,
    gather_recv,
    ex_send,
    ex_recv,
    rs_send,
    rs_recv,
    red_send,
    red_recv,
    local_sem,
):
    dp, me = lax.axis_index("dp"), lax.axis_index("expert")
    shard = D // n_dp
    slots = n_ex * capacity
    own_rows = rows_of(dp, shard)

    barrier = pltpu.get_barrier_semaphore()

    def greet_ex(step):
        pl.semaphore_signal(
            barrier, inc=1, device_id=(dp, me ^ (step + 1)), device_id_type=MESH
        )

    def greet_dp(step):
        pl.semaphore_signal(
            barrier, inc=1, device_id=(dp ^ (step + 1), me), device_id_type=MESH
        )

    loop(n_ex - 1, greet_ex)
    loop(n_dp - 1, greet_dp)
    pl.semaphore_wait(barrier, n_ex - 1 + n_dp - 1)

    def remote(source, target, send_sem, recv_sem, device):
        pltpu.make_async_remote_copy(
            src_ref=source,
            dst_ref=target,
            send_sem=send_sem,
            recv_sem=recv_sem,
            device_id=device,
            device_id_type=MESH,
        ).start()

    def gather_small(step):
        peer = (dp ^ (step + 1), me)
        remote(small_in, small.at[own_rows, :], gather_send.at[0], gather_recv.at[0], peer)

    def gather_qkv(step):
        peer = (dp ^ (step + 1), me)
        remote(qkv_in, wqkv.at[:, own_rows, :], gather_send.at[1], gather_recv.at[1], peer)

    def gather_out(step):
        peer = (dp ^ (step + 1), me)
        remote(out_in, wout.at[own_rows, :], gather_send.at[2], gather_recv.at[2], peer)

    loop(n_dp - 1, gather_small)
    loop(n_dp - 1, gather_qkv)
    loop(n_dp - 1, gather_out)
    own_copies = [
        local_copy(small_in, small.at[own_rows, :], local_sem.at[0]),
        local_copy(qkv_in, wqkv.at[:, own_rows, :], local_sem.at[1]),
        local_copy(out_in, wout.at[own_rows, :], local_sem.at[2]),
    ]

    def expert_rows(slot, peer):
        return send.at[slot, rows_of(peer, capacity), :]

    def exchange(kind, slot, micro):
        def one(step):
            peer = me ^ (step + 1)
            remote(
                expert_rows(slot, peer),
                land.at[kind, micro, rows_of(me, capacity), :],
                ex_send.at[kind, micro],
                ex_recv.at[kind, micro],
                (dp, peer),
            )

        loop(n_ex - 1, one)

    def keep_own(kind, slot, micro, sem):
        local_copy(
            expert_rows(slot, me), land.at[kind, micro, rows_of(me, capacity), :], sem
        ).wait()

    def exchange_small(source, target, kind, micro):
        def one(step):
            peer = me ^ (step + 1)
            remote(
                source.at[micro, peer],
                target.at[micro, me],
                ex_send.at[kind, micro],
                ex_recv.at[kind, micro],
                (dp, peer),
            )

        loop(n_ex - 1, one)
        target[micro, me] = source[micro, me]

    def await_rows(sems, kind, micro):
        wait_bytes(send.at[0, pl.ds(0, slots - capacity), :], sems.at[kind, micro])

    def await_small(sems, ref, kind, micro):
        wait_bytes(ref.at[micro, pl.ds(0, n_ex - 1)], sems.at[kind, micro])

    def pack(source, slot, micro):
        def one(expert):
            rows = rows_of(expert, capacity)
            send[slot, rows, :] = dot(place[micro, rows, :], source[...]).astype(low)

        loop(n_ex, one)

    def forward(tok, probs, qkv, first, mixed, second, spill_sem):
        def spills(micro):
            tokens = rows_of(micro, TOK_PAD)
            pairs = [
                (probs.at[micro], spill_probs.at[micro]),
                (qkv.at[micro], spill_qkv.at[micro]),
                (first.at[tokens], spill_rows.at[0, tokens]),
                (mixed.at[tokens], spill_rows.at[1, tokens]),
                (second.at[tokens], spill_rows.at[2, tokens]),
            ]
            return [
                pltpu.make_async_copy(source, target, spill_sem.at[micro, index])
                for index, (source, target) in enumerate(pairs)
            ]

        def send_cot(micro):
            local_copy(cot_in.at[micro], tok.at[0], local_sem.at[3]).wait()
            place_tokens(route.at[micro], capacity, named.at[micro], place.at[micro])
            pack(tok.at[0], micro, micro)
            exchange(KIND_COT, micro, micro)
            keep_own(KIND_COT, micro, micro, local_sem.at[3])

        loop(MB, send_cot)
        load = local_copy(tok_in, tok, local_sem.at[3])
        tops[...] = jnp.full(tops.shape, -jnp.inf, wide)
        own_copies[0].wait()
        wait_bytes(small.at[pl.ds(0, D - shard), :], gather_recv.at[0])
        turned = small[...].astype(wide).T
        small_t[...] = turned.astype(low)
        gains[...] = turned[n_ex : n_ex + 8, :]
        load.wait()
        own_copies[1].wait()
        wait_bytes(wqkv.at[:, pl.ds(0, D - shard), :], gather_recv.at[1])
        own_copies[2].wait()
        wait_bytes(wout.at[pl.ds(0, D - shard), :], gather_recv.at[2])

        def one(micro):
            attention_forward(
                tok.at[micro],
                gains,
                wqkv,
                wout,
                first.at[rows_of(micro, TOK_PAD)],
                qkv.at[micro],
                probs.at[micro],
                mixed.at[rows_of(micro, TOK_PAD)],
                resid.at[micro],
                second.at[rows_of(micro, TOK_PAD)],
                tops,
            )
            for copy in spills(micro):
                copy.start()
            rows = second.at[rows_of(micro, TOK_PAD)]
            gate_tokens(rows, small_t.at[pl.ds(0, n_ex)], named.at[micro], gate.at[micro])
            loop(
                n_ex,
                lambda expert: gate_slots(
                    expert, gate.at[micro], place.at[micro], capacity, gate_send.at[micro]
                ),
            )
            exchange_small(gate_send, gate_land, KIND_GATE, micro)
            pack(rows, MB + micro, micro)
            exchange(KIND_ROW, MB + micro, micro)
            keep_own(KIND_ROW, MB + micro, micro, local_sem.at[3])

        loop(MB, one)

        def spread(step):
            peer = me ^ (step + 1)
            remote(tops, tops_land.at[me], red_send.at[0], red_recv.at[0], (dp, peer))

        loop(n_ex - 1, spread)
        tops_land[me] = tops[...]
        for micro in range(MB):
            for copy in spills(micro):
                copy.wait()

    pl.run_scoped(
        forward,
        pltpu.VMEM((MB, TOK_PAD, D), low),
        pltpu.VMEM((MB, IMG_DEV * HEADS, SEQ_PAD, SEQ_PAD), low),
        pltpu.VMEM((MB, 3, TOK_PAD, D), low),
        pltpu.VMEM((MB * TOK_PAD, D), low),
        pltpu.VMEM((MB * TOK_PAD, D), low),
        pltpu.VMEM((MB * TOK_PAD, D), low),
        pltpu.SemaphoreType.DMA((MB, 5)),
    )

    def experts(w_in, w_out, rows_in, cot, grad_rows, rows_t, grad_t, hidden, grad_pre, made, sems):
        load_in = local_copy(expert_in, w_in, sems.at[0])
        load_out = local_copy(expert_out, w_out, sems.at[1])
        eye = lax.broadcasted_iota(jnp.int32, (capacity, capacity), 0) == lax.broadcasted_iota(
            jnp.int32, (capacity, capacity), 1
        )

        def gate_column(micro, source):
            row = gate_land[micro, source, 0:1, 0:capacity]
            return jnp.sum(jnp.where(eye, row, 0.0), axis=1, keepdims=True)

        load_in.wait()
        load_out.wait()

        def one(micro):
            await_rows(ex_recv, KIND_COT, micro)
            await_small(ex_recv, gate_land, KIND_GATE, micro)
            await_rows(ex_recv, KIND_ROW, micro)
            load_rows = local_copy(land.at[KIND_ROW, micro], rows_in, sems.at[0])
            load_cot = local_copy(land.at[KIND_COT, micro], cot, sems.at[1])
            load_rows.wait()
            load_cot.wait()

            def scale(source):
                rows = rows_of(source, capacity)
                wide_cot = cot[rows, :].astype(wide)
                grad_rows[rows, :] = (wide_cot * gate_column(micro, source)).astype(low)

            loop(n_ex, scale)

            def turn(index):
                rows = rows_of(index, 128)
                cols = pl.ds(pl.multiple_of(micro * slots + index * 128, 128), 128)
                rows_t[:, cols] = rows_in[rows, :].T
                grad_t[:, cols] = grad_rows[rows, :].T

            loop(slots // 128, turn)

            @pl.when(micro > 0)
            def _():
                pltpu.make_async_copy(hidden, spill_hidden, sems.at[2]).wait()
                pltpu.make_async_copy(grad_pre, spill_grad, sems.at[3]).wait()

            def through(index):
                cols = rows_of(index // (slots // BLOCK_ROWS), BLOCK_FF)
                rows = rows_of(index % (slots // BLOCK_ROWS), BLOCK_ROWS)
                value, slope = gelu_both(dot(rows_in[rows, :], w_in[:, cols]))
                hidden[rows, cols] = value.astype(low)
                grad_hidden = dot(grad_rows[rows, :], w_out[cols, :], NT)
                grad_pre[rows, cols] = (grad_hidden * slope).astype(low)

            loop((FF // BLOCK_FF) * (slots // BLOCK_ROWS), through)

            @pl.when(micro < MB - 1)
            def _():
                local_copy(hidden, spill_hidden, sems.at[2])
                local_copy(grad_pre, spill_grad, sems.at[3])

            await_rows(ex_send, KIND_COT, micro)

            def back(index):
                rows = rows_of(index, BLOCK_ROWS)
                send[micro, rows, :] = dot(grad_pre[rows, :], w_in[...], NT).astype(low)

            loop(slots // BLOCK_ROWS, back)
            exchange(KIND_BACK, micro, micro)
            await_rows(ex_send, KIND_ROW, micro)

            def forth(index):
                rows = rows_of(index, MADE_ROWS)
                made[...] = dot(hidden[rows, :], w_out[...])
                count = MADE_ROWS // capacity

                def finish(part):
                    source = index * count + part
                    own = rows_of(source, capacity)
                    values = made[rows_of(part, capacity), :]
                    column = jnp.sum(values * cot[own, :].astype(wide), axis=1, keepdims=True)
                    slope_send[micro, source, 0:1, 0:capacity] = jnp.sum(
                        jnp.where(eye, column, 0.0), axis=0, keepdims=True
                    )
                    send[MB + micro, own, :] = (values * gate_column(micro, source)).astype(low)

                loop(count, finish)

            loop(slots // MADE_ROWS, forth)
            exchange_small(slope_send, slope_land, KIND_SLOPE, micro)
            keep_own(KIND_BACK, micro, micro, sems.at[0])

        loop(MB, one)

        def send_made(micro):
            exchange(KIND_MADE, MB + micro, micro)
            keep_own(KIND_MADE, MB + micro, micro, sems.at[0])

        loop(MB, send_made)

        wait_bytes(tops_land.at[pl.ds(0, n_ex - 1)], red_recv.at[0])
        wait_bytes(tops_land.at[pl.ds(0, n_ex - 1)], red_send.at[0])
        tops[...] = jnp.max(tops_land[...], axis=0)

    def expert_phase(w_in, w_out, rows_in, cot, grad_rows, rows_t, grad_t, hidden, grad_pre, made, sems):
        experts(w_in, w_out, rows_in, cot, grad_rows, rows_t, grad_t, hidden, grad_pre, made, sems)
        weight_grads(rows_t, grad_t, hidden, grad_pre)

    def weight_grads(rows_t, grad_t, hidden, grad_pre):
        blocks = FF // GRAD_FF
        half = pl.ds(0, slots)
        other = pl.ds(slots, slots)

        def scoped(kept_hidden, kept_grad, out_in, out_out, load_sems, store_sems):
            def fetch(block, slot):
                cols = rows_of(block, GRAD_FF)
                local_copy(spill_hidden.at[:, cols], kept_hidden.at[slot], load_sems.at[0, slot])
                local_copy(spill_grad.at[:, cols], kept_grad.at[slot], load_sems.at[1, slot])

            def stored(block, slot):
                cols = rows_of(block, GRAD_FF)
                return (
                    pltpu.make_async_copy(
                        out_in.at[slot], stage_in.at[:, cols], store_sems.at[0, slot]
                    ),
                    pltpu.make_async_copy(
                        out_out.at[slot], stage_out.at[:, cols], store_sems.at[1, slot]
                    ),
                )

            def ship(block, slot):
                for copy in stored(block, slot):
                    copy.wait()
                cols = rows_of(block, GRAD_FF)

                def one(step):
                    peer = dp ^ (step + 1)
                    remote(
                        stage_in.at[rows_of(peer, shard), cols],
                        share_in.at[dp, :, cols],
                        rs_send.at[0],
                        rs_recv.at[0],
                        (peer, me),
                    )

                loop(n_dp - 1, one)

            fetch(0, 0)

            def one(block):
                slot = lax.rem(block, 2)

                @pl.when(block + 1 < blocks)
                def _():
                    fetch(block + 1, 1 - slot)

                wait_bytes(kept_hidden.at[slot], load_sems.at[0, slot])
                wait_bytes(kept_grad.at[slot], load_sems.at[1, slot])
                cols = rows_of(block, GRAD_FF)
                out_in[slot] = (
                    dot(rows_t[:, half], kept_grad[slot]) + dot(rows_t[:, other], grad_pre[:, cols])
                ).astype(low)
                out_out[slot] = (
                    dot(grad_t[:, half], kept_hidden[slot]) + dot(grad_t[:, other], hidden[:, cols])
                ).astype(low)
                for copy in stored(block, slot):
                    copy.start()

                @pl.when(block > 0)
                def _():
                    ship(block - 1, 1 - slot)

            loop(blocks, one)
            ship(blocks - 1, (blocks - 1) % 2)

        pl.run_scoped(
            scoped,
            pltpu.VMEM((2, slots, GRAD_FF), low),
            pltpu.VMEM((2, slots, GRAD_FF), low),
            pltpu.VMEM((2, D, GRAD_FF), low),
            pltpu.VMEM((2, D, GRAD_FF), low),
            pltpu.SemaphoreType.DMA((2, 2)),
            pltpu.SemaphoreType.DMA((2, 2)),
        )

    pl.run_scoped(
        expert_phase,
        pltpu.VMEM((D, FF), low),
        pltpu.VMEM((FF, D), low),
        pltpu.VMEM((slots, D), low),
        pltpu.VMEM((slots, D), low),
        pltpu.VMEM((slots, D), low),
        pltpu.VMEM((D, MB * slots), low),
        pltpu.VMEM((D, MB * slots), low),
        pltpu.VMEM((slots, FF), low),
        pltpu.VMEM((slots, FF), low),
        pltpu.VMEM((MADE_ROWS, D), wide),
        pltpu.SemaphoreType.DMA((4,)),
    )

    width = FF // n_dp

    def ship_out(step):
        peer = dp ^ (step + 1)
        remote(
            stage_out.at[:, rows_of(peer, width)],
            share_out.at[dp],
            rs_send.at[1],
            rs_recv.at[1],
            (peer, me),
        )

    loop(n_dp - 1, ship_out)

    def spread_tops(step):
        peer = dp ^ (step + 1)
        remote(tops, tops_dp.at[dp], red_send.at[1], red_recv.at[1], (peer, me))

    loop(n_dp - 1, spread_tops)
    tops_dp[dp] = tops[...]

    parts = n_ex // 2
    part_rows = part_size(n_dp, n_ex)
    core = lax.rem(me, 2)
    z = me // 2

    def backward(
        tok,
        cot,
        probs,
        qkv,
        first,
        mixed,
        second,
        arrived,
        grad,
        attended,
        proj,
        scratch,
        result,
        out,
        grads,
        own,
        half,
        sems,
    ):
        keeps = [
            local_copy(spill_rows.at[index], target, sems.at[7 + index])
            for index, target in enumerate((first, mixed, second))
        ]
        copy_in = local_copy(stage_in.at[own_rows, :], share_in.at[dp], sems.at[5])
        copy_out = local_copy(stage_out.at[:, rows_of(dp, width)], share_out.at[dp], sems.at[6])
        for copy in keeps:
            copy.wait()
        gain_sums[...] = jnp.zeros(gain_sums.shape, wide)
        small_sum[...] = jnp.zeros(small_sum.shape, wide)

        def one(micro):
            tokens = rows_of(micro, TOK_PAD)
            loads = [
                local_copy(tok_in.at[micro], tok, sems.at[0]),
                local_copy(cot_in.at[micro], cot, sems.at[1]),
                local_copy(spill_probs.at[micro], probs, sems.at[2]),
                local_copy(spill_qkv.at[micro], qkv, sems.at[10]),
            ]
            await_small(ex_recv, slope_land, KIND_SLOPE, micro)
            await_rows(ex_recv, KIND_BACK, micro)
            local_copy(land.at[KIND_BACK, micro], arrived, sems.at[3]).wait()

            expert_id = lax.broadcasted_iota(jnp.int32, (n_ex, 1), 0)
            scratch[pl.ds(0, n_ex), 0:TOK_PAD] = jnp.zeros((n_ex, TOK_PAD), wide)

            def slopes(expert):
                row = slope_land[micro, expert, 0:1, 0:capacity]
                spot = place[micro, rows_of(expert, capacity), :]
                found = sum(
                    dot(jnp.broadcast_to(part, (16, capacity)), spot) for part in split_three(row)
                )
                scratch[pl.ds(0, n_ex), 0:TOK_PAD] += jnp.where(
                    expert_id == expert, found[0:1, :], 0.0
                )

            loop(n_ex, slopes)
            gates = gate[micro]
            slope = scratch[pl.ds(0, n_ex), 0:TOK_PAD]
            grad_logits = gates * (slope - jnp.sum(gates * slope, axis=0, keepdims=True))
            grad_logits = grad_logits.astype(low)
            small_sum[pl.ds(0, n_ex), :] += dot(grad_logits, second[tokens, :])
            for block in range(D // COLS):
                cols = pl.ds(block * COLS, COLS)
                grad[:, cols] = dot(place[micro], arrived[:, cols], TN) + dot(
                    grad_logits, small_t[pl.ds(0, n_ex), cols], TN
                )
            for load in loads:
                load.wait()
            attention_backward(
                tok,
                gains,
                wqkv,
                wout,
                qkv,
                probs,
                resid.at[micro],
                grad,
                attended.at[tokens],
                proj.at[:, tokens, :],
                out,
                gain_sums,
                result,
                cot,
            )
            out[...] = grad[...].astype(low)
            local_copy(out, grad_input.at[micro], sems.at[4]).wait()

        loop(MB, one)

        def grad_block(index):
            part, block = index // (D // COLS), index % (D // COLS)
            cols = rows_of(block, COLS)
            value = dot(first[...], proj[part, :, cols], TN).astype(low)
            for owner in range(n_dp):
                grads[part, owner, :, cols] = value[owner * shard : (owner + 1) * shard, :]

        loop(3 * (D // COLS), grad_block)

        def grad_out_block(block):
            cols = rows_of(block, COLS)
            value = dot(mixed[...], attended[:, cols], TN).astype(low)
            for owner in range(n_dp):
                grads[3, owner, :, cols] = value[owner * shard : (owner + 1) * shard, :]

        loop(D // COLS, grad_out_block)
        small_sum[n_ex : n_ex + 1, :] = jnp.sum(gain_sums[0], axis=0, keepdims=True)
        small_sum[n_ex + 1 : n_ex + 2, :] = jnp.sum(gain_sums[1], axis=0, keepdims=True)
        small[...] = small_sum[...].T.astype(low)

        partner = (dp, me ^ 1)
        remote(grads.at[pl.ds(2 - 2 * core, 2)], pair_land, red_send.at[2], red_recv.at[2], partner)
        remote(small, small_pair, red_send.at[3], red_recv.at[3], partner)
        wait_bytes(small_pair, red_recv.at[3])
        wait_bytes(small, red_send.at[3])
        small[...] = (small[...].astype(wide) + small_pair[...].astype(wide)).astype(low)
        wait_bytes(pair_land, red_recv.at[2])

        def add_pair(index):
            part, owner = index // n_dp, index % n_dp
            copy = local_copy(pair_land.at[part, owner], own.at[0], sems.at[0])
            copy.wait()
            mine = grads[2 * core + part, owner].astype(wide)
            half[part, owner] = (mine + own[0].astype(wide)).astype(low)

        loop(2 * n_dp, add_pair)

        def to_owner(step):
            peer = dp ^ (step + 1)
            remote(
                half.at[:, peer], dp_land.at[dp], red_send.at[4], red_recv.at[4], (peer, me)
            )
            remote(
                small.at[rows_of(peer, shard), :],
                small_dp.at[dp],
                red_send.at[5],
                red_recv.at[5],
                (peer, me),
            )

        loop(n_dp - 1, to_owner)
        small_dp[dp] = small[own_rows, :]

        def combine(micro):
            await_rows(ex_recv, KIND_MADE, micro)
            local_copy(land.at[KIND_MADE, micro], arrived, sems.at[3]).wait()
            for block in range(D // COLS):
                cols = pl.ds(block * COLS, COLS)
                out[:, cols] = (
                    resid[micro, :, cols] + dot(place[micro], arrived[:, cols], TN)
                ).astype(low)
            local_copy(out, layer_out.at[micro], sems.at[4]).wait()

        loop(MB, combine)

        wait_bytes(dp_land.at[pl.ds(0, n_dp - 1)], red_recv.at[4])
        wait_bytes(small_dp.at[pl.ds(0, n_dp - 1)], red_recv.at[5])
        for part in range(2):
            result[pl.ds(part * shard, shard), :] = half[part, dp].astype(wide)

            def add_dp(step):
                peer = dp ^ (step + 1)
                local_copy(dp_land.at[peer, part], own.at[0], sems.at[0]).wait()
                result[pl.ds(part * shard, shard), :] += own[0].astype(wide)

            loop(n_dp - 1, add_dp)
        total = parts * part_rows
        if total > 2 * shard:
            scratch[pl.ds(2 * shard, total - 2 * shard), :] = jnp.zeros(
                (total - 2 * shard, D), wide
            )
        scratch[pl.ds(0, 2 * shard), :] = result[pl.ds(0, 2 * shard), :]
        grad_low = arrived
        grad_low[pl.ds(0, total), :] = scratch[pl.ds(0, total), :].astype(low)
        small_owner = jnp.sum(small_dp[...].astype(wide), axis=0).astype(low)
        small_part[me] = small_owner

        def to_part(step):
            peer = z ^ (step + 1)
            remote(
                grad_low.at[rows_of(peer, part_rows), :],
                part_land.at[z],
                red_send.at[6],
                red_recv.at[6],
                (dp, 2 * peer + core),
            )
            remote(
                small_part.at[me],
                small_part.at[me],
                red_send.at[7],
                red_recv.at[7],
                (dp, 2 * peer + core),
            )

        loop(parts - 1, to_part)
        wait_bytes(part_land.at[pl.ds(0, parts - 1)], red_recv.at[6])
        mine = rows_of(z, part_rows)
        result[pl.ds(0, part_rows), :] = grad_low[mine, :].astype(wide)

        def add_part(step):
            peer = z ^ (step + 1)
            local_copy(part_land.at[peer], own.at[0, pl.ds(0, part_rows), :], sems.at[0]).wait()
            result[pl.ds(0, part_rows), :] += own[0, pl.ds(0, part_rows), :].astype(wide)

        loop(parts - 1, add_part)
        out[pl.ds(0, part_rows), :] = result[pl.ds(0, part_rows), :].astype(low)

        def to_all(step):
            peer = z ^ (step + 1)
            remote(
                out.at[pl.ds(0, part_rows), :],
                half_land.at[0, mine, :],
                red_send.at[8],
                red_recv.at[8],
                (dp, 2 * peer + core),
            )

        loop(parts - 1, to_all)
        local_copy(out.at[pl.ds(0, part_rows), :], half_land.at[0, mine, :], sems.at[0]).wait()
        wait_bytes(half_land.at[0, pl.ds(0, (parts - 1) * part_rows), :], red_recv.at[8])
        mine_half = half_land.at[0, pl.ds(0, 2 * shard), :]
        remote(
            mine_half,
            half_land.at[1, pl.ds(0, 2 * shard), :],
            red_send.at[9],
            red_recv.at[9],
            partner,
        )
        local_copy(mine_half, share.at[core], sems.at[0]).wait()
        wait_bytes(small_part.at[pl.ds(0, parts - 1)], red_recv.at[7])
        chosen = jnp.zeros((shard, 128), wide)
        for chip in range(parts):
            chosen += small_part[2 * chip + core].astype(wide)
        share_small[...] = chosen
        wait_bytes(half_land.at[1, pl.ds(0, 2 * shard), :], red_recv.at[9])
        local_copy(
            half_land.at[1, pl.ds(0, 2 * shard), :], share.at[1 - core], sems.at[0]
        ).wait()
        wait_bytes(tops_dp.at[pl.ds(0, n_dp - 1)], red_recv.at[1])
        tops_out[...] = jnp.max(tops_dp[...], axis=0)
        copy_in.wait()
        copy_out.wait()

        wait_bytes(pair_land, red_send.at[2])
        wait_bytes(dp_land.at[pl.ds(0, n_dp - 1)], red_send.at[4])
        wait_bytes(grad_low.at[pl.ds(0, (parts - 1) * part_rows), :], red_send.at[6])
        wait_bytes(grad_low.at[pl.ds(0, (parts - 1) * part_rows), :], red_send.at[8])

    pl.run_scoped(
        backward,
        pltpu.VMEM((TOK_PAD, D), low),
        pltpu.VMEM((TOK_PAD, D), low),
        pltpu.VMEM((IMG_DEV * HEADS, SEQ_PAD, SEQ_PAD), low),
        pltpu.VMEM((3, TOK_PAD, D), low),
        pltpu.VMEM((MB * TOK_PAD, D), low),
        pltpu.VMEM((MB * TOK_PAD, D), low),
        pltpu.VMEM((MB * TOK_PAD, D), low),
        pltpu.VMEM((slots, D), low),
        pltpu.VMEM((TOK_PAD, D), wide),
        pltpu.VMEM((MB * TOK_PAD, D), low),
        pltpu.VMEM((3, MB * TOK_PAD, D), low),
        pltpu.VMEM((TOK_PAD, D), wide),
        pltpu.VMEM((TOK_PAD, D), wide),
        pltpu.VMEM((TOK_PAD, D), low),
        pltpu.VMEM((4, n_dp, shard, D), low),
        pltpu.VMEM((1, shard, D), low),
        pltpu.VMEM((2, n_dp, shard, D), low),
        pltpu.SemaphoreType.DMA((11,)),
    )

    wait_bytes(share_in.at[pl.ds(0, n_dp - 1)], rs_recv.at[0])
    wait_bytes(share_out.at[pl.ds(0, n_dp - 1)], rs_recv.at[1])
    wait_bytes(share_in.at[pl.ds(0, n_dp - 1)], rs_send.at[0])
    wait_bytes(share_out.at[pl.ds(0, n_dp - 1)], rs_send.at[1])
    wait_bytes(small.at[pl.ds(0, D - shard), :], gather_send.at[0])
    wait_bytes(wqkv.at[:, pl.ds(0, D - shard), :], gather_send.at[1])
    wait_bytes(wout.at[pl.ds(0, D - shard), :], gather_send.at[2])
    for micro in range(MB):
        await_rows(ex_send, KIND_BACK, micro)
        await_rows(ex_send, KIND_MADE, micro)
        await_small(ex_send, gate_land, KIND_GATE, micro)
        await_small(ex_send, slope_land, KIND_SLOPE, micro)
    wait_bytes(tops_dp.at[pl.ds(0, n_dp - 1)], red_send.at[1])
    wait_bytes(small_dp.at[pl.ds(0, n_dp - 1)], red_send.at[5])
    wait_bytes(small_part.at[pl.ds(0, parts - 1)], red_send.at[7])
    wait_bytes(half_land.at[1, pl.ds(0, 2 * shard), :], red_send.at[9])


def part_size(n_dp, n_ex):
    shard, parts = D // n_dp, n_ex // 2
    return -(-2 * shard // (parts * 16)) * 16


def run_block(n_dp, n_ex, capacity, operands):
    shard, slots = D // n_dp, n_ex * capacity
    parts, part_rows = n_ex // 2, part_size(n_dp, n_ex)
    total = parts * part_rows
    outs = [
        ((MB, TOK_PAD, D), low),
        ((MB, TOK_PAD, D), low),
        ((2, 2 * shard, D), low),
        ((shard, 128), wide),
        ((n_dp, shard, FF), low),
        ((n_dp, D, FF // n_dp), low),
        ((16, 128), wide),
        ((6, MB, slots, D), low),
        ((slots, FF), low),
        ((slots, FF), low),
        ((MB, IMG_DEV * HEADS, SEQ_PAD, SEQ_PAD), low),
        ((MB, 3, TOK_PAD, D), low),
        ((3, MB * TOK_PAD, D), low),
        ((D, FF), low),
        ((D, FF), low),
        ((2, n_dp, shard, D), low),
        ((n_dp, 2, shard, D), low),
        ((parts, part_rows, D), low),
        ((2, total, D), low),
    ]
    in_vmem = (3, 6)
    return pl.pallas_call(
        functools.partial(block_kernel, n_dp, n_ex, capacity),
        out_shape=[jax.ShapeDtypeStruct(*one) for one in outs],
        in_specs=[ANY, ANY, VMEM, ANY, ANY, ANY, ANY, ANY],
        out_specs=[VMEM if index in in_vmem else ANY for index in range(len(outs))],
        scratch_shapes=[
            pltpu.VMEM((3, D, D), low),
            pltpu.VMEM((D, D), low),
            pltpu.VMEM((D, 128), low),
            pltpu.VMEM((128, D), low),
            pltpu.VMEM((8, D), wide),
            pltpu.VMEM((MB, TOK_PAD, D), wide),
            pltpu.VMEM((MB, slots, TOK_PAD), low),
            pltpu.VMEM((MB, n_ex, TOK_PAD), wide),
            pltpu.VMEM((MB, n_ex, TOK_PAD), wide),
            pltpu.VMEM((2 * MB, slots, D), low),
            pltpu.VMEM((MB, n_ex, 8, 128), wide),
            pltpu.VMEM((MB, n_ex, 8, 128), wide),
            pltpu.VMEM((MB, n_ex, 8, 128), wide),
            pltpu.VMEM((MB, n_ex, 8, 128), wide),
            pltpu.VMEM((16, 128), wide),
            pltpu.VMEM((n_ex, 16, 128), wide),
            pltpu.VMEM((n_dp, 16, 128), wide),
            pltpu.VMEM((D, 128), low),
            pltpu.VMEM((n_dp, shard, 128), low),
            pltpu.VMEM((n_ex, shard, 128), low),
            pltpu.VMEM((128, D), wide),
            pltpu.VMEM((2, 8, D), wide),
            pltpu.SemaphoreType.DMA((3,)),
            pltpu.SemaphoreType.DMA((3,)),
            pltpu.SemaphoreType.DMA((6, MB)),
            pltpu.SemaphoreType.DMA((6, MB)),
            pltpu.SemaphoreType.DMA((2,)),
            pltpu.SemaphoreType.DMA((2,)),
            pltpu.SemaphoreType.DMA((10,)),
            pltpu.SemaphoreType.DMA((10,)),
            pltpu.SemaphoreType.DMA((4,)),
        ],
        compiler_params=pltpu.CompilerParams(
            collective_id=0, has_side_effects=True, vmem_limit_bytes=60 * 2**20
        ),
        name="encoder_block",
    )(*operands)


def padded(rows, fill=0):
    images = rows.reshape(MB, IMG_DEV, SEQ, rows.shape[-1])
    images = jnp.pad(
        images, ((0, 0), (0, 0), (0, SEQ_PAD - SEQ), (0, 0)), constant_values=fill
    )
    return images.reshape(MB, TOK_PAD, rows.shape[-1])


def unpadded(rows):
    images = rows.reshape(MB * IMG_DEV, SEQ_PAD, D)[:, :SEQ]
    return images.reshape(MB * TOK_MB, D)


def per_device(
    tokens,
    attn_qkv,
    attn_out,
    router,
    norm_gains,
    expert_in,
    expert_out,
    routes,
    clip_limit,
    cotangent,
):
    n_dp, n_ex = lax.axis_size("dp"), lax.axis_size("expert")
    capacity = max(8, (TOK_MB * 10 // (4 * n_ex) + 7) // 8 * 8)
    shard = D // n_dp
    small = jnp.concatenate(
        [router, norm_gains.T, jnp.zeros((shard, 128 - n_ex - 2), low)], axis=1
    )
    results = run_block(
        n_dp,
        n_ex,
        capacity,
        (
            padded(tokens),
            padded(cotangent),
            jnp.swapaxes(padded(routes, -1), 1, 2),
            attn_qkv,
            attn_out,
            small,
            expert_in[0],
            expert_out[0],
        ),
    )
    layer_out, grad_input, share, share_small, share_in, share_out, tops = results[:7]
    share = share.reshape(4, shard, D).astype(wide)
    head_max = tops[:HEADS, 0]
    factor = clip_limit / jnp.maximum(head_max, clip_limit)
    root_scale = jnp.repeat(jnp.sqrt(factor), HEAD_DIM)
    clipped_qk = attn_qkv[:2].astype(wide) * root_scale[None, None, :]
    return (
        unpadded(layer_out),
        unpadded(grad_input),
        share[:3],
        share[3],
        share_small[:, :n_ex],
        share_small[:, n_ex : n_ex + 2].T,
        jnp.sum(share_in.astype(wide), axis=0)[None],
        jnp.sum(share_out.astype(wide), axis=0).T[None],
        head_max,
        clipped_qk,
    )


def solution(mesh):
    placed = (
        P(("dp", "expert"), None),
        P(None, "dp", None),
        P("dp", None),
        P("dp", None),
        P(None, "dp"),
        P("expert", None, None),
        P("expert", None, None),
        P(("dp", "expert"), None),
        P(),
        P(("dp", "expert"), None),
    )
    return jax.shard_map(
        per_device,
        mesh=mesh,
        in_specs=placed,
        out_specs=(
            P(("dp", "expert"), None),
            P(("dp", "expert"), None),
            P(None, "dp", None),
            P("dp", None),
            P("dp", None),
            P(None, "dp"),
            P("expert", "dp", None),
            P("expert", "dp", None),
            P(),
            P(None, "dp", None),
        ),
        check_vma=False,
    )
```

time: 904 us -> 443 us (0.49)
  Pallas kernels: 0 us -> 413 us
  waiting for transfers between devices: 337 us -> 0 us
  matrix products: 237 us -> 0 us
  local copies, waits for them, and re-layouts: 151 us -> 18.9 us
  blocking collectives: 71.1 us -> 0 us
  other arithmetic: 46.9 us -> 7.56 us
  starting transfers between devices: 34.6 us -> 0 us
  between operations: 16.1 us -> 0.77 us
    pallas_call x0 -> x1, Pallas kernels: none -> 413 us  [run_block(): pl.pallas_call(functools.partial(block_kernel, n_dp, n_ex, capacity), out...]
    dot_general x50 -> x0, matrix products: 226 us -> none  [the longest x2 32.5 us: per_device(): jnp.einsum('rd,fd->rf', grad_rows, weight_out, preferred_element_type=jnp...]
    all_to_all x8 -> x0, waiting for transfers between devices: 130 us -> none  [the longest x2 41.1 us: per_device(): lax.all_to_all(grad_buffer, 'expert', split_axis=0, concat_axis=0, tiled=...]
    reduce_scatter x3 -> x0, waiting for transfers between devices: 99.1 us -> none  [the longest x1 57.2 us: per_device(): lax.psum_scatter(grad_out[None].astype(jnp.bfloat16), 'dp', scatter_dimen...]
    psum x1 -> x0, waiting for transfers between devices: 60.8 us -> none  [per_device(): lax.psum(attn_grads[0].astype(jnp.bfloat16), 'expert').astype(jnp.float32)]
    unnamed x255 -> x23, local copies, waits for them, and re-layouts: 44.5 us -> 4.97 us
    pmax x1 -> x0, blocking collectives: 37.3 us -> none  [per_device(): head_max = lax.pmax(running, ('dp', 'expert'))]
    all_to_all x8 -> x0, starting transfers between devices: 34.1 us -> none  [the longest x2 9.04 us: per_device(): lax.all_to_all(buffer, 'expert', split_axis=0, concat_axis=0, tiled=True)]
  transfers between devices with their start and end apart: 17 -> 0, of which waited for: 13 -> 0; matrix products, arithmetic and copies ran while one was open for 32% -> 0% of each run, Pallas kernels for 0% -> 0%
where the time goes in v2:
time: 443 us; the launch traced here: 440 us
  Pallas kernels  413 us (93%)
  local copies, waits for them, and re-layouts  18.9 us (4%)
  other arithmetic  7.56 us (2%)
    pallas_call x1, Pallas kernels, run_block(): pl.pallas_call(functools.partial(block_kernel, n_dp, n_ex, capacity), out...  413 us

profile of v2, /device:TPU:0, one launch (start us, length us, event | category | flops | bytes accessed | tf_op | source)
XLA Modules:
  0.0 440.5 jit_solution(5663622340273145204)
XLA Ops:
  0.7 0.1 pad.16.clone
  0.7 0.8 reshape.58
  1.5 0.7 reshape.59
  2.2 0.8 copy.32
  3.0 0.8 copy.31
  3.9 0.7 maximum_maximum_fusion.small_in
  4.6 1.7 reshape.54
  6.3 1.1 pad.11
  7.4 0.3 reshape.56
  7.8 1.1 pad.12
  8.9 413.3 %encoder_block.1 = (bf16[2,416,768]{2,1,0:T(8,128)(2,1)}, bf16[2,416,768]{2,1,0:T(8,128)(2,1)}, bf16[2,384,768]{2,1,0:T(8,128)(2,1)}, f32[192,128]{1,0:T(8,128)}...) custom-call(bf16[2,416,768]{2,1,0:T(8,128)(2,1)} %bitcast.26, ...), custom_call_target="tpu_custom_call" | custom-call | tf_op jit(solution)/shard_map/encoder_block/pallas_call | solution.py:1059
  422.2 1.4 slice.32
  423.5 1.3 reshape.61
  424.9 1.5 slice.33
  426.4 1.3 reshape.63
  427.7 0.1 slice_reduce_fusion
  427.8 0.0 copy-done.6
  427.8 0.0 copy-start.5
  427.9 0.1 broadcast_in_dim.15
  427.9 0.1 mul.10
  428.0 0.7 copy.33
  428.7 0.1 slice_bitcast_fusion.1
  428.8 0.7 copy.34
  429.4 0.0 copy-done.1
  429.4 1.1 convert_multiply_fusion
  430.5 1.4 slice.34
  431.9 0.2 convert.1
  432.1 0.0 slice-start.1
  432.1 0.9 slice_bitcast_fusion
  433.0 4.8 %convert_reduce_fusion.1 = f32[192,3072]{1,0:T(8,128)} fusion(bf16[4,192,3072]{2,1,0:T(8,128)(2,1)} %get-tuple-element.21), kind=kLoop, calls=%fused_computation.1 | loop fusion | flops 4128768 | bytes 7077888 | tf_op jit(solution)/shard_map/reduce_sum | solution.py:1163
  437.8 0.7 convert_reduce_fusion
  438.5 2.0 copy.35
  (19 shorter events, 0.1 us)
Async XLA Ops:
  4.6 2.8 copy-start.2
  424.9 2.8 copy-start.4
  424.9 2.9 copy-start.6
  424.9 3.1 copy-start.3
  424.9 4.6 %copy-start.1 = (bf16[3,192,768]{2,1,0:T(8,128)(2,1)S(1)}, bf16[3,192,768]{2,1,0:T(8,128)(2,1)}, u32[]{:S(2)}) copy-start(bf16[3,192,768]{2,1,0:T(8,128)(2,1)} %qkv_in.1) | copy-start | bytes 2654212
  426.4 4.2 copy-start
  427.8 4.1 copy-start.5
  430.5 7.2 %slice-start = ((s8[4718592]{0:T(1024)(128)(4,1)}), s8[4194304]{0:T(1024)(128)(4,1)S(1)}, s32[]{:S(2)}) async-start(s8[4718592]{0:T(1024)(128)(4,1)} %bitcast.30), calls=%async_computation | async-start | bytes 8388608
  432.1 5.7 %slice-start.1 = ((s8[4718592]{0:T(1024)(128)(4,1)}), s8[524288]{0:T(1024)(128)(4,1)S(1)}, s32[]{:S(2)}) async-start(s8[4718592]{0:T(1024)(128)(4,1)} %bitcast.30), calls=%async_computation.1 | async-start | bytes 1048576

commit v3 on v2

v3 whole, which is shorter than its diff:
```python
import functools
import jax
import jax.numpy as jnp
from jax import lax
from jax.experimental import pallas as pl
from jax.experimental.pallas import tpu as pltpu
from jax.sharding import PartitionSpec as P

D = 768
HEADS = 12
HEAD_DIM = 64
FF = 3072
SEQ = 197
IMG_DEV = 2
MB = 2
TOK_MB = 394
SEQ_PAD = 208
TOK_PAD = IMG_DEV * SEQ_PAD
PAIRS = HEADS // 2
UNROLL = 6
COLS = 256

epsilon = 1e-06
qk_scale = 0.125
gelu_coeff = 0.7978845608028654
low = jnp.bfloat16
wide = jnp.float32

NN = (((1,), (0,)), ((), ()))
NT = (((1,), (1,)), ((), ()))
TN = (((0,), (0,)), ((), ()))


def dot(left, right, dims=NN):
    return lax.dot_general(left, right, dims, preferred_element_type=wide)


def rows_of(index, size):
    return pl.ds(pl.multiple_of(index * size, size), size)


def loop(count, body, unroll=1):
    def step(index, carry):
        body(index)
        return carry

    lax.fori_loop(0, count, step, 0, unroll=unroll)


def norm_parts(values_in):
    row_mean = jnp.sum(values_in, axis=-1, keepdims=True) * (1.0 / D)
    centred = values_in - row_mean
    row_var = jnp.sum(centred * centred, axis=-1, keepdims=True) * (1.0 / D)
    inverse = lax.rsqrt(row_var + epsilon)
    return centred * inverse, inverse


def norm_back(unit, inverse, gain_row, incoming):
    scaled = incoming * gain_row
    mean_one = jnp.sum(scaled, axis=-1, keepdims=True) * (1.0 / D)
    mean_two = jnp.sum(scaled * unit, axis=-1, keepdims=True) * (1.0 / D)
    return (scaled - mean_one - unit * mean_two) * inverse


def fold_rows(values_in):
    return jnp.sum(values_in.reshape(-1, 8, values_in.shape[-1]), axis=0)


def gelu_both(values_in):
    squared = values_in * values_in
    bent = jnp.tanh(values_in * (gelu_coeff + (gelu_coeff * 0.044715) * squared))
    half = 0.5 + 0.5 * bent
    slope = half + half * (1.0 - bent) * values_in * (
        gelu_coeff + (3.0 * 0.044715 * gelu_coeff) * squared
    )
    return values_in * half, slope


def head_mask(half):
    lane = lax.broadcasted_iota(jnp.int32, (1, 2 * HEAD_DIM), 1)
    return (lane // HEAD_DIM) == half


def attention_forward(
    tok, gains, wqkv, wout, first, qkv, probs, mixed, resid, second, tops, after_qkv, before_out
):
    def norm_one(index):
        rows = rows_of(index, TOK_PAD)
        unit, _ = norm_parts(tok[rows, :].astype(wide))
        first[rows, :] = (unit * gains[0:1, :]).astype(low)

    loop(1, norm_one)

    def project(index):
        part, cols = index // (D // COLS), rows_of(index % (D // COLS), COLS)
        qkv[part, :, cols] = dot(first[...], wqkv[part, :, cols]).astype(low)

    loop(3 * (D // COLS), project)
    after_qkv()

    def attend(index):
        image, pair = index // PAIRS, index % PAIRS
        rows, cols = rows_of(image, SEQ_PAD), rows_of(pair, 2 * HEAD_DIM)
        query, key, value = qkv[0, rows, cols], qkv[1, rows, cols], qkv[2, rows, cols]
        key_id = lax.broadcasted_iota(jnp.int32, (SEQ_PAD, SEQ_PAD), 1)
        row_id = lax.broadcasted_iota(jnp.int32, (SEQ_PAD, 1), 0)
        total = jnp.zeros((SEQ_PAD, 2 * HEAD_DIM), wide)
        for half in range(2):
            mask = head_mask(half)
            scores = dot(jnp.where(mask, query * qk_scale, 0.0).astype(low), key, NT)
            scores = jnp.where(key_id < SEQ, scores, -jnp.inf)
            row_top = jnp.max(scores, axis=-1, keepdims=True)
            exp_scores = jnp.exp(scores - row_top)
            attn = exp_scores * (1.0 / jnp.sum(exp_scores, axis=-1, keepdims=True))
            attn = attn.astype(low)
            probs[2 * index + half] = attn
            total += dot(attn, jnp.where(mask, value, 0.0).astype(low))
            top = jnp.max(jnp.where(row_id < SEQ, row_top, -jnp.inf), axis=0, keepdims=True)
            slot = pl.ds(2 * pair + half, 1)
            tops[slot, :] = jnp.maximum(tops[slot, :], jnp.broadcast_to(top, (1, 128)))
        mixed[rows, cols] = total.astype(low)

    loop(IMG_DEV * PAIRS, attend, UNROLL)
    before_out()

    def add_out(index):
        cols = rows_of(index, COLS)
        resid[:, cols] = tok[:, cols].astype(wide) + dot(mixed[...], wout[:, cols])

    loop(D // COLS, add_out)

    def norm_two(index):
        rows = rows_of(index, TOK_PAD)
        unit, _ = norm_parts(resid[rows, :])
        second[rows, :] = (unit * gains[1:2, :]).astype(low)

    loop(1, norm_two)


def spread_rows(raw, buffer, padded):
    count = raw.shape[0]
    buffer[pl.ds(0, count), :] = raw[...].astype(wide)
    buffer[pl.ds(count, SEQ_PAD - SEQ + 1), :] = jnp.zeros((SEQ_PAD - SEQ + 1, D), wide)
    inside = lax.broadcasted_iota(jnp.int32, (SEQ_PAD, 1), 0) < SEQ
    for image in range(MB * IMG_DEV):
        rows = buffer[pl.ds(image * SEQ, SEQ_PAD), :]
        spot = pl.ds((image % IMG_DEV) * SEQ_PAD, SEQ_PAD)
        padded[image // IMG_DEV, spot, :] = jnp.where(inside, rows, 0.0).astype(low)


def compact_rows(padded, buffer, target):
    for image in range(MB * IMG_DEV):
        spot = pl.ds((image % IMG_DEV) * SEQ_PAD, SEQ_PAD)
        buffer[pl.ds(image * SEQ, SEQ_PAD), :] = padded[image // IMG_DEV, spot, :]
    target[...] = buffer[pl.ds(0, target.shape[0]), :].astype(low)


def place_tokens(route, capacity, named, place, first, count):
    experts = named.shape[0]
    expert_id = lax.broadcasted_iota(jnp.int32, (experts, TOK_PAD), 0)
    is_named = (route[0:1, :] == expert_id) | (route[1:2, :] == expert_id)
    earlier = lax.broadcasted_iota(jnp.int32, (TOK_PAD, TOK_PAD), 0) < lax.broadcasted_iota(
        jnp.int32, (TOK_PAD, TOK_PAD), 1
    )
    ones = jnp.where(is_named, 1.0, 0.0)
    before = dot(ones.astype(low), jnp.where(earlier, 1.0, 0.0).astype(low))
    named[...] = jnp.where(is_named, before, -1.0)
    slot_id = lax.broadcasted_iota(jnp.int32, (capacity, TOK_PAD), 0).astype(wide)

    def one(index):
        hit = slot_id == named[pl.ds(first + index, 1), :]
        place[rows_of(index, capacity), :] = jnp.where(hit, 1.0, 0.0).astype(low)

    loop(count, one)


def split_three(values_in):
    head = values_in.astype(low)
    rest = values_in - head.astype(wide)
    middle = rest.astype(low)
    return [head, middle, (rest - middle.astype(wide)).astype(low)]


def gate_tokens(second, router_t, named, gate):
    logits = dot(router_t[...], second[...], NT)
    is_named = named[...] >= 0.0
    top = jnp.max(jnp.where(is_named, logits, -jnp.inf), axis=0, keepdims=True)
    exp_logits = jnp.where(is_named, jnp.exp(logits - jnp.where(top > -jnp.inf, top, 0.0)), 0.0)
    total = jnp.sum(exp_logits, axis=0, keepdims=True)
    gate[...] = exp_logits / jnp.where(total > 0.0, total, 1.0)


def own_columns(experts, capacity):
    shape = (experts, experts * capacity)
    column = lax.broadcasted_iota(jnp.int32, shape, 1) // capacity
    return column == lax.broadcasted_iota(jnp.int32, shape, 0)


def exact_dot(left, right, dims):
    count = left.shape[0]
    found = dot(jnp.concatenate(split_three(left), axis=0), right, dims)
    return found[0:count] + found[count : 2 * count] + found[2 * count : 3 * count]


def gate_slots(gate, place, capacity, slot_gate):
    experts = gate.shape[0]
    found = exact_dot(gate[...], place[...], NT)
    row = jnp.sum(jnp.where(own_columns(experts, capacity), found, 0.0), axis=0, keepdims=True)
    for expert in range(experts):
        slot_gate[expert, 0:1, 0:capacity] = row[:, expert * capacity : (expert + 1) * capacity]


def backward_scores(
    gains, wout, qkv, probs, resid, grad, attended, proj, scratch, gain_sums, cot, after_norm
):
    def norm_two(index):
        rows = rows_of(index, TOK_PAD)
        unit, inverse = norm_parts(resid[rows, :])
        incoming = grad[rows, :]
        grad_resid = cot[rows, :].astype(wide) + norm_back(
            unit, inverse, gains[1:2, :], incoming
        )
        gain_sums[1] += fold_rows(incoming * unit)
        grad[rows, :] = grad_resid
        attended[rows, :] = grad_resid.astype(low)

    loop(1, norm_two)
    after_norm()

    def through_out(index):
        cols = rows_of(index, COLS)
        scratch[:, cols] = dot(attended[...], wout[cols, :], NT).astype(low)

    loop(D // COLS, through_out)

    def attend(index):
        image, pair = index // PAIRS, index % PAIRS
        rows, cols = rows_of(image, SEQ_PAD), rows_of(pair, 2 * HEAD_DIM)
        query, key, value = qkv[0, rows, cols], qkv[1, rows, cols], qkv[2, rows, cols]
        incoming = scratch[rows, cols]
        shape = (SEQ_PAD, 2 * HEAD_DIM)
        grad_query, grad_key, grad_value = (jnp.zeros(shape, wide) for _ in range(3))
        for half in range(2):
            mask = head_mask(half)
            attn_low = probs[2 * index + half]
            attn = attn_low.astype(wide)
            grad_mixed = jnp.where(mask, incoming, 0.0).astype(low)
            grad_probs = dot(grad_mixed, value, NT)
            grad_value += dot(attn_low, grad_mixed, TN)
            row_dot = jnp.sum(attn * grad_probs, axis=-1, keepdims=True)
            grad_scores = (attn * (grad_probs - row_dot)).astype(low)
            grad_query += dot(grad_scores, jnp.where(mask, key * qk_scale, 0.0).astype(low))
            grad_key += dot(grad_scores, jnp.where(mask, query * qk_scale, 0.0).astype(low), TN)
        proj[0, rows, cols] = grad_query.astype(low)
        proj[1, rows, cols] = grad_key.astype(low)
        proj[2, rows, cols] = grad_value.astype(low)

    loop(IMG_DEV * PAIRS, attend, UNROLL)


def backward_input(tok, gains, wqkv, grad, proj, gain_sums, result):
    def through_qkv(index):
        cols = rows_of(index, COLS)
        total = dot(proj[0], wqkv[0, cols, :], NT)
        total += dot(proj[1], wqkv[1, cols, :], NT)
        result[:, cols] = total + dot(proj[2], wqkv[2, cols, :], NT)

    loop(D // COLS, through_qkv)

    def norm_one(index):
        rows = rows_of(index, TOK_PAD)
        unit, inverse = norm_parts(tok[rows, :].astype(wide))
        incoming = result[rows, :]
        gain_sums[0] += fold_rows(incoming * unit)
        grad[rows, :] += norm_back(unit, inverse, gains[0:1, :], incoming)

    loop(1, norm_one)


ANY = pl.BlockSpec(memory_space=pl.ANY)
VMEM = pl.BlockSpec(memory_space=pltpu.VMEM)
MESH = pl.DeviceIdType.MESH
BLOCK_ROWS = 512
MADE_ROWS = 256
BLOCK_FF = 512
GRAD_FF = 256
KIND_COT, KIND_ROW, KIND_BACK, KIND_MADE, KIND_GATE, KIND_SLOPE = range(6)


def wait_bytes(ref, sem):
    pltpu.make_async_copy(ref, ref, sem).wait()


def local_copy(source, target, sem):
    copy = pltpu.make_async_copy(source, target, sem)
    copy.start()
    return copy


def block_kernel(
    n_dp,
    n_ex,
    capacity,
    tok_in,
    cot_in,
    route_in,
    qkv_in,
    out_in,
    router_in,
    gains_in,
    expert_in,
    expert_out,
    layer_out,
    grad_input,
    share,
    share_small,
    share_in,
    share_out,
    tops_out,
    land,
    spill_hidden,
    spill_grad,
    spill_probs,
    spill_qkv,
    spill_rows,
    spill_tok,
    spill_cot,
    spill_resid,
    land_qkv,
    land_out,
    hub_rows,
    hub_blocks,
    far_land,
    stage_in,
    stage_out,
    pair_land,
    dp_land,
    part_land,
    route,
    route_far,
    small_own,
    small_land,
    small_t,
    router_low,
    gains,
    second,
    place,
    place_far,
    named,
    named_far,
    gate,
    send,
    hub_buf,
    hub_sums,
    gate_send,
    gate_land,
    slope_send,
    slope_land,
    tops,
    tops_land,
    tops_dp,
    small_sum,
    small_pair,
    small_cut,
    small_dp,
    small_part,
    gain_sums,
    gather_send,
    gather_recv,
    share_send,
    share_sem,
    ex_send,
    ex_recv,
    far_send,
    far_recv,
    full_send,
    full_recv,
    hub_recv,
    sum_send,
    sum_recv,
    route_recv,
    own_near,
    own_far,
    own_hub,
    hub_sem,
    rs_send,
    rs_recv,
    red_send,
    red_recv,
    pair_send,
    pair_recv,
    own_send,
    own_recv,
    local_sem,
):
    dp, me = lax.axis_index("dp"), lax.axis_index("expert")
    shard = D // n_dp
    slots = n_ex * capacity
    own_rows = rows_of(dp, shard)

    barrier = pltpu.get_barrier_semaphore()

    def greet_ex(step):
        pl.semaphore_signal(
            barrier, inc=1, device_id=(dp, me ^ (step + 1)), device_id_type=MESH
        )

    def greet_dp(step):
        pl.semaphore_signal(
            barrier, inc=1, device_id=(dp ^ (step + 1), me), device_id_type=MESH
        )

    loop(n_ex - 1, greet_ex)
    loop(n_dp - 1, greet_dp)
    pl.semaphore_wait(barrier, n_ex - 1 + n_dp - 1)

    def remote(source, target, send_sem, recv_sem, device):
        pltpu.make_async_remote_copy(
            src_ref=source,
            dst_ref=target,
            send_sem=send_sem,
            recv_sem=recv_sem,
            device_id=device,
            device_id_type=MESH,
        ).start()

    small_own[...] = jnp.zeros(small_own.shape, wide)
    small_own[0:n_ex, 0:shard] = router_in[...].astype(wide)
    small_own[n_ex : n_ex + 2, 0:shard] = gains_in[...].astype(wide)

    def gather_small(step):
        peer = (dp ^ (step + 1), me)
        remote(small_own, small_land.at[dp], gather_send.at[0], gather_recv.at[0], peer)

    core = lax.rem(me, 2)
    partner = (dp, me ^ 1)
    half_shard = shard // 2

    def half_rows_of(owner):
        return pl.ds(pl.multiple_of(owner * shard + core * half_shard, half_shard), half_shard)

    source_rows = rows_of(core, half_shard)

    def gather_qkv(step):
        peer = (dp ^ (step + 1), me)
        remote(
            qkv_in.at[:, source_rows, :],
            land_qkv.at[:, half_rows_of(dp), :],
            gather_send.at[1],
            share_sem.at[0, step],
            peer,
        )

    def gather_out(step):
        peer = (dp ^ (step + 1), me)
        remote(
            out_in.at[source_rows, :],
            land_out.at[half_rows_of(dp), :],
            gather_send.at[2],
            share_sem.at[1, step],
            peer,
        )

    def hand_qkv(step):
        rows = half_rows_of(dp ^ (step + 1))
        part = land_qkv.at[:, rows, :]
        wait_bytes(part, share_sem.at[0, step])
        remote(part, part, share_send.at[0], gather_recv.at[1], partner)

    def hand_out(step):
        rows = half_rows_of(dp ^ (step + 1))
        part = land_out.at[rows, :]
        wait_bytes(part, share_sem.at[1, step])
        remote(part, part, share_send.at[1], gather_recv.at[2], partner)

    loop(n_dp - 1, gather_small)
    loop(n_dp - 1, gather_qkv)
    loop(n_dp - 1, gather_out)
    own_small = local_copy(small_own, small_land.at[dp], local_sem.at[0])

    def load_qkv(target, sem):
        local_copy(qkv_in, target.at[:, own_rows, :], sem)

        def one(step):
            rows = rows_of(dp ^ (step + 1), shard)
            local_copy(land_qkv.at[:, rows, :], target.at[:, rows, :], sem)

        loop(n_dp - 1, one)
        wait_bytes(target, sem)

    def load_out(target, sem):
        local_copy(out_in, target.at[own_rows, :], sem)

        def one(step):
            rows = rows_of(dp ^ (step + 1), shard)
            local_copy(land_out.at[rows, :], target.at[rows, :], sem)

        loop(n_dp - 1, one)
        wait_bytes(target, sem)

    half_ex, quarter_ex = n_ex // 2, n_ex // 4
    half_slots = half_ex * capacity
    side, quarter, rank = me // half_ex, me // quarter_ex, lax.rem(me, quarter_ex)
    first_ex = side * half_ex
    far_ex = (1 - side) * half_ex
    own_index = me - first_ex
    is_hub = (quarter == 1) | (quarter == 2)
    hub = (2 - side) * quarter_ex + rank
    hub_slot = lax.rem(quarter, 2)

    def served(slot):
        return far_ex + slot * quarter_ex + rank

    def block_of(area, index):
        return send.at[area, rows_of(index, capacity), :]

    def wait_blocks(sem, count):
        wait_bytes(send.at[0, pl.ds(0, count * capacity), :], sem)

    def land_block(kind, micro, index):
        return land.at[kind, micro, rows_of(index, capacity), :]

    def near_wait(sems, kind, micro):
        wait_blocks(sems.at[kind, micro], half_ex - 1)

    def far_wait(sems, kind, micro):
        @pl.when(is_hub)
        def _():
            wait_blocks(sems.at[kind, micro], half_ex - 2)

        @pl.when(jnp.logical_not(is_hub))
        def _():
            wait_blocks(sems.at[kind, micro], half_ex)

    def relay_wait(kind, micro):
        @pl.when(is_hub)
        def _():
            wait_blocks(far_send.at[kind, micro], 2 * (half_ex - 1))

    def pack(spot, spot_start, source, area, area_start):
        rows = pl.ds(spot_start, half_slots)
        send[area, pl.ds(area_start, half_slots), :] = dot(spot[rows, :], source[...]).astype(low)

    def spread(area, start, kind, micro, source, send_sem, recv_sem, own_sem):
        def one(step):
            peer = me ^ (step + 1)
            remote(
                block_of(area, start + peer - first_ex),
                land_block(kind, micro, source),
                send_sem,
                recv_sem,
                (dp, peer),
            )

        loop(half_ex - 1, one)
        local_copy(block_of(area, start + own_index), land_block(kind, micro, source), own_sem)

    def scatter_full(kind, micro, source):
        remote(
            source,
            hub_rows.at[kind, micro, hub_slot],
            full_send.at[kind, micro],
            full_recv.at[kind, micro, hub_slot],
            (dp, hub),
        )

    def scatter_near(kind, micro, source):
        area = MB + micro
        pack(place.at[micro], pl.multiple_of(first_ex * capacity, half_slots), source, area, 0)
        spread(
            area,
            0,
            kind,
            micro,
            me,
            ex_send.at[kind, micro],
            ex_recv.at[kind, micro],
            own_near.at[kind, micro],
        )

    def relay(kind, micro):
        @pl.when(is_hub)
        def _():
            if kind == KIND_ROW:
                wait_blocks(far_send.at[KIND_COT, micro], 2 * (half_ex - 1))
                wait_blocks(own_far.at[KIND_COT, micro], 2)

            def fetch(slot):
                wait_bytes(hub_rows.at[kind, micro, slot], full_recv.at[kind, micro, slot])
                local_copy(
                    hub_rows.at[kind, micro, slot],
                    hub_buf.at[slot, pl.ds(0, TOK_PAD), :],
                    hub_sem.at[slot],
                )

            def one(slot):
                rows = hub_buf.at[slot, pl.ds(0, TOK_PAD), :]
                wait_bytes(rows, hub_sem.at[slot])
                pack(
                    place_far.at[micro, slot],
                    0,
                    rows,
                    micro,
                    pl.multiple_of(slot * half_slots, half_slots),
                )
                spread(
                    micro,
                    slot * half_ex,
                    kind,
                    micro,
                    served(slot),
                    far_send.at[kind, micro],
                    far_recv.at[kind, micro],
                    own_far.at[kind, micro],
                )

            loop(2, fetch)
            loop(2, one)

    def gather(kind, micro, area):
        def to_hub(step):
            source = far_ex + step
            slot = lax.rem(source // quarter_ex, 2)
            target = hub_blocks.at[kind - KIND_BACK, micro, slot, rows_of(own_index, capacity), :]
            device = (1 + side) * quarter_ex + lax.rem(source, quarter_ex)

            @pl.when(device == me)
            def _():
                local_copy(block_of(area, source), target, own_hub.at[kind - KIND_BACK, micro, slot])

            @pl.when(device != me)
            def _():
                remote(
                    block_of(area, source),
                    target,
                    far_send.at[kind, micro],
                    hub_recv.at[kind - KIND_BACK, micro, slot],
                    (dp, device),
                )

        def to_near(step):
            peer = me ^ (step + 1)
            remote(
                block_of(area, peer),
                land_block(kind, micro, own_index),
                ex_send.at[kind, micro],
                ex_recv.at[kind, micro],
                (dp, peer),
            )

        loop(half_ex, to_hub)
        loop(half_ex - 1, to_near)
        local_copy(
            block_of(area, me), land_block(kind, micro, own_index), own_near.at[kind, micro]
        )

    def hub_sum(kind, micro):
        index = kind - KIND_BACK

        @pl.when(is_hub)
        def _():
            def fetch(slot):
                if kind == KIND_MADE:
                    wait_bytes(hub_sums.at[micro, slot], sum_send.at[0, micro, slot])
                wait_blocks(hub_recv.at[index, micro, slot], half_ex - 1)
                wait_blocks(own_hub.at[index, micro, slot], 1)
                local_copy(hub_blocks.at[index, micro, slot], hub_buf.at[slot], hub_sem.at[slot])

            def one(slot):
                wait_bytes(hub_buf.at[slot], hub_sem.at[slot])
                hub_sums[micro, slot] = dot(place_far[micro, slot], hub_buf[slot], TN).astype(low)
                remote(
                    hub_sums.at[micro, slot],
                    far_land.at[index, micro],
                    sum_send.at[index, micro, slot],
                    sum_recv.at[index, micro],
                    (dp, served(slot)),
                )

            loop(2, fetch)
            loop(2, one)

    def fetch_gathered(kind, micro, arrived, sem):
        near_wait(ex_recv, kind, micro)
        wait_blocks(own_near.at[kind, micro], 1)
        index = kind - KIND_BACK
        wait_bytes(far_land.at[index, micro], sum_recv.at[index, micro])
        near = arrived.at[pl.ds(0, half_slots), :]
        far = arrived.at[pl.ds(half_slots, TOK_PAD), :]
        local_copy(land.at[kind, micro, pl.ds(0, half_slots), :], near, sem)
        local_copy(far_land.at[index, micro], far, sem)
        wait_bytes(arrived.at[pl.ds(0, half_slots + TOK_PAD), :], sem)

    def gathered(micro, arrived, cols):
        spot = place.at[micro, pl.ds(pl.multiple_of(first_ex * capacity, half_slots), half_slots)]
        near = arrived[pl.ds(0, half_slots), cols]
        far = arrived[pl.ds(half_slots, TOK_PAD), cols]
        return dot(spot[...], near, TN) + far.astype(wide)

    def exchange_small(source, target, kind, micro):
        def one(step):
            peer = me ^ (step + 1)
            remote(
                source.at[micro, peer],
                target.at[micro, me],
                ex_send.at[kind, micro],
                ex_recv.at[kind, micro],
                (dp, peer),
            )

        loop(n_ex - 1, one)
        target[micro, me] = source[micro, me]

    def await_small(sems, ref, kind, micro):
        wait_bytes(ref.at[micro, pl.ds(0, n_ex - 1)], sems.at[kind, micro])

    def forward(wqkv, wout, tok, cot, raw, buffer, probs, qkv, first, mixed, resid, spill_sem):
        def spills(micro):
            tokens = rows_of(micro, TOK_PAD)
            pairs = [
                (probs.at[micro], spill_probs.at[micro]),
                (qkv.at[micro], spill_qkv.at[micro]),
                (first.at[tokens], spill_rows.at[0, tokens]),
                (mixed.at[tokens], spill_rows.at[1, tokens]),
                (resid.at[micro], spill_resid.at[micro]),
            ]
            return [
                pltpu.make_async_copy(source, target, spill_sem.at[micro, index])
                for index, (source, target) in enumerate(pairs)
            ]

        local_copy(cot_in, raw, local_sem.at[3]).wait()
        spread_rows(raw, buffer, cot)
        keep_cot = local_copy(cot, spill_cot, spill_sem.at[MB, 1])
        load = local_copy(tok_in, raw, local_sem.at[3])
        numbers = route_in[...].astype(wide)
        fill = jnp.full((2, SEQ_PAD - SEQ), -1.0, wide)
        for micro in range(MB):
            pieces = []
            for image in range(IMG_DEV):
                start = micro * TOK_MB + image * SEQ
                pieces += [numbers[:, start : start + SEQ], fill]
            route[micro] = jnp.concatenate(pieces, axis=1).astype(jnp.int32)

        remote(
            route, route_far.at[hub_slot], route_recv.at[2], route_recv.at[hub_slot], (dp, hub)
        )
        keep_cot.wait()

        def send_cot(micro):
            scatter_full(KIND_COT, micro, spill_cot.at[micro])
            scatter_near(KIND_COT, micro, cot.at[micro])

        def place_own(micro):
            place_tokens(
                route.at[micro], capacity, named.at[micro], place.at[micro], 0, n_ex
            )

        own_small.wait()
        loop(MB, place_own)
        send_cot(0)

        @pl.when(is_hub)
        def _():
            def one(index):
                micro, slot = index // 2, lax.rem(index, 2)
                place_tokens(
                    route_far.at[slot, micro],
                    capacity,
                    named_far,
                    place_far.at[micro, slot],
                    first_ex,
                    half_ex,
                )

            for slot in range(2):
                wait_bytes(route, route_recv.at[slot])
            loop(2 * MB, one)

        load.wait()
        spread_rows(raw, buffer, tok)
        tops[...] = jnp.full(tops.shape, -jnp.inf, wide)
        wait_bytes(small_land.at[pl.ds(0, n_dp - 1)], gather_recv.at[0])
        for owner in range(n_dp):
            small_t[:, owner * shard : (owner + 1) * shard] = small_land[owner, :, 0:shard]
        router_low[...] = small_t[pl.ds(0, n_ex), :].astype(low)
        gains[...] = small_t[pl.ds(n_ex, 8), :]
        keep_tok = local_copy(tok, spill_tok, spill_sem.at[MB, 0])
        loop(n_dp - 1, hand_qkv)
        wait_bytes(land_qkv.at[:, pl.ds(0, (D - shard) // 2), :], gather_recv.at[1])
        load_qkv(wqkv, local_sem.at[1])

        def out_arrives():
            loop(n_dp - 1, hand_out)

        def out_there():
            wait_bytes(land_out.at[pl.ds(0, (D - shard) // 2), :], gather_recv.at[2])
            load_out(wout, local_sem.at[1])

        def one(micro):
            attention_forward(
                tok.at[micro],
                gains,
                wqkv,
                wout,
                first.at[rows_of(micro, TOK_PAD)],
                qkv.at[micro],
                probs.at[micro],
                mixed.at[rows_of(micro, TOK_PAD)],
                resid.at[micro],
                second.at[rows_of(micro, TOK_PAD)],
                tops,
                lambda: pl.when(micro == 0)(out_arrives),
                lambda: pl.when(micro == 0)(out_there),
            )
            for copy in spills(micro):
                copy.start()
            rows = second.at[rows_of(micro, TOK_PAD)]
            gate_tokens(rows, router_low, named.at[micro], gate.at[micro])
            gate_slots(gate.at[micro], place.at[micro], capacity, gate_send.at[micro])
            exchange_small(gate_send, gate_land, KIND_GATE, micro)
            scatter_full(KIND_ROW, micro, rows)
            near_wait(ex_send, KIND_COT, micro)
            wait_blocks(own_near.at[KIND_COT, micro], 1)
            scatter_near(KIND_ROW, micro, rows)

            @pl.when(micro == 0)
            def _():
                send_cot(1)
                relay(KIND_COT, 0)


        loop(MB, one)

        def spread_top(step):
            peer = me ^ (step + 1)
            remote(tops, tops_land.at[me], red_send.at[0], red_recv.at[0], (dp, peer))

        loop(n_ex - 1, spread_top)
        tops_land[me] = tops[...]
        for micro in range(MB):
            for copy in spills(micro):
                copy.wait()
        keep_tok.wait()

    pl.run_scoped(
        forward,
        pltpu.VMEM((3, D, D), low),
        pltpu.VMEM((D, D), low),
        pltpu.VMEM((MB, TOK_PAD, D), low),
        pltpu.VMEM((MB, TOK_PAD, D), low),
        pltpu.VMEM((MB * TOK_MB, D), low),
        pltpu.VMEM((MB * TOK_MB + SEQ_PAD - SEQ + 1, D), wide),
        pltpu.VMEM((MB, IMG_DEV * HEADS, SEQ_PAD, SEQ_PAD), low),
        pltpu.VMEM((MB, 3, TOK_PAD, D), low),
        pltpu.VMEM((MB * TOK_PAD, D), low),
        pltpu.VMEM((MB * TOK_PAD, D), low),
        pltpu.VMEM((MB, TOK_PAD, D), wide),
        pltpu.SemaphoreType.DMA((MB + 1, 5)),
    )

    def experts(w_in, w_out, rows_in, cot, grad_rows, rows_t, grad_t, hidden, grad_pre, made, sems):
        eye = lax.broadcasted_iota(jnp.int32, (capacity, capacity), 0) == lax.broadcasted_iota(
            jnp.int32, (capacity, capacity), 1
        )

        def gate_column(micro, source):
            row = gate_land[micro, source, 0:1, 0:capacity]
            return jnp.sum(jnp.where(eye, row, 0.0), axis=1, keepdims=True)

        loads = [
            local_copy(expert_in, w_in, local_sem.at[4]),
            local_copy(expert_out, w_out, local_sem.at[5]),
        ]
        relay(KIND_ROW, 0)
        for copy in loads:
            copy.wait()

        def one(micro):
            pl.when(micro > 0)(lambda: relay(KIND_ROW, micro))
            near_wait(ex_recv, KIND_COT, micro)
            far_wait(far_recv, KIND_COT, micro)
            await_small(ex_recv, gate_land, KIND_GATE, micro)
            near_wait(ex_recv, KIND_ROW, micro)
            far_wait(far_recv, KIND_ROW, micro)
            wait_blocks(own_near.at[KIND_ROW, micro], 1)

            @pl.when(is_hub)
            def _():
                wait_blocks(own_far.at[KIND_ROW, micro], 2)

            load_rows = local_copy(land.at[KIND_ROW, micro], rows_in, sems.at[0])
            load_cot = local_copy(land.at[KIND_COT, micro], cot, sems.at[1])
            load_rows.wait()
            load_cot.wait()

            def scale(source):
                rows = rows_of(source, capacity)
                wide_cot = cot[rows, :].astype(wide)
                grad_rows[rows, :] = (wide_cot * gate_column(micro, source)).astype(low)

            loop(n_ex, scale)

            def turn(index):
                rows = rows_of(index, 128)
                cols = pl.ds(pl.multiple_of(micro * slots + index * 128, 128), 128)
                rows_t[:, cols] = rows_in[rows, :].T
                grad_t[:, cols] = grad_rows[rows, :].T

            loop(slots // 128, turn)

            @pl.when(micro > 0)
            def _():
                pltpu.make_async_copy(hidden, spill_hidden, sems.at[2]).wait()
                pltpu.make_async_copy(grad_pre, spill_grad, sems.at[3]).wait()

            def through(index):
                cols = rows_of(index // (slots // BLOCK_ROWS), BLOCK_FF)
                rows = rows_of(index % (slots // BLOCK_ROWS), BLOCK_ROWS)
                value, slope = gelu_both(dot(rows_in[rows, :], w_in[:, cols]))
                hidden[rows, cols] = value.astype(low)
                grad_hidden = dot(grad_rows[rows, :], w_out[cols, :], NT)
                grad_pre[rows, cols] = (grad_hidden * slope).astype(low)

            loop((FF // BLOCK_FF) * (slots // BLOCK_ROWS), through, 2)

            @pl.when(micro < MB - 1)
            def _():
                local_copy(hidden, spill_hidden, sems.at[2])
                local_copy(grad_pre, spill_grad, sems.at[3])

            relay_wait(KIND_ROW, micro)

            def back(index):
                rows = rows_of(index, BLOCK_ROWS)
                send[micro, rows, :] = dot(grad_pre[rows, :], w_in[...], NT).astype(low)

            loop(slots // BLOCK_ROWS, back)
            gather(KIND_BACK, micro, micro)
            near_wait(ex_send, KIND_ROW, micro)

            def forth(index):
                rows = rows_of(index, MADE_ROWS)
                made[...] = dot(hidden[rows, :], w_out[...])
                count = MADE_ROWS // capacity

                def finish(part):
                    source = index * count + part
                    own = rows_of(source, capacity)
                    values = made[rows_of(part, capacity), :]
                    column = jnp.sum(values * cot[own, :].astype(wide), axis=1, keepdims=True)
                    slope_send[micro, source, 0:1, 0:capacity] = jnp.sum(
                        jnp.where(eye, column, 0.0), axis=0, keepdims=True
                    )
                    send[MB + micro, own, :] = (values * gate_column(micro, source)).astype(low)

                loop(count, finish)

            loop(slots // MADE_ROWS, forth)
            exchange_small(slope_send, slope_land, KIND_SLOPE, micro)
            pl.when(micro == 0)(lambda: relay(KIND_COT, 1))

        loop(MB, one)

        def send_made(micro):
            gather(KIND_MADE, micro, MB + micro)

        hub_sum(KIND_BACK, 0)
        loop(MB, send_made)

        wait_bytes(tops_land.at[pl.ds(0, n_ex - 1)], red_recv.at[0])
        wait_bytes(tops_land.at[pl.ds(0, n_ex - 1)], red_send.at[0])
        tops[...] = jnp.max(tops_land[...], axis=0)

    def expert_phase(
        w_in, w_out, rows_in, cot, grad_rows, rows_t, grad_t, hidden, grad_pre, made, sems
    ):
        experts(w_in, w_out, rows_in, cot, grad_rows, rows_t, grad_t, hidden, grad_pre, made, sems)
        weight_grads(rows_t, grad_t, hidden, grad_pre)
        hub_sum(KIND_BACK, 1)

    def weight_grads(rows_t, grad_t, hidden, grad_pre):
        blocks = FF // GRAD_FF
        half = pl.ds(0, slots)
        other = pl.ds(slots, slots)

        def scoped(kept_hidden, kept_grad, out_in, out_out, load_sems, store_sems):
            def fetch(block, slot):
                cols = rows_of(block, GRAD_FF)
                local_copy(spill_hidden.at[:, cols], kept_hidden.at[slot], load_sems.at[0, slot])
                local_copy(spill_grad.at[:, cols], kept_grad.at[slot], load_sems.at[1, slot])

            def stored(block, slot):
                cols = rows_of(block, GRAD_FF)
                return (
                    pltpu.make_async_copy(
                        out_in.at[slot], stage_in.at[:, cols], store_sems.at[0, slot]
                    ),
                    pltpu.make_async_copy(
                        out_out.at[slot], stage_out.at[:, cols], store_sems.at[1, slot]
                    ),
                    pltpu.make_async_copy(
                        out_in.at[slot, own_rows, :],
                        share_in.at[dp, :, cols],
                        store_sems.at[2, slot],
                    ),
                )

            def ship(block, slot):
                for copy in stored(block, slot):
                    copy.wait()
                cols = rows_of(block, GRAD_FF)

                def one(step):
                    peer = dp ^ (step + 1)
                    remote(
                        stage_in.at[rows_of(peer, shard), cols],
                        share_in.at[dp, :, cols],
                        rs_send.at[0],
                        rs_recv.at[0],
                        (peer, me),
                    )

                loop(n_dp - 1, one)

            fetch(0, 0)

            def one(block):
                slot = lax.rem(block, 2)

                @pl.when(block + 1 < blocks)
                def _():
                    fetch(block + 1, 1 - slot)

                wait_bytes(kept_hidden.at[slot], load_sems.at[0, slot])
                wait_bytes(kept_grad.at[slot], load_sems.at[1, slot])
                cols = rows_of(block, GRAD_FF)
                out_in[slot] = (
                    dot(rows_t[:, half], kept_grad[slot]) + dot(rows_t[:, other], grad_pre[:, cols])
                ).astype(low)
                out_out[slot] = (
                    dot(grad_t[:, half], kept_hidden[slot]) + dot(grad_t[:, other], hidden[:, cols])
                ).astype(low)
                for copy in stored(block, slot):
                    copy.start()

                @pl.when(block > 0)
                def _():
                    ship(block - 1, 1 - slot)

            loop(blocks, one)
            ship(blocks - 1, (blocks - 1) % 2)

        pl.run_scoped(
            scoped,
            pltpu.VMEM((2, slots, GRAD_FF), low),
            pltpu.VMEM((2, slots, GRAD_FF), low),
            pltpu.VMEM((2, D, GRAD_FF), low),
            pltpu.VMEM((2, D, GRAD_FF), low),
            pltpu.SemaphoreType.DMA((2, 2)),
            pltpu.SemaphoreType.DMA((3, 2)),
        )

    pl.run_scoped(
        expert_phase,
        pltpu.VMEM((D, FF), low),
        pltpu.VMEM((FF, D), low),
        pltpu.VMEM((slots, D), low),
        pltpu.VMEM((slots, D), low),
        pltpu.VMEM((slots, D), low),
        pltpu.VMEM((D, MB * slots), low),
        pltpu.VMEM((D, MB * slots), low),
        pltpu.VMEM((slots, FF), low),
        pltpu.VMEM((slots, FF), low),
        pltpu.VMEM((MADE_ROWS, D), wide),
        pltpu.SemaphoreType.DMA((4,)),
    )

    width = FF // n_dp

    def ship_out(step):
        peer = dp ^ (step + 1)
        remote(
            stage_out.at[:, rows_of(peer, width)],
            share_out.at[dp],
            rs_send.at[1],
            rs_recv.at[1],
            (peer, me),
        )

    def spread_tops(step):
        peer = dp ^ (step + 1)
        remote(tops, tops_dp.at[dp], red_send.at[1], red_recv.at[1], (peer, me))

    loop(n_dp - 1, spread_tops)
    tops_dp[dp] = tops[...]

    chips = parts = n_ex // 2
    part_rows = part_size(n_dp, n_ex)
    z = me // 2

    def backward(
        wqkv,
        wout,
        resid,
        cot,
        probs,
        qkv,
        first,
        mixed,
        arrived,
        grad,
        attended,
        proj,
        result,
        out,
        grads,
        pairs,
        part_own,
        buffer,
        compact,
        sems,
    ):
        first_loads = [
            local_copy(source, target, sems.at[index])
            for index, (source, target) in enumerate(
                [
                    (spill_rows.at[0], first),
                    (spill_rows.at[1], mixed),
                    (spill_resid, resid),
                ]
            )
        ]
        kept_out = arrived.at[pl.ds(0, D), pl.ds(0, width)]
        local_copy(stage_out.at[:, rows_of(dp, width)], kept_out, sems.at[5]).wait()
        local_copy(kept_out, share_out.at[dp], sems.at[5]).wait()
        gain_sums[...] = jnp.zeros(gain_sums.shape, wide)
        small_sum[...] = jnp.zeros(small_sum.shape, wide)
        for copy in first_loads:
            copy.wait()
        load_qkv(wqkv, sems.at[4])
        load_out(wout, sems.at[4])

        def own_half(which):
            return pl.ds(pl.multiple_of(which * half_shard, half_shard), half_shard)

        def to_partner(part):
            remote(
                grads.at[part, :, own_half(1 - core), :],
                pair_land.at[part],
                pair_send.at[part],
                pair_recv.at[part],
                partner,
            )

        def to_owners(part):
            wait_bytes(pair_land.at[part], pair_recv.at[part])
            local_copy(pair_land.at[part], pairs.at[part], sems.at[5]).wait()

            def add_pair(owner):
                mine = grads[part, owner, own_half(core), :].astype(wide)
                pairs[part, owner] = (mine + pairs[part, owner].astype(wide)).astype(low)

            loop(n_dp, add_pair)

            def one(step):
                peer = dp ^ (step + 1)
                remote(
                    pairs.at[part, peer],
                    dp_land.at[dp, own_half(part), :],
                    own_send.at[part],
                    own_recv.at[part],
                    (peer, me),
                )

            loop(n_dp - 1, one)

        def grad_block(part, left, right):
            def one(block):
                cols = rows_of(block, COLS)
                value = dot(left[...], right[:, cols], TN).astype(low)
                for owner in range(n_dp):
                    grads[part, owner, :, cols] = value[owner * shard : (owner + 1) * shard, :]

            loop(D // COLS, one)
            to_partner(part)

        def one(micro):
            tokens = rows_of(micro, TOK_PAD)
            loads = [
                local_copy(spill_probs.at[micro], probs, sems.at[0]),
                local_copy(spill_qkv.at[micro], qkv, sems.at[1]),
                local_copy(spill_cot.at[micro], cot, sems.at[2]),
            ]
            await_small(ex_recv, slope_land, KIND_SLOPE, micro)
            fetch_gathered(KIND_BACK, micro, arrived, sems.at[3])
            row = jnp.concatenate(
                [slope_land[micro, expert, 0:1, 0:capacity] for expert in range(n_ex)], axis=1
            )
            blocks = jnp.where(own_columns(n_ex, capacity), row, 0.0)
            slope = exact_dot(blocks, place[micro], NN)
            gates = gate[micro]
            grad_logits = gates * (slope - jnp.sum(gates * slope, axis=0, keepdims=True))
            grad_logits = grad_logits.astype(low)
            small_sum[pl.ds(0, n_ex), :] += dot(grad_logits, second[tokens, :])
            for block in range(D // COLS):
                cols = pl.ds(block * COLS, COLS)
                grad[micro, :, cols] = gathered(micro, arrived, cols) + dot(
                    grad_logits, router_low[:, cols], TN
                )
            for load in loads:
                load.wait()
            backward_scores(
                gains,
                wout,
                qkv,
                probs,
                resid.at[micro],
                grad.at[micro],
                attended.at[tokens],
                proj.at[:, tokens, :],
                out,
                gain_sums,
                cot,
                lambda: pl.when(micro == MB - 1)(lambda: grad_block(3, mixed, attended)),
            )
            pl.when(micro == 0)(lambda: loop(2, ship_out))

        loop(MB, one)
        to_owners(3)
        hub_sum(KIND_MADE, 0)
        for part in range(3):
            grad_block(part, first, proj.at[part])
        for part in range(3):
            to_owners(part)
        loop(n_dp - 3, lambda step: ship_out(step + 2))
        hub_sum(KIND_MADE, 1)

        def finish(micro):
            local_copy(spill_tok.at[micro], cot, sems.at[2]).wait()
            backward_input(
                cot,
                gains,
                wqkv,
                grad.at[micro],
                proj.at[:, rows_of(micro, TOK_PAD), :],
                gain_sums,
                result,
            )

        loop(MB, finish)
        small_sum[n_ex : n_ex + 1, :] = jnp.sum(gain_sums[0], axis=0, keepdims=True)
        small_sum[n_ex + 1 : n_ex + 2, :] = jnp.sum(gain_sums[1], axis=0, keepdims=True)
        remote(small_sum, small_pair, red_send.at[3], red_recv.at[3], partner)
        compact_rows(grad, buffer, compact)
        store = local_copy(compact, grad_input, sems.at[4])
        wait_bytes(small_pair, red_recv.at[3])
        both = small_sum[...] + small_pair[...]
        small_cut[...] = jnp.zeros(small_cut.shape, wide)
        for owner in range(n_dp):
            small_cut[owner, :, 0:shard] = both[:, owner * shard : (owner + 1) * shard]

        def small_to_owner(step):
            peer = dp ^ (step + 1)
            remote(
                small_cut.at[peer], small_dp.at[dp], red_send.at[5], red_recv.at[5], (peer, me)
            )

        loop(n_dp - 1, small_to_owner)
        small_dp[dp] = small_cut[dp]
        for part in range(4):
            wait_bytes(dp_land.at[pl.ds(0, n_dp - 1), own_half(part), :], own_recv.at[part])
            result[pl.ds(part * half_shard, half_shard), :] = pairs[part, dp].astype(wide)

        def load_dp(step):
            peer = dp ^ (step + 1)
            local_copy(dp_land.at[peer], proj_rows(step), sems.at[0])

        def proj_rows(step):
            return proj.at[lax.rem(step, 3), rows_of(step // 3, 2 * shard), :]

        loop(n_dp - 1, load_dp)
        wait_bytes(dp_land.at[pl.ds(0, n_dp - 1)], sems.at[0])

        def add_dp(step):
            result[pl.ds(0, 2 * shard), :] += proj_rows(step)[...].astype(wide)

        loop(n_dp - 1, add_dp)
        total = parts * part_rows
        if total > 2 * shard:
            result[pl.ds(2 * shard, total - 2 * shard), :] = jnp.zeros(
                (total - 2 * shard, D), wide
            )
        grad_low = arrived
        grad_low[pl.ds(0, total), :] = result[pl.ds(0, total), :].astype(low)

        def chip(index):
            return (dp, 2 * index + core)

        def to_part(step):
            peer = z ^ (step + 1)
            remote(
                grad_low.at[rows_of(peer, part_rows), :],
                part_land.at[z],
                red_send.at[6],
                red_recv.at[6],
                chip(peer),
            )

        loop(parts - 1, to_part)
        wait_bytes(small_dp.at[pl.ds(0, n_dp - 1)], red_recv.at[5])
        small_part[me] = jnp.sum(small_dp[...], axis=0)

        def to_chip(step):
            remote(
                small_part.at[me],
                small_part.at[me],
                red_send.at[7],
                red_recv.at[7],
                chip(z ^ (step + 1)),
            )

        loop(parts - 1, to_chip)
        mine = rows_of(z, part_rows)
        result[pl.ds(0, part_rows), :] = grad_low[mine, :].astype(wide)
        wait_bytes(part_land.at[pl.ds(0, parts - 1)], red_recv.at[6])

        def load_part(step):
            peer = z ^ (step + 1)
            local_copy(part_land.at[peer], part_own.at[step], sems.at[0])

        loop(parts - 1, load_part)
        wait_bytes(part_own, sems.at[0])

        def add_part(step):
            result[pl.ds(0, part_rows), :] += part_own[step].astype(wide)

        loop(parts - 1, add_part)

        summed = out.at[pl.ds(0, part_rows), :]
        summed[...] = result[pl.ds(0, part_rows), :].astype(low)

        def to_all(step):
            remote(
                summed,
                share.at[core, mine, :],
                red_send.at[8],
                red_recv.at[8],
                chip(z ^ (step + 1)),
            )

        loop(parts - 1, to_all)
        local_copy(summed, share.at[core, mine, :], sems.at[0]).wait()
        wait_bytes(grad_low.at[pl.ds(0, (parts - 1) * part_rows), :], red_send.at[6])

        def combine(micro):
            fetch_gathered(KIND_MADE, micro, arrived, sems.at[3])
            for block in range(D // COLS):
                cols = pl.ds(block * COLS, COLS)
                grad[micro, :, cols] = resid[micro, :, cols] + gathered(micro, arrived, cols)

        loop(MB, combine)
        store.wait()
        compact_rows(grad, buffer, compact)
        store = local_copy(compact, layer_out, sems.at[4])
        wait_bytes(share.at[0, pl.ds(0, (parts - 1) * part_rows), :], red_recv.at[8])
        half_rows = pl.ds(0, 2 * shard)
        remote(
            share.at[core, half_rows, :],
            share.at[core, half_rows, :],
            red_send.at[9],
            red_recv.at[9],
            partner,
        )
        wait_bytes(small_part.at[pl.ds(0, parts - 1)], red_recv.at[7])
        chosen = small_part[core]
        for index in range(1, chips):
            chosen += small_part[2 * index + core]
        share_small[...] = chosen
        wait_bytes(tops_dp.at[pl.ds(0, n_dp - 1)], red_recv.at[1])
        tops_out[...] = jnp.max(tops_dp[...], axis=0)
        wait_bytes(share.at[0, half_rows, :], red_recv.at[9])
        store.wait()

        for part in range(4):
            wait_bytes(pair_land.at[part], pair_send.at[part])
            wait_bytes(dp_land.at[pl.ds(0, n_dp - 1), own_half(part), :], own_send.at[part])
        wait_bytes(grad_low.at[pl.ds(0, (parts - 1) * part_rows), :], red_send.at[8])

    pl.run_scoped(
        backward,
        pltpu.VMEM((3, D, D), low),
        pltpu.VMEM((D, D), low),
        pltpu.VMEM((MB, TOK_PAD, D), wide),
        pltpu.VMEM((TOK_PAD, D), low),
        pltpu.VMEM((IMG_DEV * HEADS, SEQ_PAD, SEQ_PAD), low),
        pltpu.VMEM((3, TOK_PAD, D), low),
        pltpu.VMEM((MB * TOK_PAD, D), low),
        pltpu.VMEM((MB * TOK_PAD, D), low),
        pltpu.VMEM((slots, D), low),
        pltpu.VMEM((MB, TOK_PAD, D), wide),
        pltpu.VMEM((MB * TOK_PAD, D), low),
        pltpu.VMEM((3, MB * TOK_PAD, D), low),
        pltpu.VMEM((TOK_PAD, D), wide),
        pltpu.VMEM((TOK_PAD, D), low),
        pltpu.VMEM((4, n_dp, shard, D), low),
        pltpu.VMEM((4, n_dp, half_shard, D), low),
        pltpu.VMEM((parts - 1, part_rows, D), low),
        pltpu.VMEM((MB * TOK_MB + SEQ_PAD - SEQ + 1, D), wide),
        pltpu.VMEM((MB * TOK_MB, D), low),
        pltpu.SemaphoreType.DMA((6,)),
    )

    wait_bytes(share_in.at[pl.ds(0, n_dp - 1)], rs_recv.at[0])
    wait_bytes(share_out.at[pl.ds(0, n_dp - 1)], rs_recv.at[1])
    wait_bytes(share_in.at[pl.ds(0, n_dp - 1)], rs_send.at[0])
    wait_bytes(share_out.at[pl.ds(0, n_dp - 1)], rs_send.at[1])
    wait_bytes(small_land.at[pl.ds(0, n_dp - 1)], gather_send.at[0])
    wait_bytes(small_pair, red_send.at[3])
    others_half = pl.ds(0, (D - shard) // 2)
    for sems in (gather_send.at[1], share_send.at[0]):
        wait_bytes(land_qkv.at[:, others_half, :], sems)
    for sems in (gather_send.at[2], share_send.at[1]):
        wait_bytes(land_out.at[others_half, :], sems)
    wait_bytes(route, route_recv.at[2])
    for micro in range(MB):
        for kind in (KIND_COT, KIND_ROW):
            wait_bytes(spill_cot.at[micro], full_send.at[kind, micro])
        for kind in (KIND_BACK, KIND_MADE):
            near_wait(ex_send, kind, micro)
            far_wait(far_send, kind, micro)
        await_small(ex_send, gate_land, KIND_GATE, micro)
        await_small(ex_send, slope_land, KIND_SLOPE, micro)
    wait_bytes(tops_dp.at[pl.ds(0, n_dp - 1)], red_send.at[1])

    @pl.when(is_hub)
    def _():
        for micro in range(MB):
            for slot in range(2):
                wait_bytes(hub_sums.at[micro, slot], sum_send.at[1, micro, slot])

    wait_bytes(small_dp.at[pl.ds(0, n_dp - 1)], red_send.at[5])
    wait_bytes(small_part.at[pl.ds(0, parts - 1)], red_send.at[7])
    wait_bytes(share.at[0, pl.ds(0, 2 * shard), :], red_send.at[9])


def part_size(n_dp, n_ex):
    shard, parts = D // n_dp, n_ex // 2
    return -(-2 * shard // (parts * 16)) * 16


def run_block(n_dp, n_ex, capacity, operands):
    shard, slots = D // n_dp, n_ex * capacity
    parts, part_rows = n_ex // 2, part_size(n_dp, n_ex)
    total = parts * part_rows
    lanes = -(-shard // 128) * 128
    outs = [
        ((MB * TOK_MB, D), low),
        ((MB * TOK_MB, D), low),
        ((2, total, D), low),
        ((n_ex + 8, lanes), wide),
        ((n_dp, shard, FF), low),
        ((n_dp, D, FF // n_dp), low),
        ((16, 128), wide),
        ((4, MB, slots, D), low),
        ((slots, FF), low),
        ((slots, FF), low),
        ((MB, IMG_DEV * HEADS, SEQ_PAD, SEQ_PAD), low),
        ((MB, 3, TOK_PAD, D), low),
        ((2, MB * TOK_PAD, D), low),
        ((MB, TOK_PAD, D), low),
        ((MB, TOK_PAD, D), low),
        ((MB, TOK_PAD, D), wide),
        ((3, D, D), low),
        ((D, D), low),
        ((2, MB, 2, TOK_PAD, D), low),
        ((2, MB, 2, slots // 2, D), low),
        ((2, MB, TOK_PAD, D), low),
        ((D, FF), low),
        ((D, FF), low),
        ((4, n_dp, shard // 2, D), low),
        ((n_dp, 2 * shard, D), low),
        ((parts, part_rows, D), low),
    ]
    in_vmem = (3, 6)
    return pl.pallas_call(
        functools.partial(block_kernel, n_dp, n_ex, capacity),
        out_shape=[jax.ShapeDtypeStruct(*one) for one in outs],
        in_specs=[ANY, ANY, VMEM, ANY, ANY, VMEM, VMEM, ANY, ANY],
        out_specs=[VMEM if index in in_vmem else ANY for index in range(len(outs))],
        scratch_shapes=[
            pltpu.VMEM((MB, 2, TOK_PAD), jnp.int32),
            pltpu.VMEM((2, MB, 2, TOK_PAD), jnp.int32),
            pltpu.VMEM((n_ex + 8, lanes), wide),
            pltpu.VMEM((n_dp, n_ex + 8, lanes), wide),
            pltpu.VMEM((n_ex + 8, D), wide),
            pltpu.VMEM((n_ex, D), low),
            pltpu.VMEM((8, D), wide),
            pltpu.VMEM((MB * TOK_PAD, D), low),
            pltpu.VMEM((MB, slots, TOK_PAD), low),
            pltpu.VMEM((MB, 2, slots // 2, TOK_PAD), low),
            pltpu.VMEM((MB, n_ex, TOK_PAD), wide),
            pltpu.VMEM((n_ex, TOK_PAD), wide),
            pltpu.VMEM((MB, n_ex, TOK_PAD), wide),
            pltpu.VMEM((2 * MB, slots, D), low),
            pltpu.VMEM((2, slots // 2, D), low),
            pltpu.VMEM((MB, 2, TOK_PAD, D), low),
            pltpu.VMEM((MB, n_ex, 8, 128), wide),
            pltpu.VMEM((MB, n_ex, 8, 128), wide),
            pltpu.VMEM((MB, n_ex, 8, 128), wide),
            pltpu.VMEM((MB, n_ex, 8, 128), wide),
            pltpu.VMEM((16, 128), wide),
            pltpu.VMEM((n_ex, 16, 128), wide),
            pltpu.VMEM((n_dp, 16, 128), wide),
            pltpu.VMEM((n_ex + 8, D), wide),
            pltpu.VMEM((n_ex + 8, D), wide),
            pltpu.VMEM((n_dp, n_ex + 8, lanes), wide),
            pltpu.VMEM((n_dp, n_ex + 8, lanes), wide),
            pltpu.VMEM((n_ex, n_ex + 8, lanes), wide),
            pltpu.VMEM((2, 8, D), wide),
            pltpu.SemaphoreType.DMA((3,)),
            pltpu.SemaphoreType.DMA((3,)),
            pltpu.SemaphoreType.DMA((2,)),
            pltpu.SemaphoreType.DMA((2, n_dp - 1)),
            pltpu.SemaphoreType.DMA((6, MB)),
            pltpu.SemaphoreType.DMA((6, MB)),
            pltpu.SemaphoreType.DMA((4, MB)),
            pltpu.SemaphoreType.DMA((4, MB)),
            pltpu.SemaphoreType.DMA((2, MB)),
            pltpu.SemaphoreType.DMA((2, MB, 2)),
            pltpu.SemaphoreType.DMA((2, MB, 2)),
            pltpu.SemaphoreType.DMA((2, MB, 2)),
            pltpu.SemaphoreType.DMA((2, MB)),
            pltpu.SemaphoreType.DMA((3,)),
            pltpu.SemaphoreType.DMA((4, MB)),
            pltpu.SemaphoreType.DMA((2, MB)),
            pltpu.SemaphoreType.DMA((2, MB, 2)),
            pltpu.SemaphoreType.DMA((2,)),
            pltpu.SemaphoreType.DMA((2,)),
            pltpu.SemaphoreType.DMA((2,)),
            pltpu.SemaphoreType.DMA((10,)),
            pltpu.SemaphoreType.DMA((10,)),
            pltpu.SemaphoreType.DMA((4,)),
            pltpu.SemaphoreType.DMA((4,)),
            pltpu.SemaphoreType.DMA((4,)),
            pltpu.SemaphoreType.DMA((4,)),
            pltpu.SemaphoreType.DMA((6,)),
        ],
        compiler_params=pltpu.CompilerParams(
            collective_id=0, has_side_effects=True, vmem_limit_bytes=60 * 2**20
        ),
        name="encoder_block",
    )(*operands)


def per_device(
    tokens,
    attn_qkv,
    attn_out,
    router,
    norm_gains,
    expert_in,
    expert_out,
    routes,
    clip_limit,
    cotangent,
):
    n_dp, n_ex = lax.axis_size("dp"), lax.axis_size("expert")
    capacity = max(8, (TOK_MB * 10 // (4 * n_ex) + 7) // 8 * 8)
    shard = D // n_dp
    results = run_block(
        n_dp,
        n_ex,
        capacity,
        (
            tokens,
            cotangent,
            routes.T,
            attn_qkv,
            attn_out,
            router.T,
            norm_gains,
            expert_in[0],
            expert_out[0],
        ),
    )
    layer_out, grad_input, share, share_small, share_in, share_out, tops = results[:7]
    share = share[:, : 2 * shard].reshape(2, 4, shard // 2, D).astype(wide)
    share = jnp.swapaxes(share, 0, 1).reshape(4, shard, D)
    head_max = tops[:HEADS, 0]
    factor = clip_limit / jnp.maximum(head_max, clip_limit)
    root_scale = jnp.repeat(jnp.sqrt(factor), HEAD_DIM)
    clipped_qk = attn_qkv[:2].astype(wide) * root_scale[None, None, :]
    return (
        layer_out,
        grad_input,
        share[:3],
        share[3],
        share_small[:n_ex, :shard].T,
        share_small[n_ex : n_ex + 2, :shard],
        jnp.sum(share_in.astype(wide), axis=0)[None],
        jnp.sum(share_out.astype(wide), axis=0).T[None],
        head_max,
        clipped_qk,
    )


def solution(mesh):
    placed = (
        P(("dp", "expert"), None),
        P(None, "dp", None),
        P("dp", None),
        P("dp", None),
        P(None, "dp"),
        P("expert", None, None),
        P("expert", None, None),
        P(("dp", "expert"), None),
        P(),
        P(("dp", "expert"), None),
    )
    return jax.shard_map(
        per_device,
        mesh=mesh,
        in_specs=placed,
        out_specs=(
            P(("dp", "expert"), None),
            P(("dp", "expert"), None),
            P(None, "dp", None),
            P("dp", None),
            P("dp", None),
            P(None, "dp"),
            P("expert", "dp", None),
            P("expert", "dp", None),
            P(),
            P(None, "dp", None),
        ),
        check_vma=False,
    )
```

time: 443 us -> 358 us (0.81)
  Pallas kernels: 413 us -> 340 us
  local copies, waits for them, and re-layouts: 18.9 us -> 12 us
    pallas_call x1, Pallas kernels: 413 us -> 340 us  [run_block(): pl.pallas_call(functools.partial(block_kernel, n_dp, n_ex, capacity), out...]
    reshape x7 -> x0, local copies, waits for them, and re-layouts: 6.19 us -> none  [the longest x4 2.81 us: padded(): images = rows.reshape(MB, IMG_DEV, SEQ, rows.shape[-1])]
where the time goes in v3:
time: 358 us; the launch traced here: 357 us
  Pallas kernels  340 us (95%)
  local copies, waits for them, and re-layouts  12 us (3%)
  other arithmetic  4.32 us (1%)
    pallas_call x1, Pallas kernels, run_block(): pl.pallas_call(functools.partial(block_kernel, n_dp, n_ex, capacity), out...  340 us

profile of v3, /device:TPU:0, one launch (start us, length us, event | category | flops | bytes accessed | tf_op | source)
XLA Modules:
  0.0 356.9 jit_solution(8669473151106278918)
XLA Ops:
  0.6 0.0 copy-start.5
  0.7 0.0 copy-start.1
  0.7 339.8 %encoder_block.1 = (bf16[788,768]{1,0:T(8,128)(2,1)}, bf16[788,768]{1,0:T(8,128)(2,1)}, bf16[2,384,768]{2,1,0:T(8,128)(2,1)}, f32[16,256]{1,0:T(8,128)}, bf16[4,...) custom-call(bf16[788,768]{1,0:T(8,128)(2,1)} %tok_in.1, ...), custom_call_target="tpu_custom_call" | custom-call | tf_op jit(solution)/shard_map/encoder_block/pallas_call | solution.py:1486
  340.5 0.0 copy-start.3
  340.5 0.9 slice_reduce_fusion
  341.4 0.0 copy-done.5
  341.4 0.0 copy-start.4
  341.4 1.3 slice.26
  342.7 1.3 slice_bitcast_fusion
  344.0 0.1 broadcast_in_dim.11
  344.1 0.1 mul.10
  344.1 0.0 copy-done.1
  344.1 1.1 convert_multiply_fusion
  345.2 0.0 copy-done.3
  345.2 0.0 copy-start
  345.2 0.2 convert_bitcast_fusion
  345.5 0.0 copy-done.4
  345.5 0.0 slice-start
  345.5 0.9 slice.30
  346.3 0.2 slice.29
  346.5 0.0 slice-start.1
  346.5 1.3 copy.22
  347.8 0.5 copy-done
  348.4 2.3 convert_reduce_fusion.1
  350.6 0.0 slice-done
  350.6 0.0 slice-done.1
  350.7 0.7 convert_reduce_fusion
  351.4 2.0 copy.23
  353.3 0.0 copy-start.2
  353.3 2.5 copy.26
  355.8 0.0 copy-done.2
  355.8 1.0 copy.27
  (2 shorter events, 0.0 us)
Async XLA Ops:
  0.6 340.7 %copy-start.5 = (f32[12]{0:T(128)S(1)}, f32[12]{0:T(128)}, u32[]{:S(2)}) copy-start(f32[12]{0:T(128)} %param.18) | copy-start | bytes 148
  0.7 343.5 %copy-start.1 = (bf16[3,192,768]{2,1,0:T(8,128)(2,1)S(1)}, bf16[3,192,768]{2,1,0:T(8,128)(2,1)}, u32[]{:S(2)}) copy-start(bf16[3,192,768]{2,1,0:T(8,128)(2,1)} %qkv_in.1) | copy-start | bytes 2654212
  340.5 4.8 %copy-start.3 = (bf16[2,384,768]{2,1,0:T(8,128)(2,1)S(1)}, bf16[2,384,768]{2,1,0:T(8,128)(2,1)}, u32[]{:S(2)}) copy-start(bf16[2,384,768]{2,1,0:T(8,128)(2,1)} %get-tuple-element.19) | copy-start | bytes 3538948
  341.4 4.1 %copy-start.4 = (f32[12]{0:T(128)}, f32[12]{0:T(128)S(1)}, u32[]{:S(2)}) copy-start(f32[12]{0:T(128)S(1)} %slice_reduce_fusion) | copy-start | bytes 148
  345.2 3.1 copy-start
  345.5 5.2 %slice-start = ((s8[4718592]{0:T(1024)(128)(4,1)}), s8[4194304]{0:T(1024)(128)(4,1)S(1)}, s32[]{:S(2)}) async-start(s8[4718592]{0:T(1024)(128)(4,1)} %bitcast.19), calls=%async_computation | async-start | bytes 8388608
  346.5 4.2 %slice-start.1 = ((s8[4718592]{0:T(1024)(128)(4,1)}), s8[524288]{0:T(1024)(128)(4,1)S(1)}, s32[]{:S(2)}) async-start(s8[4718592]{0:T(1024)(128)(4,1)} %bitcast.19), calls=%async_computation.1 | async-start | bytes 1048576
  353.3 2.5 copy-start.2

commit v4 on v3

--- a/solution.py
+++ b/solution.py
@@ -284,6 +284,7 @@
 MADE_ROWS = 256
 BLOCK_FF = 512
 GRAD_FF = 256
+REDUCE_ORDER = (3, 0, 1, 2)
 KIND_COT, KIND_ROW, KIND_BACK, KIND_MADE, KIND_GATE, KIND_SLOPE = range(6)
 
 
@@ -318,8 +319,8 @@
     share_out,
     tops_out,
     land,
-    spill_hidden,
-    spill_grad,
+    half_in,
+    half_out,
     spill_probs,
     spill_qkv,
     spill_rows,
@@ -391,6 +392,10 @@
     pair_recv,
     own_send,
     own_recv,
+    chip_send,
+    chip_recv,
+    core_send,
+    core_recv,
     local_sem,
 ):
     dp, me = lax.axis_index("dp"), lax.axis_index("expert")
@@ -859,7 +864,20 @@
         pltpu.SemaphoreType.DMA((MB + 1, 5)),
     )
 
-    def experts(w_in, w_out, rows_in, cot, grad_rows, rows_t, grad_t, hidden, grad_pre, made, sems):
+    def experts(
+        w_in,
+        w_out,
+        rows_in,
+        cot,
+        grad_rows,
+        rows_t,
+        grad_t,
+        hidden,
+        grad_pre,
+        made,
+        first_grads,
+        sems,
+    ):
         eye = lax.broadcasted_iota(jnp.int32, (capacity, capacity), 0) == lax.broadcasted_iota(
             jnp.int32, (capacity, capacity), 1
         )
@@ -877,7 +895,7 @@
             copy.wait()
 
         def one(micro):
-            pl.when(micro > 0)(lambda: relay(KIND_ROW, micro))
+            pl.when(micro > 0)(lambda: relay(KIND_ROW, 1))
             near_wait(ex_recv, KIND_COT, micro)
             far_wait(far_recv, KIND_COT, micro)
             await_small(ex_recv, gate_land, KIND_GATE, micro)
@@ -903,16 +921,11 @@
 
             def turn(index):
                 rows = rows_of(index, 128)
-                cols = pl.ds(pl.multiple_of(micro * slots + index * 128, 128), 128)
+                cols = pl.ds(pl.multiple_of(index * 128, 128), 128)
                 rows_t[:, cols] = rows_in[rows, :].T
                 grad_t[:, cols] = grad_rows[rows, :].T
 
             loop(slots // 128, turn)
-
-            @pl.when(micro > 0)
-            def _():
-                pltpu.make_async_copy(hidden, spill_hidden, sems.at[2]).wait()
-                pltpu.make_async_copy(grad_pre, spill_grad, sems.at[3]).wait()
 
             def through(index):
                 cols = rows_of(index // (slots // BLOCK_ROWS), BLOCK_FF)
@@ -923,11 +936,6 @@
                 grad_pre[rows, cols] = (grad_hidden * slope).astype(low)
 
             loop((FF // BLOCK_FF) * (slots // BLOCK_ROWS), through, 2)
-
-            @pl.when(micro < MB - 1)
-            def _():
-                local_copy(hidden, spill_hidden, sems.at[2])
-                local_copy(grad_pre, spill_grad, sems.at[3])
 
             relay_wait(KIND_ROW, micro)
 
@@ -958,57 +966,88 @@
 
             loop(slots // MADE_ROWS, forth)
             exchange_small(slope_send, slope_land, KIND_SLOPE, micro)
-            pl.when(micro == 0)(lambda: relay(KIND_COT, 1))
+
+            @pl.when(micro == 0)
+            def _():
+                relay(KIND_COT, 1)
+                first_grads()
 
         loop(MB, one)
-
-        def send_made(micro):
-            gather(KIND_MADE, micro, MB + micro)
-
         hub_sum(KIND_BACK, 0)
-        loop(MB, send_made)
+        loop(MB, lambda micro: gather(KIND_MADE, micro, MB + micro))
 
         wait_bytes(tops_land.at[pl.ds(0, n_ex - 1)], red_recv.at[0])
         wait_bytes(tops_land.at[pl.ds(0, n_ex - 1)], red_send.at[0])
         tops[...] = jnp.max(tops_land[...], axis=0)
 
     def expert_phase(
-        w_in, w_out, rows_in, cot, grad_rows, rows_t, grad_t, hidden, grad_pre, made, sems
+        w_in,
+        w_out,
+        rows_in,
+        cot,
+        grad_rows,
+        rows_t,
+        grad_t,
+        hidden,
+        grad_pre,
+        made,
+        kept_in,
+        kept_out,
+        block_in,
+        block_out,
+        load_sems,
+        store_sems,
+        sems,
     ):
-        experts(w_in, w_out, rows_in, cot, grad_rows, rows_t, grad_t, hidden, grad_pre, made, sems)
-        weight_grads(rows_t, grad_t, hidden, grad_pre)
-        hub_sum(KIND_BACK, 1)
-
-    def weight_grads(rows_t, grad_t, hidden, grad_pre):
         blocks = FF // GRAD_FF
-        half = pl.ds(0, slots)
-        other = pl.ds(slots, slots)
-
-        def scoped(kept_hidden, kept_grad, out_in, out_out, load_sems, store_sems):
+
+        def stores(block, slot, target_in, target_out):
+            cols = rows_of(block, GRAD_FF)
+            return (
+                pltpu.make_async_copy(
+                    block_in.at[slot], target_in.at[:, cols], store_sems.at[0, slot]
+                ),
+                pltpu.make_async_copy(
+                    block_out.at[slot], target_out.at[:, cols], store_sems.at[1, slot]
+                ),
+            )
+
+        def own_store(block, slot):
+            cols = rows_of(block, GRAD_FF)
+            return pltpu.make_async_copy(
+                block_in.at[slot, own_rows, :], share_in.at[dp, :, cols], store_sems.at[2, slot]
+            )
+
+        def first_grads():
+            def one(block):
+                slot = lax.rem(block, 2)
+
+                @pl.when(block > 1)
+                def _():
+                    for copy in stores(block - 2, slot, half_in, half_out):
+                        copy.wait()
+
+                cols = rows_of(block, GRAD_FF)
+                block_in[slot] = dot(rows_t[...], grad_pre[:, cols]).astype(low)
+                block_out[slot] = dot(grad_t[...], hidden[:, cols]).astype(low)
+                for copy in stores(block, slot, half_in, half_out):
+                    copy.start()
+
+            loop(blocks, one)
+            for block in (blocks - 2, blocks - 1):
+                for copy in stores(block, block % 2, half_in, half_out):
+                    copy.wait()
+
+        def second_grads():
             def fetch(block, slot):
                 cols = rows_of(block, GRAD_FF)
-                local_copy(spill_hidden.at[:, cols], kept_hidden.at[slot], load_sems.at[0, slot])
-                local_copy(spill_grad.at[:, cols], kept_grad.at[slot], load_sems.at[1, slot])
-
-            def stored(block, slot):
-                cols = rows_of(block, GRAD_FF)
-                return (
-                    pltpu.make_async_copy(
-                        out_in.at[slot], stage_in.at[:, cols], store_sems.at[0, slot]
-                    ),
-                    pltpu.make_async_copy(
-                        out_out.at[slot], stage_out.at[:, cols], store_sems.at[1, slot]
-                    ),
-                    pltpu.make_async_copy(
-                        out_in.at[slot, own_rows, :],
-                        share_in.at[dp, :, cols],
-                        store_sems.at[2, slot],
-                    ),
-                )
+                local_copy(half_in.at[:, cols], kept_in.at[slot], load_sems.at[0, slot])
+                local_copy(half_out.at[:, cols], kept_out.at[slot], load_sems.at[1, slot])
 
             def ship(block, slot):
-                for copy in stored(block, slot):
+                for copy in stores(block, slot, stage_in, stage_out):
                     copy.wait()
+                own_store(block, slot).wait()
                 cols = rows_of(block, GRAD_FF)
 
                 def one(step):
@@ -1032,17 +1071,16 @@
                 def _():
                     fetch(block + 1, 1 - slot)
 
-                wait_bytes(kept_hidden.at[slot], load_sems.at[0, slot])
-                wait_bytes(kept_grad.at[slot], load_sems.at[1, slot])
+                wait_bytes(kept_in.at[slot], load_sems.at[0, slot])
+                wait_bytes(kept_out.at[slot], load_sems.at[1, slot])
                 cols = rows_of(block, GRAD_FF)
-                out_in[slot] = (
-                    dot(rows_t[:, half], kept_grad[slot]) + dot(rows_t[:, other], grad_pre[:, cols])
-                ).astype(low)
-                out_out[slot] = (
-                    dot(grad_t[:, half], kept_hidden[slot]) + dot(grad_t[:, other], hidden[:, cols])
-                ).astype(low)
-                for copy in stored(block, slot):
+                value_in = dot(rows_t[...], grad_pre[:, cols]) + kept_in[slot].astype(wide)
+                block_in[slot] = value_in.astype(low)
+                value_out = dot(grad_t[...], hidden[:, cols]) + kept_out[slot].astype(wide)
+                block_out[slot] = value_out.astype(low)
+                for copy in stores(block, slot, stage_in, stage_out):
                     copy.start()
+                own_store(block, slot).start()
 
                 @pl.when(block > 0)
                 def _():
@@ -1051,15 +1089,22 @@
             loop(blocks, one)
             ship(blocks - 1, (blocks - 1) % 2)
 
-        pl.run_scoped(
-            scoped,
-            pltpu.VMEM((2, slots, GRAD_FF), low),
-            pltpu.VMEM((2, slots, GRAD_FF), low),
-            pltpu.VMEM((2, D, GRAD_FF), low),
-            pltpu.VMEM((2, D, GRAD_FF), low),
-            pltpu.SemaphoreType.DMA((2, 2)),
-            pltpu.SemaphoreType.DMA((3, 2)),
+        experts(
+            w_in,
+            w_out,
+            rows_in,
+            cot,
+            grad_rows,
+            rows_t,
+            grad_t,
+            hidden,
+            grad_pre,
+            made,
+            first_grads,
+            sems,
         )
+        second_grads()
+        hub_sum(KIND_BACK, 1)
 
     pl.run_scoped(
         expert_phase,
@@ -1068,25 +1113,33 @@
         pltpu.VMEM((slots, D), low),
         pltpu.VMEM((slots, D), low),
         pltpu.VMEM((slots, D), low),
-        pltpu.VMEM((D, MB * slots), low),
-        pltpu.VMEM((D, MB * slots), low),
+        pltpu.VMEM((D, slots), low),
+        pltpu.VMEM((D, slots), low),
         pltpu.VMEM((slots, FF), low),
         pltpu.VMEM((slots, FF), low),
         pltpu.VMEM((MADE_ROWS, D), wide),
+        pltpu.VMEM((2, D, GRAD_FF), low),
+        pltpu.VMEM((2, D, GRAD_FF), low),
+        pltpu.VMEM((2, D, GRAD_FF), low),
+        pltpu.VMEM((2, D, GRAD_FF), low),
+        pltpu.SemaphoreType.DMA((2, 2)),
+        pltpu.SemaphoreType.DMA((3, 2)),
         pltpu.SemaphoreType.DMA((4,)),
     )
 
     width = FF // n_dp
 
-    def ship_out(step):
+    def ship_out(step, rows=pl.ds(0, D)):
         peer = dp ^ (step + 1)
         remote(
-            stage_out.at[:, rows_of(peer, width)],
-            share_out.at[dp],
+            stage_out.at[rows, rows_of(peer, width)],
+            share_out.at[dp, rows, :],
             rs_send.at[1],
             rs_recv.at[1],
             (peer, me),
         )
+
+    loop(2, ship_out)
 
     def spread_tops(step):
         peer = dp ^ (step + 1)
@@ -1113,9 +1166,11 @@
         attended,
         proj,
         result,
-        out,
         grads,
         pairs,
+        total_rows,
+        grad_low,
+        summed,
         part_own,
         buffer,
         compact,
@@ -1167,7 +1222,7 @@
                 peer = dp ^ (step + 1)
                 remote(
                     pairs.at[part, peer],
-                    dp_land.at[dp, own_half(part), :],
+                    dp_land.at[dp, own_half(REDUCE_ORDER.index(part)), :],
                     own_send.at[part],
                     own_recv.at[part],
                     (peer, me),
@@ -1219,22 +1274,113 @@
                 grad.at[micro],
                 attended.at[tokens],
                 proj.at[:, tokens, :],
-                out,
+                arrived.at[pl.ds(0, TOK_PAD), :],
                 gain_sums,
                 cot,
                 lambda: pl.when(micro == MB - 1)(lambda: grad_block(3, mixed, attended)),
             )
-            pl.when(micro == 0)(lambda: loop(2, ship_out))
+
+            pl.when(micro == 0)(lambda: hub_sum(KIND_MADE, 0))
+
 
         loop(MB, one)
+        half_rows = pl.ds(0, shard)
+
+        def chip(index):
+            return (dp, 2 * index + core)
+
+        mine = rows_of(z, part_rows)
+
+        def to_chips(group):
+            for slot in range(2):
+                position = 2 * group + slot
+                part = REDUCE_ORDER[position]
+                wait_bytes(
+                    dp_land.at[pl.ds(0, n_dp - 1), own_half(position), :], own_recv.at[part]
+                )
+                total_rows[own_half(slot), :] = pairs[part, dp].astype(wide)
+
+            def place_for(step):
+                return qkv.at[lax.rem(step, 3), rows_of(step // 3, shard), :]
+
+            def load(step):
+                peer = dp ^ (step + 1)
+                local_copy(dp_land.at[peer, rows_of(group, shard), :], place_for(step), sems.at[0])
+
+            loop(n_dp - 1, load)
+            wait_bytes(dp_land.at[pl.ds(0, n_dp - 1), half_rows, :], sems.at[0])
+
+            def add(step):
+                total_rows[half_rows, :] += place_for(step)[...].astype(wide)
+
+            loop(n_dp - 1, add)
+            total = parts * part_rows
+            if total > shard:
+                grad_low[group, pl.ds(shard, total - shard), :] = jnp.zeros(
+                    (total - shard, D), low
+                )
+            grad_low[group, half_rows, :] = total_rows[half_rows, :].astype(low)
+
+            def one(step):
+                peer = z ^ (step + 1)
+                remote(
+                    grad_low.at[group, rows_of(peer, part_rows), :],
+                    part_land.at[group, z],
+                    chip_send.at[0, group],
+                    chip_recv.at[0, group],
+                    chip(peer),
+                )
+
+            loop(parts - 1, one)
+
+        def to_all_chips(group):
+            wait_bytes(part_land.at[group, pl.ds(0, parts - 1)], chip_recv.at[0, group])
+
+            def load(step):
+                peer = z ^ (step + 1)
+                local_copy(part_land.at[group, peer], part_own.at[step], sems.at[0])
+
+            loop(parts - 1, load)
+            part_total = total_rows.at[pl.ds(0, part_rows), :]
+            part_total[...] = grad_low[group, mine, :].astype(wide)
+            wait_bytes(part_own, sems.at[0])
+
+            def add(step):
+                part_total[...] += part_own[step].astype(wide)
+
+            loop(parts - 1, add)
+            summed[group] = part_total[...].astype(low)
+
+            def one(step):
+                peer = z ^ (step + 1)
+                remote(
+                    summed.at[group],
+                    share.at[core, group, mine, :],
+                    chip_send.at[1, group],
+                    chip_recv.at[1, group],
+                    chip(peer),
+                )
+
+            loop(parts - 1, one)
+            local_copy(summed.at[group], share.at[core, group, mine, :], sems.at[0]).wait()
+
+        def to_core(group):
+            wait_bytes(
+                share.at[0, group, pl.ds(0, (parts - 1) * part_rows), :], chip_recv.at[1, group]
+            )
+            half = share.at[core, group, half_rows, :]
+            remote(half, half, core_send.at[group], core_recv.at[group], partner)
+
+        hub_sum(KIND_MADE, 1)
+        grad_block(0, first, proj.at[0])
         to_owners(3)
-        hub_sum(KIND_MADE, 0)
-        for part in range(3):
-            grad_block(part, first, proj.at[part])
-        for part in range(3):
-            to_owners(part)
-        loop(n_dp - 3, lambda step: ship_out(step + 2))
-        hub_sum(KIND_MADE, 1)
+        grad_block(1, first, proj.at[1])
+        to_owners(0)
+        grad_block(2, first, proj.at[2])
+        to_owners(1)
+        to_owners(2)
+        loop(n_dp - 3, lambda step: ship_out(step + 2, pl.ds(0, D // 2)))
+        to_chips(0)
 
         def finish(micro):
             local_copy(spill_tok.at[micro], cot, sems.at[2]).wait()
@@ -1248,7 +1394,9 @@
                 result,
             )
 
-        loop(MB, finish)
+        finish(0)
+        to_all_chips(0)
+        finish(1)
         small_sum[n_ex : n_ex + 1, :] = jnp.sum(gain_sums[0], axis=0, keepdims=True)
         small_sum[n_ex + 1 : n_ex + 2, :] = jnp.sum(gain_sums[1], axis=0, keepdims=True)
         remote(small_sum, small_pair, red_send.at[3], red_recv.at[3], partner)
@@ -1267,47 +1415,10 @@
             )
 
         loop(n_dp - 1, small_to_owner)
+        loop(n_dp - 3, lambda step: ship_out(step + 2, pl.ds(D // 2, D // 2)))
         small_dp[dp] = small_cut[dp]
-        for part in range(4):
-            wait_bytes(dp_land.at[pl.ds(0, n_dp - 1), own_half(part), :], own_recv.at[part])
-            result[pl.ds(part * half_shard, half_shard), :] = pairs[part, dp].astype(wide)
-
-        def load_dp(step):
-            peer = dp ^ (step + 1)
-            local_copy(dp_land.at[peer], proj_rows(step), sems.at[0])
-
-        def proj_rows(step):
-            return proj.at[lax.rem(step, 3), rows_of(step // 3, 2 * shard), :]
-
-        loop(n_dp - 1, load_dp)
-        wait_bytes(dp_land.at[pl.ds(0, n_dp - 1)], sems.at[0])
-
-        def add_dp(step):
-            result[pl.ds(0, 2 * shard), :] += proj_rows(step)[...].astype(wide)
-
-        loop(n_dp - 1, add_dp)
-        total = parts * part_rows
-        if total > 2 * shard:
-            result[pl.ds(2 * shard, total - 2 * shard), :] = jnp.zeros(
-                (total - 2 * shard, D), wide
-            )
-        grad_low = arrived
-        grad_low[pl.ds(0, total), :] = result[pl.ds(0, total), :].astype(low)
-
-        def chip(index):
-            return (dp, 2 * index + core)
-
-        def to_part(step):
-            peer = z ^ (step + 1)
-            remote(
-                grad_low.at[rows_of(peer, part_rows), :],
-                part_land.at[z],
-                red_send.at[6],
-                red_recv.at[6],
-                chip(peer),
-            )
-
-        loop(parts - 1, to_part)
+        to_chips(1)
+        to_core(0)
         wait_bytes(small_dp.at[pl.ds(0, n_dp - 1)], red_recv.at[5])
         small_part[me] = jnp.sum(small_dp[...], axis=0)
 
@@ -1321,37 +1432,7 @@
             )
 
         loop(parts - 1, to_chip)
-        mine = rows_of(z, part_rows)
-        result[pl.ds(0, part_rows), :] = grad_low[mine, :].astype(wide)
-        wait_bytes(part_land.at[pl.ds(0, parts - 1)], red_recv.at[6])
-
-        def load_part(step):
-            peer = z ^ (step + 1)
-            local_copy(part_land.at[peer], part_own.at[step], sems.at[0])
-
-        loop(parts - 1, load_part)
-        wait_bytes(part_own, sems.at[0])
-
-        def add_part(step):
-            result[pl.ds(0, part_rows), :] += part_own[step].astype(wide)
-
-        loop(parts - 1, add_part)
-
-        summed = out.at[pl.ds(0, part_rows), :]
-        summed[...] = result[pl.ds(0, part_rows), :].astype(low)
-
-        def to_all(step):
-            remote(
-                summed,
-                share.at[core, mine, :],
-                red_send.at[8],
-                red_recv.at[8],
-                chip(z ^ (step + 1)),
-            )
-
-        loop(parts - 1, to_all)
-        local_copy(summed, share.at[core, mine, :], sems.at[0]).wait()
-        wait_bytes(grad_low.at[pl.ds(0, (parts - 1) * part_rows), :], red_send.at[6])
+        to_all_chips(1)
 
         def combine(micro):
             fetch_gathered(KIND_MADE, micro, arrived, sems.at[3])
@@ -1359,19 +1440,12 @@
                 cols = pl.ds(block * COLS, COLS)
                 grad[micro, :, cols] = resid[micro, :, cols] + gathered(micro, arrived, cols)
 
-        loop(MB, combine)
+        combine(0)
+        to_core(1)
+        combine(1)
         store.wait()
         compact_rows(grad, buffer, compact)
         store = local_copy(compact, layer_out, sems.at[4])
-        wait_bytes(share.at[0, pl.ds(0, (parts - 1) * part_rows), :], red_recv.at[8])
-        half_rows = pl.ds(0, 2 * shard)
-        remote(
-            share.at[core, half_rows, :],
-            share.at[core, half_rows, :],
-            red_send.at[9],
-            red_recv.at[9],
-            partner,
-        )
         wait_bytes(small_part.at[pl.ds(0, parts - 1)], red_recv.at[7])
         chosen = small_part[core]
         for index in range(1, chips):
@@ -1379,13 +1453,19 @@
         share_small[...] = chosen
         wait_bytes(tops_dp.at[pl.ds(0, n_dp - 1)], red_recv.at[1])
         tops_out[...] = jnp.max(tops_dp[...], axis=0)
-        wait_bytes(share.at[0, half_rows, :], red_recv.at[9])
+        for group in range(2):
+            wait_bytes(share.at[0, group, half_rows, :], core_recv.at[group])
         store.wait()
 
         for part in range(4):
             wait_bytes(pair_land.at[part], pair_send.at[part])
             wait_bytes(dp_land.at[pl.ds(0, n_dp - 1), own_half(part), :], own_send.at[part])
-        wait_bytes(grad_low.at[pl.ds(0, (parts - 1) * part_rows), :], red_send.at[8])
+        for group in range(2):
+            for step in range(2):
+                wait_bytes(
+                    grad_low.at[0, pl.ds(0, (parts - 1) * part_rows), :],
+                    chip_send.at[step, group],
+                )
 
     pl.run_scoped(
         backward,
@@ -1402,9 +1482,11 @@
         pltpu.VMEM((MB * TOK_PAD, D), low),
         pltpu.VMEM((3, MB * TOK_PAD, D), low),
         pltpu.VMEM((TOK_PAD, D), wide),
-        pltpu.VMEM((TOK_PAD, D), low),
         pltpu.VMEM((4, n_dp, shard, D), low),
         pltpu.VMEM((4, n_dp, half_shard, D), low),
+        pltpu.VMEM((max(shard, part_rows), D), wide),
+        pltpu.VMEM((2, parts * part_rows, D), low),
+        pltpu.VMEM((2, part_rows, D), low),
         pltpu.VMEM((parts - 1, part_rows, D), low),
         pltpu.VMEM((MB * TOK_MB + SEQ_PAD - SEQ + 1, D), wide),
         pltpu.VMEM((MB * TOK_MB, D), low),
@@ -1441,12 +1523,13 @@
 
     wait_bytes(small_dp.at[pl.ds(0, n_dp - 1)], red_send.at[5])
     wait_bytes(small_part.at[pl.ds(0, parts - 1)], red_send.at[7])
-    wait_bytes(share.at[0, pl.ds(0, 2 * shard), :], red_send.at[9])
+    for group in range(2):
+        wait_bytes(share.at[0, group, pl.ds(0, shard), :], core_send.at[group])
 
 
 def part_size(n_dp, n_ex):
     shard, parts = D // n_dp, n_ex // 2
-    return -(-2 * shard // (parts * 16)) * 16
+    return -(-shard // (parts * 16)) * 16
 
 
 def run_block(n_dp, n_ex, capacity, operands):
@@ -1457,14 +1540,14 @@
     outs = [
         ((MB * TOK_MB, D), low),
         ((MB * TOK_MB, D), low),
-        ((2, total, D), low),
+        ((2, 2, total, D), low),
         ((n_ex + 8, lanes), wide),
         ((n_dp, shard, FF), low),
         ((n_dp, D, FF // n_dp), low),
         ((16, 128), wide),
         ((4, MB, slots, D), low),
-        ((slots, FF), low),
-        ((slots, FF), low),
+        ((D, FF), low),
+        ((D, FF), low),
         ((MB, IMG_DEV * HEADS, SEQ_PAD, SEQ_PAD), low),
         ((MB, 3, TOK_PAD, D), low),
         ((2, MB * TOK_PAD, D), low),
@@ -1480,7 +1563,7 @@
         ((D, FF), low),
         ((4, n_dp, shard // 2, D), low),
         ((n_dp, 2 * shard, D), low),
-        ((parts, part_rows, D), low),
+        ((2, parts, part_rows, D), low),
     ]
     in_vmem = (3, 6)
     return pl.pallas_call(
@@ -1544,10 +1627,14 @@
             pltpu.SemaphoreType.DMA((4,)),
             pltpu.SemaphoreType.DMA((4,)),
             pltpu.SemaphoreType.DMA((4,)),
+            pltpu.SemaphoreType.DMA((2, 2)),
+            pltpu.SemaphoreType.DMA((2, 2)),
+            pltpu.SemaphoreType.DMA((2,)),
+            pltpu.SemaphoreType.DMA((2,)),
             pltpu.SemaphoreType.DMA((6,)),
         ],
         compiler_params=pltpu.CompilerParams(
-            collective_id=0, has_side_effects=True, vmem_limit_bytes=60 * 2**20
+            collective_id=0, has_side_effects=True, vmem_limit_bytes=61 * 2**20
         ),
         name="encoder_block",
     )(*operands)
@@ -1585,7 +1672,7 @@
         ),
     )
     layer_out, grad_input, share, share_small, share_in, share_out, tops = results[:7]
-    share = share[:, : 2 * shard].reshape(2, 4, shard // 2, D).astype(wide)
+    share = share[:, :, :shard].reshape(2, 4, shard // 2, D).astype(wide)
     share = jnp.swapaxes(share, 0, 1).reshape(4, shard, D)
     head_max = tops[:HEADS, 0]
     factor = clip_limit / jnp.maximum(head_max, clip_limit)
@@ -1594,8 +1681,8 @@
     return (
         layer_out,
         grad_input,
-        share[:3],
-        share[3],
+        share[1:],
+        share[0],
         share_small[:n_ex, :shard].T,
         share_small[n_ex : n_ex + 2, :shard],
         jnp.sum(share_in.astype(wide), axis=0)[None],

time: 358 us -> 343 us (0.958)
  Pallas kernels: 340 us -> 323 us
    pallas_call x1, Pallas kernels: 340 us -> 323 us  [run_block(): pl.pallas_call(functools.partial(block_kernel, n_dp, n_ex, capacity), out...]
where the time goes in v4:
time: 343 us; the launch traced here: 340 us
  Pallas kernels  323 us (94%)
  local copies, waits for them, and re-layouts  12 us (3%)
  other arithmetic  4.32 us (1%)
    pallas_call x1, Pallas kernels, run_block(): pl.pallas_call(functools.partial(block_kernel, n_dp, n_ex, capacity), out...  323 us

profile of v4, /device:TPU:0, one launch (start us, length us, event | category | flops | bytes accessed | tf_op | source)
XLA Modules:
  0.0 340.1 jit_solution(5940152607090141734)
XLA Ops:
  0.6 0.0 copy-start.5
  0.7 0.0 copy-start.1
  0.7 323.0 %encoder_block.1 = (bf16[788,768]{1,0:T(8,128)(2,1)}, bf16[788,768]{1,0:T(8,128)(2,1)}, bf16[2,2,192,768]{3,2,1,0:T(8,128)(2,1)}, f32[16,256]{1,0:T(8,128)}, bf1...) custom-call(bf16[788,768]{1,0:T(8,128)(2,1)} %tok_in.1, ...), custom_call_target="tpu_custom_call" | custom-call | tf_op jit(solution)/shard_map/encoder_block/pallas_call | solution.py:1569
  323.7 0.0 copy-start.3
  323.7 0.9 slice_reduce_fusion
  324.6 0.0 copy-done.5
  324.6 0.0 copy-start.4
  324.6 1.3 slice.26
  325.9 1.3 slice_bitcast_fusion
  327.2 0.1 broadcast_in_dim.11
  327.3 0.1 mul.10
  327.4 0.0 copy-done.1
  327.4 1.1 convert_multiply_fusion
  328.5 0.0 copy-done.3
  328.5 0.0 copy-start
  328.5 0.2 convert_bitcast_fusion
  328.7 0.0 copy-done.4
  328.7 0.0 slice-start
  328.7 0.9 slice.30
  329.6 0.2 slice.29
  329.7 0.0 slice-start.1
  329.7 1.3 copy.22
  331.1 0.5 copy-done
  331.6 2.3 convert_reduce_fusion.1
  333.9 0.0 slice-done
  333.9 0.0 slice-done.1
  333.9 0.7 convert_reduce_fusion
  334.6 2.0 copy.23
  336.6 0.0 copy-start.2
  336.6 2.5 copy.26
  339.0 0.0 copy-done.2
  339.1 1.0 copy.27
  (2 shorter events, 0.0 us)
Async XLA Ops:
  0.6 324.0 %copy-start.5 = (f32[12]{0:T(128)S(1)}, f32[12]{0:T(128)}, u32[]{:S(2)}) copy-start(f32[12]{0:T(128)} %param.18) | copy-start | bytes 148
  0.7 326.7 %copy-start.1 = (bf16[3,192,768]{2,1,0:T(8,128)(2,1)S(1)}, bf16[3,192,768]{2,1,0:T(8,128)(2,1)}, u32[]{:S(2)}) copy-start(bf16[3,192,768]{2,1,0:T(8,128)(2,1)} %qkv_in.1) | copy-start | bytes 2654212
  323.7 4.8 %copy-start.3 = (bf16[2,2,192,768]{3,2,1,0:T(8,128)(2,1)S(1)}, bf16[2,2,192,768]{3,2,1,0:T(8,128)(2,1)}, u32[]{:S(2)}) copy-start(bf16[2,2,192,768]{3,2,1,0:T(8,128)(2,1)} %get-tuple-element.19) | copy-start | bytes 3538948
  324.6 4.1 %copy-start.4 = (f32[12]{0:T(128)}, f32[12]{0:T(128)S(1)}, u32[]{:S(2)}) copy-start(f32[12]{0:T(128)S(1)} %slice_reduce_fusion) | copy-start | bytes 148
  328.5 3.1 copy-start
  328.7 5.2 %slice-start = ((s8[4718592]{0:T(1024)(128)(4,1)}), s8[4194304]{0:T(1024)(128)(4,1)S(1)}, s32[]{:S(2)}) async-start(s8[4718592]{0:T(1024)(128)(4,1)} %bitcast.19), calls=%async_computation | async-start | bytes 8388608
  329.7 4.2 %slice-start.1 = ((s8[4718592]{0:T(1024)(128)(4,1)}), s8[524288]{0:T(1024)(128)(4,1)S(1)}, s32[]{:S(2)}) async-start(s8[4718592]{0:T(1024)(128)(4,1)} %bitcast.19), calls=%async_computation.1 | async-start | bytes 1048576
  336.6 2.5 copy-start.2
